TPU v7x, 32 devices: a whole 2x2x4 slice. The times are simulated.
32 devices in a mesh: tm: 4 (over y, x), chan: 8 (over z, core).
Axes of the slice: x: 2, y: 2, z: 4, core: 2. Of those that a mesh axis runs over, the one named last changes fastest.
Arguments:
- latent_input: bfloat16 [2048, 320], P('chan', 'tm'), may hold values from -6 to 6
- upsample_kernel: bfloat16 [16, 1024, 2048], P(None, 'chan', 'tm'), may hold values from -0.09375 to 0.09375
- dilated_kernel: bfloat16 [2, 7, 1024, 1024], P(None, None, 'chan'), may hold values from -0.0625 to 0.0625
- pointwise_kernel: bfloat16 [2, 1024, 1024], P(None, 'chan'), may hold values from -0.1875 to 0.1875
- dilated_prune_mask: int32 [2, 7, 1024, 128], P(None, None, 'chan'), may hold values 0 or 1
- pointwise_prune_mask: int32 [2, 1024, 128], P(None, 'chan'), may hold values 0 or 1
- snake_freq_upsample: float32 [2048], P('chan'), may hold values from 0.5 to 3
- snake_freq_dilated: float32 [2, 1024], P(None, 'chan'), may hold values from 0.5 to 3
- snake_freq_pointwise: float32 [2, 1024], P(None, 'chan'), may hold values from 0.5 to 3
- segment_lengths: int32 [3], replicated, may hold values from 1 to 240, as said below
- cotangent: bfloat16 [1024, 2560], P('chan', 'tm'), may hold values from -6 to 6
Outputs:
- decoded: bfloat16 [1024, 2560], P('chan', 'tm')
- dil_saliency: float32 [2, 7, 1024, 1024], P(None, None, 'chan')
- point_saliency: float32 [2, 1024, 1024], P(None, 'chan')
Inputs may be any that keep to these rules, and one draw needn't show every extreme that they name: `segment_lengths`: 3 lengths in latent frames that sum to 320, in an order drawn with them; the longest is exactly 240.
All inputs are finite; a program needn't handle non-finite values. No bound on the sum of `dilated_prune_mask` or of `pointwise_prune_mask` on one device may be relied on, other than what follows from the above.
Results may differ from a plain program's by a relative error of at most 0.035.
Values may be sent and summed in bfloat16 or wider, within the bound.
A program may use at most 128 MiB of HBM per device.

v0:
```python
import jax
import jax.numpy as jnp
from jax import lax
from jax.sharding import PartitionSpec as P


def with_halo(cells, sides, width):
    for axis, dim in sides:
        count = lax.axis_size(axis)
        ends = count - 1
        head = lax.slice_in_dim(cells, 0, width, axis=dim)
        tail = lax.slice_in_dim(cells, cells.shape[dim] - width, cells.shape[dim], axis=dim)
        cells = jnp.concatenate(
            [
                lax.ppermute(tail, axis, [(i, (i + 1) % count) for i in range(ends)]),
                cells,
                lax.ppermute(head, axis, [((i + 1) % count, i) for i in range(ends)]),
            ],
            axis=dim,
        )
    return cells


def snake_act(values, alpha):
    scale = alpha[:, None]
    return values + jnp.sin(scale * values) ** 2 / scale


def snake_slope(values, alpha):
    return 1.0 + jnp.sin(2.0 * alpha[:, None] * values)


def track_ids(lengths, frame_index, total_frames):
    starts = jnp.cumsum(lengths) - lengths
    found = jnp.sum((starts[:, None] <= frame_index[None, :]).astype(jnp.int32), axis=0) - 1
    return jnp.where(frame_index < 0, -1, jnp.where(frame_index >= total_frames, -2, found))


def per_device(
    latent_input,
    upsample_kernel,
    dilated_kernel,
    pointwise_kernel,
    dilated_prune_mask,
    pointwise_prune_mask,
    snake_freq_upsample,
    snake_freq_dilated,
    snake_freq_pointwise,
    segment_lengths,
    cotangent,
):
    stride = upsample_kernel.shape[0] // 2
    half_stride = stride // 2
    frame_count = latent_input.shape[1]
    row_count = frame_count * stride
    total_frames = frame_count * lax.axis_size("tm")
    out_local = upsample_kernel.shape[1]
    residual_unit_count = dilated_kernel.shape[0]
    kernel_tap_count = dilated_kernel.shape[1]
    total_frame_width = dilated_kernel.shape[3]
    prune_block_width = total_frame_width // dilated_prune_mask.shape[3]
    activated = snake_act(latent_input.astype(jnp.float32), snake_freq_upsample).astype(
        jnp.bfloat16
    )
    bordered = with_halo(activated, (("tm", 1),), 1)
    channels_all = lax.all_gather(bordered, "chan", axis=0, tiled=True)
    weight_block = lax.all_gather(upsample_kernel, "tm", axis=2, tiled=True)
    number = weight_block.shape[2]
    middle = jnp.dot(
        weight_block[half_stride : half_stride + stride].reshape(stride * out_local, number),
        channels_all[:, 1:-1],
        preferred_element_type=jnp.float32,
    )
    lower = jnp.dot(
        weight_block[half_stride + stride :].reshape(half_stride * out_local, number),
        channels_all[:, :-2],
        preferred_element_type=jnp.float32,
    )
    upper = jnp.dot(
        weight_block[:half_stride].reshape(half_stride * out_local, number),
        channels_all[:, 2:],
        preferred_element_type=jnp.float32,
    )
    middle, lower, upper = (middle, lower, upper)
    frame_pos = lax.axis_index("tm") * frame_count + jnp.arange(frame_count, dtype=jnp.int32)
    frame_ids = track_ids(segment_lengths, frame_pos, total_frames)
    prev_ok = (frame_ids == track_ids(segment_lengths, frame_pos - 1, total_frames)).astype(
        jnp.float32
    )
    next_ok = (frame_ids == track_ids(segment_lengths, frame_pos + 1, total_frames)).astype(
        jnp.float32
    )
    neighbour = jnp.concatenate(
        [
            (lower * prev_ok[None, :]).reshape(half_stride, out_local, frame_count),
            (upper * next_ok[None, :]).reshape(half_stride, out_local, frame_count),
        ],
        axis=0,
    )
    hidden_state = (
        (middle.reshape(stride, out_local, frame_count) + neighbour)
        .transpose(1, 2, 0)
        .reshape(out_local, row_count)
    )
    row_pos = lax.axis_index("tm") * row_count + jnp.arange(row_count, dtype=jnp.int32)
    own_ids = track_ids(segment_lengths, jnp.floor_divide(row_pos, stride), total_frames)

    def tap_mask(offset):
        other = track_ids(segment_lengths, jnp.floor_divide(row_pos + offset, stride), total_frames)
        return (own_ids == other).astype(jnp.float32)

    saved_residuals = []
    for residual_unit_index in range(residual_unit_count):
        spacing = 3 ** (residual_unit_index + 1)
        margin = 3 * spacing
        dilated_effective = dilated_kernel[residual_unit_index] * jnp.repeat(
            dilated_prune_mask[residual_unit_index], prune_block_width, axis=-1
        ).astype(jnp.bfloat16)
        pointwise_effective = pointwise_kernel[residual_unit_index] * jnp.repeat(
            pointwise_prune_mask[residual_unit_index], prune_block_width, axis=-1
        ).astype(jnp.bfloat16)
        first = snake_act(hidden_state, snake_freq_dilated[residual_unit_index]).astype(
            jnp.bfloat16
        )
        first_all = lax.all_gather(first, "chan", axis=0, tiled=True)
        padded_input = with_halo(first_all, (("tm", 1),), margin)
        kernel_tap_masks = jnp.stack(
            [
                tap_mask((kernel_tap_index - 3) * spacing)
                for kernel_tap_index in range(kernel_tap_count)
            ]
        )
        track_window_list = jnp.stack(
            [
                padded_input[:, kernel_tap_index * spacing : kernel_tap_index * spacing + row_count]
                for kernel_tap_index in range(kernel_tap_count)
            ]
        )
        conv_result = jnp.zeros((out_local, row_count), jnp.float32)
        for kernel_tap_index in range(kernel_tap_count):
            conv_result = conv_result + kernel_tap_masks[kernel_tap_index][None, :] * jnp.dot(
                dilated_effective[kernel_tap_index],
                track_window_list[kernel_tap_index],
                preferred_element_type=jnp.float32,
            )
        second_activation = snake_act(
            conv_result, snake_freq_pointwise[residual_unit_index]
        ).astype(jnp.bfloat16)
        second_activation_all = lax.all_gather(second_activation, "chan", axis=0, tiled=True)
        saved_residuals.append(
            (
                hidden_state,
                track_window_list,
                conv_result,
                second_activation_all,
                dilated_effective,
                pointwise_effective,
            )
        )
        hidden_state = hidden_state + jnp.dot(
            pointwise_effective, second_activation_all, preferred_element_type=jnp.float32
        )
    decoded = hidden_state.astype(jnp.bfloat16)
    grad_out = cotangent.astype(jnp.float32)
    dilated_gradient_list = [None] * residual_unit_count
    point_grads = [None] * residual_unit_count
    dilated_gradient_sum = [None] * residual_unit_count
    pointwise_gradient_sum = [None] * residual_unit_count
    for residual_unit_index in reversed(range(residual_unit_count)):
        spacing = 3 ** (residual_unit_index + 1)
        margin = 3 * spacing
        (
            hidden_input,
            track_window_list,
            conv_result,
            second_activation_all,
            dilated_effective,
            pointwise_effective,
        ) = saved_residuals[residual_unit_index]
        grad_b = grad_out.astype(jnp.bfloat16)
        pointwise_gradient = lax.dot_general(
            grad_b,
            second_activation_all,
            (((1,), (1,)), ((), ())),
            preferred_element_type=jnp.float32,
        )
        grad_second = lax.psum_scatter(
            lax.dot_general(
                pointwise_effective,
                grad_b,
                (((0,), (0,)), ((), ())),
                preferred_element_type=jnp.float32,
            ).astype(jnp.bfloat16),
            "chan",
            scatter_dimension=0,
            tiled=True,
        ).astype(jnp.float32)
        grad_conv = (
            grad_second * snake_slope(conv_result, snake_freq_pointwise[residual_unit_index])
        ).astype(jnp.bfloat16)
        src_masks = jnp.stack(
            [
                tap_mask((kernel_tap_index - 3) * spacing)
                for kernel_tap_index in range(kernel_tap_count)
            ]
        )
        masked_kernel = grad_conv[None, :, :] * src_masks[:, None, :].astype(jnp.bfloat16)
        dilated_gradient = lax.dot_general(
            masked_kernel,
            track_window_list,
            (((2,), (2,)), ((0,), (0,))),
            preferred_element_type=jnp.float32,
        )
        dilated_gradient_list[residual_unit_index] = dilated_gradient
        point_grads[residual_unit_index] = pointwise_gradient
        dilated_gradient_sum[residual_unit_index], pointwise_gradient_sum[residual_unit_index] = (
            lax.psum(dilated_gradient.astype(jnp.bfloat16), "tm").astype(jnp.float32),
            lax.psum(pointwise_gradient.astype(jnp.bfloat16), "tm").astype(jnp.float32),
        )
        if residual_unit_index > 0:
            grad_wide = with_halo(grad_conv, (("tm", 1),), margin)
            shifted = []
            for kernel_tap_index in range(kernel_tap_count):
                dest_mask = tap_mask(-(kernel_tap_index - 3) * spacing).astype(jnp.bfloat16)
                track_window = grad_wide[
                    :,
                    (6 - kernel_tap_index) * spacing : (6 - kernel_tap_index) * spacing + row_count,
                ]
                shifted.append(track_window * dest_mask[None, :])
            shifted = jnp.stack(shifted)
            grad_first = lax.psum_scatter(
                lax.dot_general(
                    dilated_effective,
                    shifted,
                    (((0, 1), (0, 1)), ((), ())),
                    preferred_element_type=jnp.float32,
                ).astype(jnp.bfloat16),
                "chan",
                scatter_dimension=0,
                tiled=True,
            ).astype(jnp.float32)
            grad_out = grad_out + grad_first * snake_slope(
                hidden_input, snake_freq_dilated[residual_unit_index]
            )
    dilated_gradient_total = jnp.stack(dilated_gradient_sum)
    pointwise_gradient_total = jnp.stack(pointwise_gradient_sum)
    dilated_effective_list = jnp.stack([list_entry[4] for list_entry in saved_residuals]).astype(
        jnp.float32
    )
    pointwise_effective_list = jnp.stack([list_entry[5] for list_entry in saved_residuals]).astype(
        jnp.float32
    )
    return (
        decoded,
        dilated_effective_list * dilated_gradient_total,
        pointwise_effective_list * pointwise_gradient_total,
    )


def solution(mesh):
    return jax.shard_map(
        per_device,
        mesh=mesh,
        in_specs=(
            P("chan", "tm"),
            P(None, "chan", "tm"),
            P(None, None, "chan", None),
            P(None, "chan", None),
            P(None, None, "chan", None),
            P(None, "chan", None),
            P("chan"),
            P(None, "chan"),
            P(None, "chan"),
            P(),
            P("chan", "tm"),
        ),
        out_specs=(P("chan", "tm"), P(None, None, "chan", None), P(None, "chan", None)),
        check_vma=False,
    )
```

profile of v0, /device:TPU:0, one launch (start us, length us, event | category | flops | bytes accessed | tf_op | source)
XLA Modules:
  0.0 477.6 jit_solution(5585210042914226931)
XLA Ops:
  8.3 4.8 %collective-permute-start = (bf16[256,1]{0,1:T(2,128)(2,1)S(1)}, bf16[256,1]{0,1:T(2,128)(2,1)S(1)}, u32[]{:S(2)}, u32[]{:S(2)}) collective-permute-start(bf16[256,1]{0,1:T(2,128)(2,1)S(1)} %get-tuple-element.59), channel_id=1, source_target_pairs={{0,8},{8,16},{16,24},{1,9},{9,17},{17,25},{2,10},{10,18},{18,26},{... | collective-permute-start | bytes 1544 | tf_op jit(solution)/shard_map/ppermute | solution.py:15
  15.4 3.3 collective-permute-done.1
  18.6 14.7 %all_gather.18 = bf16[2048,82]{0,1:T(8,128)(2,1)S(1)} all-gather(bf16[256,82]{0,1:T(8,128)(2,1)S(1)} %pad_maximum_fusion.6), channel_id=1, replica_groups=mesh['tm'=4,'chan'=8] {'chan'}, dimensions={0}, use_global_device_ids=true | all-gather | bytes 377856 | tf_op jit(solution)/shard_map/all_gather | solution.py:66
  33.3 66.7 %all-gather.6.cloned.1.call-done = bf16[16,128,2048]{2,1,0:T(8,128)(2,1)} async-done(((bf16[16,128,512]{2,1,0:T(8,128)(2,1)}), bf16[16,128,2048]{2,1,0:T(8,128)(2,1)}) %all-gather.6.cloned.1.call-update) | async-done | bytes 8388624 | tf_op jit(solution)/shard_map/all_gather | solution.py:67
  100.1 2.6 fusion.149
  104.4 2.2 slice-done
  108.3 1.9 add_convert_fusion.4
  110.7 1.9 broadcast_bitcast_fusion.2
  112.6 2.7 copy.37
  115.2 1.9 broadcast_bitcast_fusion
  117.1 2.5 copy.44
  121.1 4.8 %bitcast_multiply_fusion = (bf16[7,128,1024]{2,1,0:T(8,128)(2,1)}, bf16[7,128,1024]{2,1,0:T(8,128)(2,1)S(1)}) fusion(bf16[7,128,1024]{2,1,0:T(8,128)(2,1)} %copy.44, bf16[2,7,128,1024]{3,2,1,0:T(8,128)(2,1)} %param.13, bf16[7,128,1024]{2,1,0:T(8,128)(2,1)} %copy.37), kind=kLoop, calls=%fused_computation.6 | loop fusion | flops 1835008 | bytes 11010048 | tf_op jit(solution)/shard_map/mul | solution.py:116
  125.9 7.8 %all-gather.8.cloned.1.call-done = bf16[1024,640]{1,0:T(8,128)(2,1)} async-done(((bf16[128,640]{1,0:T(8,128)(2,1)}), bf16[1024,640]{1,0:T(8,128)(2,1)}) %all-gather.8.cloned.1.call-update) | async-done | bytes 1310736 | tf_op jit(solution)/shard_map/all_gather | solution.py:125
  135.1 3.4 collective-permute-start.2
  139.9 1.7 fusion.37
  141.8 10.2 %collective-permute-done.3 = bf16[1024,9]{1,0:T(8,128)(2,1)S(1)} collective-permute-done((bf16[1024,9]{1,0:T(8,128)(2,1)S(1)}, bf16[1024,9]{1,0:T(8,128)(2,1)S(1)}, u32[]{:S(2)}, u32[]{:S(2)}) %collective-permute-start.3) | collective-permute-done | bytes 18464 | tf_op jit(solution)/shard_map/ppermute | solution.py:17
  155.4 3.5 add_convert_fusion.3
  160.1 21.0 %all-gather.10.cloned.1.call-done = bf16[1024,640]{1,0:T(8,128)(2,1)} async-done(((bf16[128,640]{1,0:T(8,128)(2,1)}), bf16[1024,640]{1,0:T(8,128)(2,1)}) %all-gather.10.cloned.1.call-update) | async-done | bytes 1310736 | tf_op jit(solution)/shard_map/all_gather | solution.py:149
  181.1 3.5 add_convert_fusion.2
  185.7 1.6 convolution_convert_fusion.1
  188.0 19.7 %all-gather.12.cloned.1.call-done = bf16[1024,640]{1,0:T(8,128)(2,1)} async-done(((bf16[128,640]{1,0:T(8,128)(2,1)}), bf16[1024,640]{1,0:T(8,128)(2,1)}) %all-gather.12.cloned.1.call-update) | async-done | bytes 1310736 | tf_op jit(solution)/shard_map/all_gather | solution.py:125
  209.0 3.4 collective-permute-start.4
  213.9 2.5 fusion.36
  216.6 9.3 %collective-permute-done.5 = bf16[1024,27]{1,0:T(8,128)(2,1)S(1)} collective-permute-done((bf16[1024,27]{1,0:T(8,128)(2,1)S(1)}, bf16[1024,27]{1,0:T(8,128)(2,1)S(1)}, u32[]{:S(2)}, u32[]{:S(2)}) %collective-permute-start.5) | collective-permute-done | bytes 55328 | tf_op jit(solution)/shard_map/ppermute | solution.py:17
  232.9 9.6 %reduce-scatter.4.cloned.1.call-done = bf16[128,640]{1,0:T(8,128)(2,1)} async-done(((bf16[1024,640]{1,0:T(8,128)(2,1)}), bf16[128,640]{1,0:T(8,128)(2,1)}) %reduce-scatter.4.cloned.1.call-update) | async-done | bytes 163856 | tf_op jit(solution)/shard_map/reduce_scatter | solution.py:187
  242.5 5.1 %multiply_convert_fusion.1 = (bf16[128,640]{1,0:T(8,128)(2,1)S(1)}, bf16[128,640]{1,0:T(8,128)(2,1)}) fusion(bf16[128,640]{1,0:T(8,128)(2,1)} %reduce-scatter.4.cloned.1.call-done, f32[128]{0:T(128)} %get-tuple-element.89, f32[128]{0:T(128)S(1)} %copy-done.47, f32[128,640]{1,0:T(8,128)} %convolution_multiply_fusion, ...), kind=kOutput, calls=%fused_computation.99 | convolution fusion | flops 171786240 | bytes 4296192 | tf_op jit(solution)/shard_map/dot_general | solution.py:141
  249.2 4.5 collective-permute-start.7
  255.7 2.9 bitcast_convert_fusion
  261.8 2.6 bitcast_dynamic-update-slice_fusion.13
  264.3 1.7 bitcast_dynamic-update-slice_fusion.12
  266.0 1.7 bitcast_dynamic-update-slice_fusion.11
  269.6 1.7 bitcast_dynamic-update-slice_fusion.9
  271.3 1.7 bitcast_dynamic-update-slice_fusion.8
  273.0 18.9 %reduce-scatter.6.cloned.1.call-done = bf16[128,640]{1,0:T(8,128)(2,1)} async-done(((bf16[1024,640]{1,0:T(8,128)(2,1)}), bf16[128,640]{1,0:T(8,128)(2,1)}) %reduce-scatter.6.cloned.1.call-update) | async-done | bytes 163856 | tf_op jit(solution)/shard_map/reduce_scatter | solution.py:231
  291.9 2.1 add_convert_fusion
  294.0 1.6 convolution_convert_fusion
  296.0 3.1 bitcast_dynamic-update-slice_fusion.7
  304.2 4.3 convert_bitcast_fusion
  308.6 7.1 %all-gather.14.cloned.1.call-done = bf16[1024,640]{1,0:T(8,128)(2,1)} async-done(((bf16[128,640]{1,0:T(8,128)(2,1)}), bf16[1024,640]{1,0:T(8,128)(2,1)}) %all-gather.14.cloned.1.call-update) | async-done | bytes 1310736 | tf_op jit(solution)/shard_map/all_gather | solution.py:149
  315.6 2.6 fusion.17
  319.4 31.3 %reduce-scatter.8.cloned.1.call-done = bf16[128,640]{1,0:T(8,128)(2,1)} async-done(((bf16[1024,640]{1,0:T(8,128)(2,1)}), bf16[128,640]{1,0:T(8,128)(2,1)}) %reduce-scatter.8.cloned.1.call-update) | async-done | bytes 163856 | tf_op jit(solution)/shard_map/reduce_scatter | solution.py:187
  350.7 2.1 multiply_convert_fusion
  352.8 7.8 %convert_bitcast_fusion.1 = bf16[1,7,128,1024]{3,2,1,0:T(8,128)(2,1)} fusion(bf16[7,1024,640]{2,1,0:T(8,128)(2,1)} %bitcast_dynamic-update-slice_fusion.7, bf16[7,640]{1,0:T(8,128)(2,1)S(1)} %stack.156, bf16[128,640]{1,0:T(8,128)(2,1)S(1)} %multiply_convert_fusion), kind=kOutput, calls=%fused_computation.9 | convolution fusion | flops 1175896064 | bytes 11182848 | tf_op jit(solution)/shard_map/dot_general | solution.py:208
  362.3 2.9 copy.45
  365.2 3.8 copy.46
  369.9 5.1 %slice_multiply_fusion.1 = (bf16[1,7,128,1024]{3,2,1,0:T(8,128)(2,1)S(1)}, bf16[1,7,128,1024]{3,2,1,0:T(8,128)(2,1)}) fusion(bf16[1,7,128,1024]{3,2,1,0:T(8,128)(2,1)} %copy.45, bf16[2,7,128,1024]{3,2,1,0:T(8,128)(2,1)} %param.13, bf16[1,7,128,1024]{3,2,1,0:T(8,128)(2,1)} %copy.46), kind=kLoop, calls=%fused_computation.11 | loop fusion | flops 1835008 | bytes 11010048 | tf_op jit(solution)/shard_map/mul | solution.py:116
  376.1 87.6 %all-reduce.3.cloned.1.call-done = (bf16[1,7,128,1024]{3,2,1,0:T(8,128)(2,1)}, bf16[1,7,128,1024]{3,2,1,0:T(8,128)(2,1)}, bf16[1,128,1024]{2,1,0:T(8,128)(2,1)}, bf16[1,128,1024]{2,1,0:T(8,128)(2,1)}) async-done(((bf16[1,7,128,1024]{3,2,1,0:T(8,128)(2,1)}, bf16[1,7,128,1024]{3,2,1,0:T(8,128)(2,1)}, bf16[1,128,1024]{2,1,0:T(8,128)(2,1)}, bf16[1,128,1024]{2,1,0:T(8,128)(2,1)}), ...) | async-done | bytes 4194320 | tf_op jit(solution)/shard_map/psum | solution.py:217
  463.7 5.7 %convert_multiply_fusion = f32[2,7,128,1024]{3,2,1,0:T(8,128)} fusion(bf16[1,7,128,1024]{3,2,1,0:T(8,128)(2,1)} %get-tuple-element.38, bf16[1,7,128,1024]{3,2,1,0:T(8,128)(2,1)S(1)} %get-tuple-element.37, bf16[1,7,128,1024]{3,2,1,0:T(8,128)(2,1)} %get-tuple-element.17, bf16[1,7,128,1024]{3,2,1,0:T(8,128)(2,1)} %get-tuple-element.18), kind=kLoop, calls=%fused_computation | loop fusion | flops 9175040 | bytes 14680064 | tf_op jit(solution)/shard_map/mul | solution.py:255
  (219 shorter events, 47.2 us)
Async XLA Ops:
  7.2 7.3 %copy-start.48 = (s32[3]{0:T(128)S(1)}, s32[3]{0:T(128)}, u32[]{:S(2)}) copy-start(s32[3]{0:T(128)} %param.20) | copy-start | bytes 40
  7.2 7.6 %copy-start.44 = (f32[2,128]{1,0:T(2,128)S(1)}, f32[2,128]{1,0:T(2,128)}, u32[]{:S(2)}) copy-start(f32[2,128]{1,0:T(2,128)} %param.18) | copy-start | bytes 3076
  7.2 92.9 %all-gather.6.cloned.1.call-start = ((), (), s32[]{:S(2)}) async-start(), calls=%async_computation.3 | async-start | bytes 10485760 | tf_op jit(solution)/shard_map/all_gather | solution.py:67
  7.9 125.8 %all-gather.8.cloned.1.call-start = ((), (), s32[]{:S(2)}) async-start(), calls=%async_computation.4 | async-start | bytes 1474560 | tf_op jit(solution)/shard_map/all_gather | solution.py:125
  8.3 7.1 %collective-permute-start = (bf16[256,1]{0,1:T(2,128)(2,1)S(1)}, bf16[256,1]{0,1:T(2,128)(2,1)S(1)}, u32[]{:S(2)}, u32[]{:S(2)}) collective-permute-start(bf16[256,1]{0,1:T(2,128)(2,1)S(1)} %get-tuple-element.59), channel_id=1, source_target_pairs={{0,8},{8,16},{16,24},{1,9},{9,17},{17,25},{2,10},{10,18},{18,26},{... | collective-permute-start | bytes 1544 | tf_op jit(solution)/shard_map/ppermute | solution.py:15
  13.2 5.5 %collective-permute-start.1 = (bf16[256,1]{0,1:T(2,128)(2,1)S(1)}, bf16[256,1]{0,1:T(2,128)(2,1)S(1)}, u32[]{:S(2)}, u32[]{:S(2)}) collective-permute-start(bf16[256,1]{0,1:T(2,128)(2,1)S(1)} %get-tuple-element.60), channel_id=1, source_target_pairs={{8,0},{16,8},{24,16},{9,1},{17,9},{25,17},{10,2},{18,10},{26,18},{... | collective-permute-start | bytes 1544 | tf_op jit(solution)/shard_map/ppermute | solution.py:17
  110.2 70.9 %all-gather.10.cloned.1.call-start = ((), (), s32[]{:S(2)}) async-start(), calls=%async_computation.5 | async-start | bytes 1474560 | tf_op jit(solution)/shard_map/all_gather | solution.py:149
  121.1 32.1 %copy-start.36 = (f32[640]{0:T(1024)}, f32[640]{0:T(1024)S(1)}, u32[]{:S(2)}) copy-start(f32[640]{0:T(1024)S(1)} %get-tuple-element.70) | copy-start | bytes 7684
  121.1 34.2 %copy-start.39 = (f32[640]{0:T(1024)}, f32[640]{0:T(1024)S(1)}, u32[]{:S(2)}) copy-start(f32[640]{0:T(1024)S(1)} %get-tuple-element.78) | copy-start | bytes 7684
  125.9 28.7 %copy-start.11 = (bf16[7,128,1024]{2,1,0:T(8,128)(2,1)}, bf16[7,128,1024]{2,1,0:T(8,128)(2,1)S(1)}, u32[]{:S(2)}) copy-start(bf16[7,128,1024]{2,1,0:T(8,128)(2,1)S(1)} %get-tuple-element.40) | copy-start | bytes 5505028
  133.8 7.9 %copy-start = (bf16[1024,640]{1,0:T(8,128)(2,1)S(1)}, bf16[1024,640]{1,0:T(8,128)(2,1)}, u32[]{:S(2)}) copy-start(bf16[1024,640]{1,0:T(8,128)(2,1)} %all-gather.8.cloned.1.call-done) | copy-start | bytes 3932164
  135.1 18.9 %collective-permute-start.2 = (bf16[1024,9]{1,0:T(8,128)(2,1)S(1)}, bf16[1024,9]{1,0:T(8,128)(2,1)S(1)}, u32[]{:S(2)}, u32[]{:S(2)}) collective-permute-start(bf16[1024,9]{1,0:T(8,128)(2,1)S(1)} %get-tuple-element.43), channel_id=1, source_target_pairs={{0,8},{8,16},{16,24},{1,9},{9,17},{17,25},{2,10},{10,18},{18,26},{... | collective-permute-start | bytes 55304 | tf_op jit(solution)/shard_map/ppermute | solution.py:15
  138.5 13.5 %collective-permute-start.3 = (bf16[1024,9]{1,0:T(8,128)(2,1)S(1)}, bf16[1024,9]{1,0:T(8,128)(2,1)S(1)}, u32[]{:S(2)}, u32[]{:S(2)}) collective-permute-start(bf16[1024,9]{1,0:T(8,128)(2,1)S(1)} %get-tuple-element.44), channel_id=1, source_target_pairs={{8,0},{16,8},{24,16},{9,1},{17,9},{25,17},{10,2},{18,10},{26,18},{... | collective-permute-start | bytes 55304 | tf_op jit(solution)/shard_map/ppermute | solution.py:17
  155.3 3.6 copy-start.34
  155.4 25.7 %copy-start.8 = (bf16[2,128,1024]{2,1,0:T(8,128)(2,1)S(1)}, bf16[2,128,1024]{2,1,0:T(8,128)(2,1)}, u32[]{:S(2)}) copy-start(bf16[2,128,1024]{2,1,0:T(8,128)(2,1)} %param.14) | copy-start | bytes 1572868
  155.4 25.7 %copy-start.23 = (f32[128,640]{1,0:T(8,128)S(1)}, f32[128,640]{1,0:T(8,128)}, u32[]{:S(2)}) copy-start(f32[128,640]{1,0:T(8,128)} %copy-done.22) | copy-start | bytes 983044
  155.4 25.7 %copy-start.46 = (f32[128]{0:T(128)S(1)}, f32[128]{0:T(128)}, u32[]{:S(2)}) copy-start(f32[128]{0:T(128)} %get-tuple-element.92) | copy-start | bytes 1540
  158.9 48.8 %all-gather.12.cloned.1.call-start = ((), (), s32[]{:S(2)}) async-start(), calls=%async_computation.6 | async-start | bytes 1474560 | tf_op jit(solution)/shard_map/all_gather | solution.py:125
  160.1 24.5 %copy-start.24 = (bf16[128,1024]{1,0:T(8,128)(2,1)}, bf16[128,1024]{1,0:T(8,128)(2,1)S(1)}, u32[]{:S(2)}) copy-start(bf16[128,1024]{1,0:T(8,128)(2,1)S(1)} %copy.35) | copy-start | bytes 786436
  181.1 4.6 copy-start.18
  184.6 57.9 %reduce-scatter.4.cloned.1.call-start = ((), (), s32[]{:S(2)}) async-start(), calls=%async_computation.8 | async-start | bytes 1474560 | tf_op jit(solution)/shard_map/reduce_scatter | solution.py:187
  187.4 104.5 %reduce-scatter.6.cloned.1.call-start = ((), (), s32[]{:S(2)}) async-start(), calls=%async_computation.9 | async-start | bytes 1474560 | tf_op jit(solution)/shard_map/reduce_scatter | solution.py:231
  207.7 8.7 %copy-start.1 = (bf16[1024,640]{1,0:T(8,128)(2,1)S(1)}, bf16[1024,640]{1,0:T(8,128)(2,1)}, u32[]{:S(2)}) copy-start(bf16[1024,640]{1,0:T(8,128)(2,1)} %all-gather.12.cloned.1.call-done) | copy-start | bytes 3932164
  209.0 16.9 %collective-permute-start.4 = (bf16[1024,27]{1,0:T(8,128)(2,1)S(1)}, bf16[1024,27]{1,0:T(8,128)(2,1)S(1)}, u32[]{:S(2)}, u32[]{:S(2)}) collective-permute-start(bf16[1024,27]{1,0:T(8,128)(2,1)S(1)} %get-tuple-element.41), channel_id=1, source_target_pairs={{0,8},{8,16},{16,24},{1,9},{9,17},{17,25},{2,10},{10,18},{18,26},{... | collective-permute-start | bytes 165896 | tf_op jit(solution)/shard_map/ppermute | solution.py:15
  212.4 13.5 %collective-permute-start.5 = (bf16[1024,27]{1,0:T(8,128)(2,1)S(1)}, bf16[1024,27]{1,0:T(8,128)(2,1)S(1)}, u32[]{:S(2)}, u32[]{:S(2)}) collective-permute-start(bf16[1024,27]{1,0:T(8,128)(2,1)S(1)} %get-tuple-element.42), channel_id=1, source_target_pairs={{8,0},{16,8},{24,16},{9,1},{17,9},{25,17},{10,2},{18,10},{26,18},{... | collective-permute-start | bytes 165896 | tf_op jit(solution)/shard_map/ppermute | solution.py:17
  216.4 9.5 %copy-start.9 = (bf16[7,128,1024]{2,1,0:T(8,128)(2,1)S(1)}, bf16[7,128,1024]{2,1,0:T(8,128)(2,1)}, u32[]{:S(2)}) copy-start(bf16[7,128,1024]{2,1,0:T(8,128)(2,1)} %get-tuple-element.39) | copy-start | bytes 5505028
  216.4 9.5 %copy-start.40 = (f32[640]{0:T(1024)S(1)}, f32[640]{0:T(1024)}, u32[]{:S(2)}) copy-start(f32[640]{0:T(1024)} %copy-done.39) | copy-start | bytes 7684
  216.6 10.9 %copy-start.38 = (f32[640]{0:T(1024)S(1)}, f32[640]{0:T(1024)}, u32[]{:S(2)}) copy-start(f32[640]{0:T(1024)} %get-tuple-element.72) | copy-start | bytes 7684
  225.9 5.6 %copy-start.4 = (bf16[1024,667]{1,0:T(8,128)(2,1)}, bf16[1024,667]{1,0:T(8,128)(2,1)S(1)}, u32[]{:S(2)}) copy-start(bf16[1024,667]{1,0:T(8,128)(2,1)S(1)} %constant_dynamic-update-slice_fusion.2) | copy-start | bytes 4098052
  231.5 11.0 %copy-start.47 = (f32[128]{0:T(128)S(1)}, f32[128]{0:T(128)}, u32[]{:S(2)}) copy-start(f32[128]{0:T(128)} %get-tuple-element.90) | copy-start | bytes 1540
  247.7 8.0 %copy-start.10 = (bf16[7,128,1024]{2,1,0:T(8,128)(2,1)S(1)}, bf16[7,128,1024]{2,1,0:T(8,128)(2,1)}, u32[]{:S(2)}) copy-start(bf16[7,128,1024]{2,1,0:T(8,128)(2,1)} %get-tuple-element.39) | copy-start | bytes 5505028
  247.8 6.0 %collective-permute-start.6 = (bf16[128,27]{1,0:T(8,128)(2,1)S(1)}, bf16[128,27]{1,0:T(8,128)(2,1)S(1)}, u32[]{:S(2)}, u32[]{:S(2)}) collective-permute-start(bf16[128,27]{1,0:T(8,128)(2,1)S(1)} %get-tuple-element.56), channel_id=1, source_target_pairs={{8,0},{16,8},{24,16},{9,1},{17,9},{25,17},{10,2},{18,10},{26,18},{... | collective-permute-start | bytes 20744 | tf_op jit(solution)/shard_map/ppermute | solution.py:17
  249.2 6.1 %collective-permute-start.7 = (bf16[128,27]{1,0:T(8,128)(2,1)S(1)}, bf16[128,27]{1,0:T(8,128)(2,1)S(1)}, u32[]{:S(2)}, u32[]{:S(2)}) collective-permute-start(bf16[128,27]{1,0:T(8,128)(2,1)S(1)} %get-tuple-element.55), channel_id=1, source_target_pairs={{0,8},{8,16},{16,24},{1,9},{9,17},{17,25},{2,10},{10,18},{18,26},{... | collective-permute-start | bytes 20744 | tf_op jit(solution)/shard_map/ppermute | solution.py:15
  258.7 57.0 %all-gather.14.cloned.1.call-start = ((), (), s32[]{:S(2)}) async-start(), calls=%async_computation.7 | async-start | bytes 1474560 | tf_op jit(solution)/shard_map/all_gather | solution.py:149
  259.4 91.3 %reduce-scatter.8.cloned.1.call-start = ((), (), s32[]{:S(2)}) async-start(), calls=%async_computation.10 | async-start | bytes 1474560 | tf_op jit(solution)/shard_map/reduce_scatter | solution.py:187
  271.3 20.6 %copy-start.19 = (f32[128,640]{1,0:T(8,128)S(1)}, f32[128,640]{1,0:T(8,128)}, u32[]{:S(2)}) copy-start(f32[128,640]{1,0:T(8,128)} %get-tuple-element.99) | copy-start | bytes 983044
  271.3 22.7 %copy-start.25 = (bf16[128,1024]{1,0:T(8,128)(2,1)S(1)}, bf16[128,1024]{1,0:T(8,128)(2,1)}, u32[]{:S(2)}) copy-start(bf16[128,1024]{1,0:T(8,128)(2,1)} %copy-done.24) | copy-start | bytes 786436
  295.7 168.0 %all-reduce.3.cloned.1.call-start = ((), (), s32[]{:S(2)}) async-start(), calls=%async_computation.11 | async-start | bytes 8388608 | tf_op jit(solution)/shard_map/psum | solution.py:217
  308.5 9.6 %copy-start.21 = (bf16[1024,640]{1,0:T(8,128)(2,1)S(1)}, bf16[1024,640]{1,0:T(8,128)(2,1)}, u32[]{:S(2)}) copy-start(bf16[1024,640]{1,0:T(8,128)(2,1)} %all-gather.10.cloned.1.call-done) | copy-start | bytes 3932164
  308.5 42.2 %copy-start.31 = (f32[128,640]{1,0:T(8,128)S(1)}, f32[128,640]{1,0:T(8,128)}, u32[]{:S(2)}) copy-start(f32[128,640]{1,0:T(8,128)} %get-tuple-element.97) | copy-start | bytes 983044
  308.5 42.2 %copy-start.43 = (f32[128]{0:T(128)S(1)}, f32[128]{0:T(128)}, u32[]{:S(2)}) copy-start(f32[128]{0:T(128)} %get-tuple-element.88) | copy-start | bytes 1540
  369.9 5.1 %copy-start.7 = (bf16[1024,640]{1,0:T(8,128)(2,1)S(1)}, bf16[1024,640]{1,0:T(8,128)(2,1)}, u32[]{:S(2)}) copy-start(bf16[1024,640]{1,0:T(8,128)(2,1)} %all-gather.14.cloned.1.call-done) | copy-start | bytes 3932164
  369.9 5.1 %copy-start.13 = (bf16[128,1024]{1,0:T(8,128)(2,1)S(1)}, bf16[128,1024]{1,0:T(8,128)(2,1)}, u32[]{:S(2)}) copy-start(bf16[128,1024]{1,0:T(8,128)(2,1)} %copy-done.12) | copy-start | bytes 786436
  369.9 5.1 %copy-start.20 = (f32[128,640]{1,0:T(8,128)S(1)}, f32[128,640]{1,0:T(8,128)}, u32[]{:S(2)}) copy-start(f32[128,640]{1,0:T(8,128)} %get-tuple-element.99) | copy-start | bytes 983044
  463.7 5.7 %copy-start.28 = (bf16[1,128,1024]{2,1,0:T(8,128)(2,1)S(1)}, bf16[1,128,1024]{2,1,0:T(8,128)(2,1)}, u32[]{:S(2)}) copy-start(bf16[1,128,1024]{2,1,0:T(8,128)(2,1)} %get-tuple-element.47) | copy-start | bytes 786436
  463.7 5.7 %copy-start.29 = (bf16[1,128,1024]{2,1,0:T(8,128)(2,1)S(1)}, bf16[1,128,1024]{2,1,0:T(8,128)(2,1)}, u32[]{:S(2)}) copy-start(bf16[1,128,1024]{2,1,0:T(8,128)(2,1)} %get-tuple-element.48) | copy-start | bytes 786436
  463.7 5.7 %copy-start.32 = (bf16[1,128,1024]{2,1,0:T(8,128)(2,1)S(1)}, bf16[1,128,1024]{2,1,0:T(8,128)(2,1)}, u32[]{:S(2)}) copy-start(bf16[1,128,1024]{2,1,0:T(8,128)(2,1)} %get-tuple-element.19) | copy-start | bytes 786436
  463.7 5.7 %copy-start.33 = (bf16[1,128,1024]{2,1,0:T(8,128)(2,1)S(1)}, bf16[1,128,1024]{2,1,0:T(8,128)(2,1)}, u32[]{:S(2)}) copy-start(bf16[1,128,1024]{2,1,0:T(8,128)(2,1)} %get-tuple-element.20) | copy-start | bytes 786436
  (19 other events, 35.3 us)
Sparse Core Ops, SparseCore 0:
  9.9 90.1 all-gather.5
  110.3 23.4 all-gather.7
  159.0 22.0 all-gather.9
  184.8 22.9 all-gather.11
  209.8 32.6 reduce-scatter.3
  258.8 33.0 reduce-scatter.5
  294.1 21.4 all-gather.13
  317.9 32.7 reduce-scatter.7
  360.8 102.8 all-reduce.2
where the time goes:
time: 485 us; the launch traced here: 478 us
  waiting for transfers between devices  295 us (61%)
  matrix products  52.6 us (11%)
  local copies, waits for them, and re-layouts  41.7 us (9%)
  other arithmetic  36 us (7%)
  starting transfers between devices  22.5 us (5%)
  between operations  15.2 us (3%)
  blocking collectives  14.7 us (3%)
    psum x1, waiting for transfers between devices, per_device(): lax.psum(dilated_gradient.astype(jnp.bfloat16), 'tm').astype(jnp.float32)  87.6 us
    all_gather x1, waiting for transfers between devices, per_device(): weight_block = lax.all_gather(upsample_kernel, 'tm', axis=2, tiled=True)  66.7 us
    reduce_scatter x2, waiting for transfers between devices, per_device(): lax.psum_scatter(lax.dot_general(pointwise_effective, grad_b, (((0,), (0,...  40.9 us
    all_gather x2, waiting for transfers between devices, per_device(): lax.all_gather(second_activation, 'chan', axis=0, tiled=True)  28.1 us
    all_gather x2, waiting for transfers between devices, per_device(): first_all = lax.all_gather(first, 'chan', axis=0, tiled=True)  27.6 us
    dot_general x14, matrix products, per_device(): jnp.dot(dilated_effective[kernel_tap_index], track_window_list[kernel_tap...  23 us
    ppermute x4, waiting for transfers between devices, with_halo(): lax.ppermute(head, axis, [((i + 1) % count, i) for i in range(ends)])  22.7 us
    reduce_scatter x1, waiting for transfers between devices, per_device(): lax.psum_scatter(lax.dot_general(dilated_effective, shifted, (((0, 1), (0...  18.9 us
  transfers between devices with their start and end apart: 17, of which 13 were waited for; matrix products, arithmetic and copies ran while one was open for 17% of the time, Pallas kernels for 0%

commit v1 on v0

v1 whole, which is shorter than its diff:
```python
import functools

import jax
import jax.numpy as jnp
from jax import lax
from jax.experimental import pallas as pl
from jax.experimental.pallas import tpu as pltpu
from jax.sharding import PartitionSpec as P

MESH = pl.DeviceIdType.MESH
BF16 = jnp.bfloat16
F32 = jnp.float32
VMEM_LIMIT = 48 * 1024 * 1024


def remote(src, dst, send, recv, device):
    return pltpu.make_async_remote_copy(
        src_ref=src, dst_ref=dst, send_sem=send, recv_sem=recv, device_id=device, device_id_type=MESH
    )


def greet(devices):
    barrier = pltpu.get_barrier_semaphore()
    for device in devices:
        pl.semaphore_signal(barrier, inc=1, device_id=device, device_id_type=MESH)
    pl.semaphore_wait(barrier, len(devices))


def chan_place():
    tm, chan = lax.axis_index("tm"), lax.axis_index("chan")
    chips = lax.axis_size("chan") // 2
    chip, core = chan // 2, chan % 2
    partner = (tm, chan + 1 - 2 * core)

    def at(step):
        return ((chip + step + chips) % chips) * 2 + core

    return tm, chan, core, chips, partner, at


def column(index, width):
    return pl.ds(pl.multiple_of(index * width, width), width)


def chan_gather_kernel(halo, x_ref, o_ref, send, recv, fsend, frecv, hsend, hrecv):
    tm, chan, core, chips, partner, at = chan_place()
    frames = lax.axis_size("tm")
    rows, width = x_ref.shape
    greeted = [partner] + [(tm, at(step)) for step in range(1, chips)]
    after = ((tm + 1) % frames, chan)
    before = ((tm + frames - 1) % frames, chan)
    if halo:
        greeted += [before, after]
    greet(greeted)
    spans = [pl.ds(halo, rows)]
    sources = [x_ref]
    mine = column(chan, width)
    if halo:
        spans += [pl.ds(0, halo), pl.ds(halo + rows, halo)]
        sources += [o_ref.at[spans[1], mine], o_ref.at[spans[2], mine]]
        edges = [
            remote(x_ref.at[pl.ds(rows - halo, halo)], o_ref.at[spans[1], mine], hsend.at[0], hrecv.at[0], after),
            remote(x_ref.at[pl.ds(0, halo)], o_ref.at[spans[2], mine], hsend.at[1], hrecv.at[1], before),
        ]
        for edge in edges:
            edge.start()
    started = []

    def spread(part):
        for step in range(1, chips):
            copy = remote(
                sources[part], o_ref.at[spans[part], mine], send.at[part, step], recv.at[part, step], (tm, at(step))
            )
            copy.start()
            started.append(copy)
        copy = remote(sources[part], o_ref.at[spans[part], mine], send.at[part, 0], recv.at[part, 0], partner)
        copy.start()
        started.append(copy)

    spread(0)
    if halo:
        for edge in edges:
            edge.wait_recv()
        spread(1)
        spread(2)
    o_ref[spans[0], mine] = x_ref[...]

    def arrival(part, index, sems, step):
        slot = o_ref.at[spans[part], column(index, width)]
        return remote(slot, slot, send.at[part, step], sems.at[part, step], partner)

    for step in range(1, chips):
        for part in range(len(spans)):
            index = at(-step)
            arrival(part, index, recv, step).wait_recv()
            slot = o_ref.at[spans[part], column(index, width)]
            copy = remote(slot, slot, fsend.at[part, step], frecv.at[part, step], partner)
            copy.start()
            started.append(copy)
    other = 1 - 2 * core
    for part in range(len(spans)):
        arrival(part, chan + other, recv, 0).wait_recv()
        for step in range(1, chips):
            arrival(part, at(-step) + other, frecv, step).wait_recv()
    for copy in started:
        copy.wait_send()
    if halo:
        for edge in edges:
            edge.wait_send()


def chan_scatter_kernel(x_ref, o_ref, pair, summed, landed, psend, precv, send, recv):
    tm, chan, core, chips, partner, at = chan_place()
    width = o_ref.shape[1]
    greet([partner] + [(tm, at(step)) for step in range(1, chips)])
    other = 1 - 2 * core
    order = list(range(1, chips)) + [0]
    started = []
    pairs = {}
    for step in order:
        copy = remote(
            x_ref.at[:, column(at(step) + other, width)], pair.at[step], psend.at[step], precv.at[step], partner
        )
        copy.start()
        pairs[step] = copy
    for step in range(1, chips):
        pairs[step].wait_recv()
        summed[step] = (
            x_ref[:, column(at(step), width)].astype(F32) + pair[step].astype(F32)
        ).astype(summed.dtype)
        copy = remote(summed.at[step], landed.at[step], send.at[step], recv.at[step], (tm, at(step)))
        copy.start()
        started.append(copy)
    pairs[0].wait_recv()
    o_ref[...] = x_ref[:, column(chan, width)].astype(F32) + pair[0].astype(F32)
    for copy, step in zip(started, range(1, chips)):
        copy.wait_recv()
        o_ref[...] += landed[step].astype(F32)
    for copy in started:
        copy.wait_send()
    for step in order:
        pairs[step].wait_send()


def tm_scatter_kernel(x_ref, o_ref, landed, send, recv):
    tm, chan = lax.axis_index("tm"), lax.axis_index("chan")
    count = lax.axis_size("tm")
    rows = o_ref.shape[0]
    greet([((tm + step) % count, chan) for step in range(1, count)])
    started = []
    for step in range(1, count):
        to = (tm + step) % count
        copy = remote(
            x_ref.at[pl.ds(pl.multiple_of(to * rows, rows), rows)],
            landed.at[step],
            send.at[step],
            recv.at[step],
            (to, chan),
        )
        copy.start()
        started.append(copy)
    o_ref[...] = x_ref[pl.ds(pl.multiple_of(tm * rows, rows), rows)].astype(F32)
    for step in range(1, count):
        started[step - 1].wait_recv()
        o_ref[...] += landed[step].astype(F32)
    for copy in started:
        copy.wait_send()


def tm_gather_kernel(x_ref, o_ref, send, recv):
    tm, chan = lax.axis_index("tm"), lax.axis_index("chan")
    count = lax.axis_size("tm")
    rows = x_ref.shape[0]
    greet([((tm + step) % count, chan) for step in range(1, count)])

    def slot(index):
        return o_ref.at[pl.ds(pl.multiple_of(index * rows, rows), rows)]

    started = []
    for step in range(1, count):
        copy = remote(x_ref, slot(tm), send.at[step], recv.at[step], ((tm + step) % count, chan))
        copy.start()
        started.append(copy)
    o_ref[pl.ds(pl.multiple_of(tm * rows, rows), rows)] = x_ref[...]
    for step in range(1, count):
        landing = slot((tm + count - step) % count)
        remote(landing, landing, send.at[step], recv.at[step], (tm, chan)).wait_recv()
    for copy in started:
        copy.wait_send()


def turn_kernel(x_ref, o_ref, send, recv):
    tm, chan = lax.axis_index("tm"), lax.axis_index("chan")
    frames, chans = lax.axis_size("tm"), lax.axis_size("chan")
    ratio = chans // frames
    rows, width = x_ref.shape
    target = chan // ratio
    own = target == tm
    barrier = pltpu.get_barrier_semaphore()
    for frame in range(frames):
        for part in range(ratio):
            source = (frame, tm * ratio + part)

            @pl.when(jnp.logical_or(frame != tm, source[1] != chan))
            def _():
                pl.semaphore_signal(barrier, inc=1, device_id=source, device_id_type=MESH)

    @pl.when(own)
    def _():
        pl.semaphore_wait(barrier, chans - 1)

    @pl.when(jnp.logical_not(own))
    def _():
        pl.semaphore_wait(barrier, chans)

    slot_rows = pl.ds(pl.multiple_of(tm * rows, rows), rows)
    slot_columns = column(chan % ratio, width)
    which = tm * ratio + chan % ratio

    def outgoing(step):
        return remote(
            x_ref,
            o_ref.at[slot_rows, slot_columns],
            send.at[step],
            recv.at[which],
            (target, (chan + step) % chans),
        )

    for step in range(1, chans):
        outgoing(step).start()

    @pl.when(own)
    def _():
        o_ref[slot_rows, slot_columns] = x_ref[...]

    @pl.when(jnp.logical_not(own))
    def _():
        outgoing(0).start()

    for frame in range(frames):
        for part in range(ratio):

            @pl.when(jnp.logical_or(frame != tm, tm * ratio + part != chan))
            def _():
                landing = o_ref.at[pl.ds(frame * rows, rows), pl.ds(part * width, width)]
                remote(
                    landing, landing, send.at[0], recv.at[frame * ratio + part], (tm, chan)
                ).wait_recv()

    for step in range(1, chans):
        outgoing(step).wait_send()

    @pl.when(jnp.logical_not(own))
    def _():
        outgoing(0).wait_send()


def run(kernel, out_shape, dtype, scratch, number, value):
    whole = pl.BlockSpec(memory_space=pltpu.VMEM)
    return pl.pallas_call(
        kernel,
        out_shape=jax.ShapeDtypeStruct(out_shape, dtype),
        in_specs=[whole],
        out_specs=whole,
        scratch_shapes=scratch,
        compiler_params=pltpu.CompilerParams(
            collective_id=number, has_side_effects=True, vmem_limit_bytes=VMEM_LIMIT
        ),
    )(value)


def plain_kernels(*widths):
    return all(width % 128 == 0 for width in widths)


def with_halo(cells, width):
    count = lax.axis_size("tm")
    head, tail = cells[:width], cells[-width:]
    return jnp.concatenate(
        [
            lax.ppermute(tail, "tm", [(i, (i + 1) % count) for i in range(count)]),
            cells,
            lax.ppermute(head, "tm", [((i + 1) % count, i) for i in range(count)]),
        ],
        axis=0,
    )


def chan_gather(value, halo, number):
    rows, width = value.shape
    chans = lax.axis_size("chan")
    if not plain_kernels(width):
        return lax.all_gather(with_halo(value, halo) if halo else value, "chan", axis=1, tiled=True)
    chips = chans // 2
    dma = pltpu.SemaphoreType.DMA
    return run(
        functools.partial(chan_gather_kernel, halo),
        (rows + 2 * halo, width * chans),
        value.dtype,
        [dma((3, chips))] * 4 + [dma((2,))] * 2,
        number,
        value,
    )


def chan_scatter(value, number):
    rows, total = value.shape
    chans = lax.axis_size("chan")
    width = total // chans
    if not plain_kernels(width):
        return lax.psum_scatter(value, "chan", scatter_dimension=1, tiled=True).astype(F32)
    chips = chans // 2
    dma = pltpu.SemaphoreType.DMA
    return run(
        chan_scatter_kernel,
        (rows, width),
        F32,
        [pltpu.VMEM((chips, rows, width), value.dtype)] * 3 + [dma((chips,))] * 4,
        number,
        value,
    )


def tm_scatter(value, number):
    count = lax.axis_size("tm")
    rows, width = value.shape[0] // count, value.shape[1]
    if not plain_kernels(width):
        return lax.psum_scatter(value, "tm", scatter_dimension=0, tiled=True).astype(F32)
    dma = pltpu.SemaphoreType.DMA
    return run(
        tm_scatter_kernel,
        (rows, width),
        F32,
        [pltpu.VMEM((count, rows, width), value.dtype)] + [dma((count,))] * 2,
        number,
        value,
    )


def tm_gather(value, number):
    count = lax.axis_size("tm")
    rows, width = value.shape
    if not plain_kernels(width):
        return lax.all_gather(value, "tm", axis=0, tiled=True)
    return run(
        tm_gather_kernel, (rows * count, width), value.dtype, [pltpu.SemaphoreType.DMA((count,))] * 2, number, value
    )


def turn(value, number):
    frames, chans = lax.axis_size("tm"), lax.axis_size("chan")
    rows, width = value.shape
    if not plain_kernels(width) or chans % frames:
        return lax.all_to_all(
            lax.all_gather(value, "chan", axis=1, tiled=True), "tm", split_axis=1, concat_axis=0, tiled=True
        )
    return run(
        turn_kernel,
        (rows * frames, width * chans // frames),
        value.dtype,
        [pltpu.SemaphoreType.DMA((chans,))] * 2,
        number,
        value,
    )


def snake_act(values, alpha):
    return values + jnp.sin(alpha * values) ** 2 / alpha


def snake_slope(values, alpha):
    return 1.0 + jnp.sin(2.0 * alpha * values)


def track_ids(lengths, frame_index, total_frames):
    starts = jnp.cumsum(lengths) - lengths
    found = jnp.sum((starts[:, None] <= frame_index[None, :]).astype(jnp.int32), axis=0) - 1
    return jnp.where(frame_index < 0, -1, jnp.where(frame_index >= total_frames, -2, found))


def dot_last(left, right):
    return lax.dot_general(left, right, (((1,), (1,)), ((), ())), preferred_element_type=F32)


def dot_first(left, right):
    return lax.dot_general(left, right, (((0,), (0,)), ((), ())), preferred_element_type=F32)


def expand(kernel, mask):
    width, blocks = kernel.shape[-1], mask.shape[-1]
    spread = (
        jnp.arange(width, dtype=jnp.int32)[None, :] // (width // blocks)
        == jnp.arange(blocks, dtype=jnp.int32)[:, None]
    ).astype(BF16)
    keep = jnp.dot(mask.reshape(-1, blocks).astype(BF16), spread, preferred_element_type=F32)
    return (kernel.reshape(-1, width) * keep.astype(BF16)).reshape(kernel.shape)


def per_device(
    latent_input,
    upsample_kernel,
    dilated_kernel,
    pointwise_kernel,
    dilated_prune_mask,
    pointwise_prune_mask,
    snake_freq_upsample,
    snake_freq_dilated,
    snake_freq_pointwise,
    segment_lengths,
    cotangent,
):
    taps, out_local, in_local = upsample_kernel.shape
    stride = taps // 2
    half = stride // 2
    frame_count = latent_input.shape[1]
    rows = frame_count * stride
    tm_count = lax.axis_size("tm")
    tm_index = lax.axis_index("tm")
    total_frames = frame_count * tm_count
    units, kernel_taps, _, channels = dilated_kernel.shape

    def tap_mask(pos, offset):
        own = track_ids(segment_lengths, jnp.floor_divide(pos, stride), total_frames)
        other = track_ids(segment_lengths, jnp.floor_divide(pos + offset, stride), total_frames)
        return (own == other)[:, None]

    row_pos = tm_index * rows + jnp.arange(rows, dtype=jnp.int32)
    all_pos = jnp.arange(rows * tm_count, dtype=jnp.int32)
    frame_pos = jnp.arange(total_frames, dtype=jnp.int32)

    dil_eff = expand(dilated_kernel, dilated_prune_mask)
    point_eff = expand(pointwise_kernel, pointwise_prune_mask)

    act = snake_act(latent_input.astype(F32), snake_freq_upsample[:, None]).astype(BF16).T
    cot = cotangent.T
    grad_second_last = lax.psum_scatter(
        jnp.dot(cot, point_eff[units - 1], preferred_element_type=F32).astype(BF16),
        "chan",
        scatter_dimension=1,
        tiled=True,
    ).astype(F32)

    act_all = turn(act, 0)
    product = dot_last(act_all, upsample_kernel.reshape(taps * out_local, in_local)).reshape(
        total_frames, taps, out_local
    )
    frame_ids = track_ids(segment_lengths, frame_pos, total_frames)
    prev_ok = (frame_ids == track_ids(segment_lengths, frame_pos - 1, total_frames))[:, None, None]
    next_ok = (frame_ids == track_ids(segment_lengths, frame_pos + 1, total_frames))[:, None, None]
    low = jnp.pad(product[:-1, half + stride :], ((1, 0), (0, 0), (0, 0)))
    high = jnp.pad(product[1:, :half], ((0, 1), (0, 0), (0, 0)))
    partial = product[:, half : half + stride] + jnp.concatenate(
        [jnp.where(prev_ok, low, 0.0), jnp.where(next_ok, high, 0.0)], axis=1
    )
    hidden = tm_scatter(partial.astype(BF16).reshape(rows * tm_count, out_local), 1)

    saved = []
    number = 2
    for unit in range(units):
        spacing = 3 ** (unit + 1)
        margin = (kernel_taps // 2) * spacing
        halo = -(-margin // 16) * 16
        first = snake_act(hidden, snake_freq_dilated[unit]).astype(BF16)
        first_all = chan_gather(first, halo, number)
        number += 1
        spans = dot_last(first_all, dil_eff[unit].reshape(kernel_taps * out_local, channels))
        conv = jnp.zeros((rows, out_local), F32)
        for tap in range(kernel_taps):
            shift = (tap - kernel_taps // 2) * spacing
            piece = spans[halo + shift : halo + shift + rows, tap * out_local : (tap + 1) * out_local]
            conv = conv + jnp.where(tap_mask(row_pos, shift), piece, 0.0)
        second = snake_act(conv, snake_freq_pointwise[unit]).astype(BF16)
        if unit < units - 1:
            second_all = chan_gather(second, 0, number)
            number += 1
        else:
            second_all = lax.all_gather(second, "chan", axis=1, tiled=True)
        saved.append((hidden, first_all[halo : halo + rows], conv, second_all))
        hidden = hidden + dot_last(second_all, point_eff[unit])
    decoded = hidden.astype(BF16).T

    first_frames = lax.all_gather(saved[0][1], "tm", axis=0, tiled=True)

    def shifted_taps(grad_wide, pos, halo, spacing):
        count = pos.shape[0]
        pieces = []
        for tap in range(kernel_taps):
            shift = (tap - kernel_taps // 2) * spacing
            window = grad_wide[halo - shift : halo - shift + count]
            pieces.append(jnp.where(tap_mask(pos, -shift), window, jnp.zeros((), BF16)))
        return jnp.concatenate(pieces, axis=1)

    grad_out = cot.astype(F32)
    dil_out = [None] * units
    point_out = [None] * units
    for unit in reversed(range(units)):
        spacing = 3 ** (unit + 1)
        margin = (kernel_taps // 2) * spacing
        hidden_in, first_own, conv, second_all = saved[unit]
        grad_b = grad_out.astype(BF16)
        point_grad = dot_first(grad_b, second_all)
        if unit == units - 1:
            grad_second = grad_second_last
        else:
            grad_second = chan_scatter(
                jnp.dot(grad_b, point_eff[unit], preferred_element_type=F32).astype(BF16), number
            )
            number += 1
        grad_conv = (grad_second * snake_slope(conv, snake_freq_pointwise[unit])).astype(BF16)
        weights = dil_eff[unit].reshape(kernel_taps * out_local, channels)
        if unit > 0:
            shifted = shifted_taps(with_halo(grad_conv, margin), row_pos, margin, spacing)
            grad_first = chan_scatter(
                jnp.dot(shifted, weights, preferred_element_type=F32).astype(BF16), number
            )
            number += 1
            dil_part, point_part = lax.psum(
                (dot_first(shifted, first_own).astype(BF16), point_grad.astype(BF16)), "tm"
            )
            dil_grad = dil_part.astype(F32)
            grad_out = grad_out + grad_first * snake_slope(hidden_in, snake_freq_dilated[unit])
        else:
            grad_frames = jnp.pad(tm_gather(grad_conv, number), ((margin, margin), (0, 0)))
            number += 1
            dil_grad = dot_first(shifted_taps(grad_frames, all_pos, margin, spacing), first_frames)
            point_part = lax.psum(point_grad.astype(BF16), "tm")
        dil_out[unit] = (weights.astype(F32) * dil_grad).reshape(kernel_taps, out_local, channels)
        point_out[unit] = point_eff[unit].astype(F32) * point_part.astype(F32)
    return decoded, jnp.stack(dil_out), jnp.stack(point_out)


def solution(mesh):
    return jax.shard_map(
        per_device,
        mesh=mesh,
        in_specs=(
            P("chan", "tm"),
            P(None, "chan", "tm"),
            P(None, None, "chan", None),
            P(None, "chan", None),
            P(None, None, "chan", None),
            P(None, "chan", None),
            P("chan"),
            P(None, "chan"),
            P(None, "chan"),
            P(),
            P("chan", "tm"),
        ),
        out_specs=(P("chan", "tm"), P(None, None, "chan", None), P(None, "chan", None)),
        check_vma=False,
    )
```

time: 485 us -> 352 us (0.73); the launches traced: 478 us -> 351 us
  waiting for transfers between devices: 295 us -> 88.3 us
  Pallas kernels: 0 us -> 144 us
  starting transfers between devices: 22.5 us -> 2.47 us
  matrix products: 52.6 us -> 34.3 us
  blocking collectives: 14.7 us -> 0 us
  local copies, waits for them, and re-layouts: 41.7 us -> 31.1 us
    pallas_call x0 -> x8, Pallas kernels: none -> 144 us  [run(): pl.pallas_call(kernel, out_shape=jax.ShapeDtypeStruct(out_shape, dtype),...]
    all_gather x5 -> x2, waiting for transfers between devices: 122 us -> 52.5 us  [the longest x1 52.5 us: per_device(): first_frames = lax.all_gather(saved[0][1], 'tm', axis=0, tiled=True)]
    reduce_scatter x3 -> x0, waiting for transfers between devices: 59.8 us -> none  [the longest x2 40.9 us: per_device(): lax.psum_scatter(lax.dot_general(pointwise_effective, grad_b, (((0,), (0,...]
    psum x1, waiting for transfers between devices: 87.6 us -> 32.3 us  [per_device(): lax.psum((dot_first(shifted, first_own).astype(BF16), point_grad.astype(B...]
    ppermute x8 -> x2, waiting for transfers between devices: 23.9 us -> 3.37 us  [the longest x1 3.36 us: with_halo(): lax.ppermute(tail, 'tm', [(i, (i + 1) % count) for i in range(count)])]
    ppermute x8 -> x2, starting transfers between devices: 21.8 us -> 2.31 us  [the longest x1 1.67 us: with_halo(): lax.ppermute(head, 'tm', [((i + 1) % count, i) for i in range(count)])]
    dot_general x26 -> x14, matrix products: 52.6 us -> 34.3 us  [the longest x4 17.4 us: dot_first(): lax.dot_general(left, right, (((0,), (0,)), ((), ())), preferred_element_...]
    convert_element_type x16 -> x1, local copies, waits for them, and re-layouts: 18.4 us -> 0.43 us  [per_device(): partial.astype(BF16).reshape(rows * tm_count, out_local)]
  transfers between devices with their start and end apart: 17 -> 6, of which waited for: 13 -> 3; matrix products, arithmetic and copies ran while one was open for 17% -> 17% of each run, Pallas kernels for 0% -> 41%
where the time goes in v1:
time: 352 us; the launch traced here: 351 us
  Pallas kernels  144 us (41%)
  waiting for transfers between devices  88.3 us (25%)
  other arithmetic  37.3 us (11%)
  matrix products  34.3 us (10%)
  local copies, waits for them, and re-layouts  31.1 us (9%)
  between operations  14.4 us (4%)
    pallas_call x8, Pallas kernels, run(): pl.pallas_call(kernel, out_shape=jax.ShapeDtypeStruct(out_shape, dtype),...  144 us
    all_gather x1, waiting for transfers between devices, per_device(): first_frames = lax.all_gather(saved[0][1], 'tm', axis=0, tiled=True)  52.5 us
    psum x1, waiting for transfers between devices, per_device(): lax.psum((dot_first(shifted, first_own).astype(BF16), point_grad.astype(B...  32.3 us
    dot_general x4, matrix products, dot_first(): lax.dot_general(left, right, (((0,), (0,)), ((), ())), preferred_element_...  17.4 us
    unnamed x58, local copies, waits for them, and re-layouts  11.9 us
    mul x2, local copies, waits for them, and re-layouts, per_device(): weights.astype(F32) * dil_grad  10.1 us
    unnamed x10, other arithmetic  8.91 us
    dot_general x5, matrix products, dot_last(): lax.dot_general(left, right, (((1,), (1,)), ((), ())), preferred_element_...  8.23 us
  transfers between devices with their start and end apart: 6, of which 3 were waited for; matrix products, arithmetic and copies ran while one was open for 17% of the time, Pallas kernels for 41%

profile of v1, /device:TPU:0, one launch (start us, length us, event | category | flops | bytes accessed | tf_op | source)
XLA Modules:
  0.0 351.5 jit_solution(8084963231729797825)
XLA Ops:
  7.2 1.4 copy.65
  8.7 0.9 convert_element_type.240
  10.7 1.6 convolution_convert_fusion.4
  13.6 13.2 %shard_map.130 = bf16[320,512]{1,0:T(8,128)(2,1)S(1)} custom-call(bf16[80,256]{1,0:T(8,128)(2,1)S(1)} %fusion.54.x_ref), custom_call_target="tpu_custom_call" | custom-call | tf_op jit(solution)/shard_map/pallas_call | solution.py:260
  27.7 1.5 copy-done.4
  30.3 1.5 copy-done.5
  32.4 12.1 %shard_map.131 = f32[640,128]{1,0:T(8,128)S(1)} custom-call(bf16[2560,128]{1,0:T(8,128)(2,1)S(1)} %bitcast.70), custom_call_target="tpu_custom_call" | custom-call | tf_op jit(solution)/shard_map/pallas_call | solution.py:260
  44.6 1.1 add_convert_fusion.3.x_ref
  45.7 23.2 %shard_map.132 = bf16[672,1024]{1,0:T(8,128)(2,1)S(1)} custom-call(bf16[640,128]{1,0:T(8,128)(2,1)S(1)} %add_convert_fusion.3.x_ref), custom_call_target="tpu_custom_call" | custom-call | tf_op jit(solution)/shard_map/pallas_call | solution.py:260
  68.9 6.0 %copy.51 = bf16[1792,1024]{0,1:T(8,128)(2,1)} copy(bf16[1792,1024]{1,0:T(8,128)(2,1)} %bitcast.73) | data formatting | bytes 7340032 | tf_op jit(solution)/shard_map/reshape | solution.py:396
  75.2 3.2 bitcast_multiply_fusion
  78.5 1.6 fusion
  80.0 2.8 add_convert_fusion.2
  82.9 16.7 %shard_map.133 = bf16[640,1024]{1,0:T(8,128)(2,1)S(1)} custom-call(bf16[640,128]{1,0:T(8,128)(2,1)S(1)} %get-tuple-element.41.x_ref), custom_call_target="tpu_custom_call" | custom-call | tf_op jit(solution)/shard_map/pallas_call | solution.py:260
  99.6 2.1 add_convert_fusion.1
  101.8 23.8 %shard_map.134 = bf16[704,1024]{1,0:T(8,128)(2,1)S(1)} custom-call(bf16[640,128]{1,0:T(8,128)(2,1)S(1)} %get-tuple-element.74.x_ref), custom_call_target="tpu_custom_call" | custom-call | tf_op jit(solution)/shard_map/pallas_call | solution.py:260
  125.6 1.1 copy-done.2
  126.8 3.1 fusion.3
  129.9 1.1 copy.67
  130.9 4.0 %multiply_convert_fusion.1 = (bf16[640,128]{1,0:T(8,128)(2,1)S(1)}, f32[640,128]{1,0:T(8,128)S(1)}) fusion(bf16[640,128]{1,0:T(8,128)(2,1)S(1)} %copy.67, f32[128]{0:T(128)S(1)} %get-tuple-element.68, f32[704,896]{1,0:T(8,128)} %fusion.3, pred[640]{0:T(1024)(128)(4,1)S(1)} %get-tuple-element.64, pred[640]{0:T(1024)(128)(4,1)S(1)} %get-tuple-element.56, ...), kind=kLoop, calls=%fused_computation.70 | loop fusion | flops 1392640 | bytes 2953472 | tf_op jit(solution)/shard_map/convert_element_type | solution.py:509
  134.9 1.7 collective-permute-start
  136.6 1.8 add_convert_fusion
  139.7 3.4 collective-permute-done.1
  143.7 3.1 convolution_convert_fusion.3.x_ref
  146.8 21.9 %shard_map.135 = f32[640,128]{1,0:T(8,128)S(1)} custom-call(bf16[640,1024]{1,0:T(8,128)(2,1)S(1)} %convolution_convert_fusion.3.x_ref), custom_call_target="tpu_custom_call" | custom-call | tf_op jit(solution)/shard_map/pallas_call | solution.py:260
  168.7 1.1 fusion.25
  169.8 1.3 convolution_convert_fusion.7
  171.1 3.0 convolution_convert_fusion.1
  174.1 2.6 fusion.9
  176.8 1.2 slice.182
  178.9 20.0 %shard_map.136 = f32[640,128]{1,0:T(8,128)S(1)} custom-call(bf16[640,1024]{1,0:T(8,128)(2,1)S(1)} %convolution_convert_fusion.2.x_ref), custom_call_target="tpu_custom_call" | custom-call | tf_op jit(solution)/shard_map/pallas_call | solution.py:260
  198.9 1.1 multiply_convert_fusion.x_ref
  200.0 12.7 %shard_map.137 = bf16[2560,128]{1,0:T(8,128)(2,1)S(1)} custom-call(bf16[640,128]{1,0:T(8,128)(2,1)S(1)} %multiply_convert_fusion.x_ref), custom_call_target="tpu_custom_call" | custom-call | tf_op jit(solution)/shard_map/pallas_call | solution.py:260
  212.7 1.6 select_dynamic-update-slice_fusion.5
  214.3 1.6 select_dynamic-update-slice_fusion.4
  215.9 1.6 select_dynamic-update-slice_fusion.3
  217.7 1.6 select_dynamic-update-slice_fusion.2
  219.3 1.6 select_dynamic-update-slice_fusion.1
  220.9 1.6 select_dynamic-update-slice_fusion
  222.6 2.1 copy-done.20
  226.0 32.3 %all-reduce.6.cloned.1.call-done = (bf16[896,1024]{0,1:T(8,128)(2,1)}, bf16[128,1024]{0,1:T(8,128)(2,1)}, bf16[128,1024]{0,1:T(8,128)(2,1)}) async-done(((bf16[896,1024]{0,1:T(8,128)(2,1)}, bf16[128,1024]{0,1:T(8,128)(2,1)}, bf16[128,1024]{0,1:T(8,128)(2,1)}), (bf16[896,1024]{0,1:T(8,128)(2,1)}, bf16[128,1024]{0,1:T(8,128)(2,1)}, bf16[128,1024]{0,1:T(8,128)(2,1)})) %all-reduce.6.cloned.1.call-update) | async-done | bytes 2359312 | tf_op jit(solution)/shard_map/psum | solution.py:517
  258.4 4.2 %convert_multiply_fusion = f32[896,1024]{0,1:T(8,128)} fusion(bf16[896,1024]{0,1:T(8,128)(2,1)} %get-tuple-element.36, bf16[1792,1024]{0,1:T(8,128)(2,1)} %copy-done.6), kind=kLoop, calls=%fused_computation.3 | loop fusion | flops 2752512 | bytes 7340032 | tf_op jit(solution)/shard_map/mul | solution.py:527
  262.6 5.1 %copy.58 = f32[896,1024]{1,0:T(8,128)} copy(f32[896,1024]{0,1:T(8,128)} %convert_multiply_fusion) | data formatting | bytes 7340032 | tf_op jit(solution)/shard_map/mul | solution.py:527
  267.9 1.3 copy.61
  269.2 52.5 %all-gather.5.cloned.1.call-done = bf16[2560,1024]{1,0:T(8,128)(2,1)} async-done(((bf16[640,1024]{1,0:T(8,128)(2,1)}), bf16[2560,1024]{1,0:T(8,128)(2,1)}) %all-gather.5.cloned.1.call-update) | async-done | bytes 5242896 | tf_op jit(solution)/shard_map/all_gather | solution.py:482
  321.7 10.5 %convert_multiply_fusion.1 = f32[896,1024]{0,1:T(8,128)} fusion(bf16[2560,896]{1,0:T(8,128)(2,1)} %copy-done.20, bf16[2560,1024]{1,0:T(8,128)(2,1)} %all-gather.5.cloned.1.call-done, bf16[1792,1024]{0,1:T(8,128)(2,1)} %copy-done.6), kind=kOutput, calls=%fused_computation.4 | convolution fusion | flops 4699455488 | bytes 15335424 | tf_op jit(solution)/shard_map/dot_general | solution.py:386
  332.1 5.0 %copy.56 = f32[896,1024]{1,0:T(8,128)} copy(f32[896,1024]{0,1:T(8,128)} %convert_multiply_fusion.1) | data formatting | bytes 7340032 | tf_op jit(solution)/shard_map/mul | solution.py:527
  337.2 7.7 %pad_maximum_fusion = f32[2,7,128,1024]{3,2,1,0:T(8,128)} fusion(f32[1,7,128,1024]{3,2,1,0:T(8,128)} %bitcast.71, f32[1,7,128,1024]{3,2,1,0:T(8,128)} %bitcast.72), kind=kLoop, calls=%fused_computation | loop fusion | flops 1835008 | bytes 14680064 | tf_op jit(solution)/shard_map/stack | solution.py:529
  (106 shorter events, 9.8 us)
Async XLA Ops:
  7.2 19.7 %copy-start = (bf16[16,128,512]{2,1,0:T(8,128)(2,1)S(1)}, bf16[16,128,512]{2,1,0:T(8,128)(2,1)}, u32[]{:S(2)}) copy-start(bf16[16,128,512]{2,1,0:T(8,128)(2,1)} %param.12) | copy-start | bytes 6291460
  7.2 3.6 %copy-start.11 = (bf16[128,640]{1,0:T(8,128)(2,1)S(1)}, bf16[128,640]{1,0:T(8,128)(2,1)}, u32[]{:S(2)}) copy-start(bf16[128,640]{1,0:T(8,128)(2,1)} %param.21) | copy-start | bytes 491524
  7.2 122.7 %reduce-scatter.4.cloned.1.call-start = ((), (), s32[]{:S(2)}) async-start(), calls=%async_computation.3 | async-start | bytes 1474560
  9.6 3.7 %copy-start.23 = (f32[2,128]{1,0:T(2,128)S(1)}, f32[2,128]{1,0:T(2,128)}, u32[]{:S(2)}) copy-start(f32[2,128]{1,0:T(2,128)} %param.18) | copy-start | bytes 3076
  9.6 3.7 %copy-start.21 = (bf16[256,80]{0,1:T(8,128)(2,1)S(1)}, bf16[256,80]{0,1:T(8,128)(2,1)}, u32[]{:S(2)}) copy-start(bf16[256,80]{0,1:T(8,128)(2,1)} %param.11) | copy-start | bytes 122884
  9.6 3.7 %copy-start.24 = (f32[256]{0:T(256)S(1)}, f32[256]{0:T(256)}, u32[]{:S(2)}) copy-start(f32[256]{0:T(256)} %param.17) | copy-start | bytes 3076
  9.9 0.8 copy-start.7
  12.3 161.8 %all-gather.3.cloned.1.call-start = ((), (), s32[]{:S(2)}) async-start(), calls=%async_computation.1 | async-start | bytes 1474560 | tf_op jit(solution)/shard_map/all_gather | solution.py:477
  27.7 1.5 copy-start.4
  29.2 0.7 copy-start.25
  30.0 1.8 copy-start.5
  68.8 6.0 %copy-start.16 = (s32[2,7,128,128]{3,2,1,0:T(8,128)S(1)}, s32[2,7,128,128]{3,2,1,0:T(8,128)}, u32[]{:S(2)}) copy-start(s32[2,7,128,128]{3,2,1,0:T(8,128)} %param.15) | copy-start | bytes 2752516
  68.9 6.3 %copy-start.22 = (f32[2,128]{1,0:T(2,128)S(1)}, f32[2,128]{1,0:T(2,128)}, u32[]{:S(2)}) copy-start(f32[2,128]{1,0:T(2,128)} %param.19) | copy-start | bytes 3076
  78.4 47.2 %copy-start.6 = (bf16[1792,1024]{0,1:T(8,128)(2,1)}, bf16[1792,1024]{0,1:T(8,128)(2,1)S(1)}, u32[]{:S(2)}) copy-start(bf16[1792,1024]{0,1:T(8,128)(2,1)S(1)} %bitcast_multiply_fusion) | copy-start | bytes 11010052
  80.0 19.6 %copy-start.8 = (bf16[256,1024]{0,1:T(8,128)(2,1)S(1)}, bf16[256,1024]{0,1:T(8,128)(2,1)}, u32[]{:S(2)}) copy-start(bf16[256,1024]{0,1:T(8,128)(2,1)} %copy-done.7) | copy-start | bytes 1572868
  125.6 1.1 copy-start.2
  134.9 4.2 %collective-permute-start = (bf16[27,128]{1,0:T(8,128)(2,1)S(1)}, bf16[27,128]{1,0:T(8,128)(2,1)S(1)}, u32[]{:S(2)}, u32[]{:S(2)}) collective-permute-start(bf16[27,128]{1,0:T(8,128)(2,1)S(1)} %get-tuple-element.48), channel_id=1, source_target_pairs={{8,0},{16,8},{24,16},{0,24},{9,1},{17,9},{25,17},{1,25},{10,2},{18... | collective-permute-start | bytes 20744 | tf_op jit(solution)/shard_map/ppermute | solution.py:283
  138.4 119.9 %all-reduce.6.cloned.1.call-start = ((), (), s32[]{:S(2)}) async-start(), calls=%async_computation.4 | async-start | bytes 4718592 | tf_op jit(solution)/shard_map/psum | solution.py:517
  138.5 4.6 %collective-permute-start.1 = (bf16[27,128]{1,0:T(8,128)(2,1)S(1)}, bf16[27,128]{1,0:T(8,128)(2,1)S(1)}, u32[]{:S(2)}, u32[]{:S(2)}) collective-permute-start(bf16[27,128]{1,0:T(8,128)(2,1)S(1)} %get-tuple-element.47), channel_id=1, source_target_pairs={{0,8},{8,16},{16,24},{24,0},{1,9},{9,17},{17,25},{25,1},{2,10},{10... | collective-permute-start | bytes 20744 | tf_op jit(solution)/shard_map/ppermute | solution.py:281
  143.6 25.1 %copy-start.13 = (f32[640,128]{1,0:T(8,128)S(1)}, f32[640,128]{1,0:T(8,128)}, u32[]{:S(2)}) copy-start(f32[640,128]{1,0:T(8,128)} %get-tuple-element.75) | copy-start | bytes 983044
  143.7 25.1 %copy-start.17 = (bf16[128,640]{0,1:T(8,128)(2,1)S(1)}, bf16[128,640]{0,1:T(8,128)(2,1)}, u32[]{:S(2)}) copy-start(bf16[128,640]{0,1:T(8,128)(2,1)} %copy.53) | copy-start | bytes 491524
  146.8 24.3 %copy-start.3 = (bf16[704,1024]{1,0:T(8,128)(2,1)S(1)}, bf16[704,1024]{1,0:T(8,128)(2,1)}, u32[]{:S(2)}) copy-start(bf16[704,1024]{1,0:T(8,128)(2,1)} %copy-done.2) | copy-start | bytes 4325380
  171.1 3.0 copy-start.12
  176.8 1.6 copy-start.9
  176.8 144.9 %all-gather.5.cloned.1.call-start = ((), (), s32[]{:S(2)}) async-start(), calls=%async_computation.2 | async-start | bytes 6553600 | tf_op jit(solution)/shard_map/all_gather | solution.py:482
  178.0 20.9 %copy-start.15 = (f32[640,128]{1,0:T(8,128)S(1)}, f32[640,128]{1,0:T(8,128)}, u32[]{:S(2)}) copy-start(f32[640,128]{1,0:T(8,128)} %get-tuple-element.42) | copy-start | bytes 983044
  217.7 7.0 %copy-start.10 = (bf16[640,1024]{1,0:T(8,128)(2,1)S(1)}, bf16[640,1024]{1,0:T(8,128)(2,1)}, u32[]{:S(2)}) copy-start(bf16[640,1024]{1,0:T(8,128)(2,1)} %all-gather.3.cloned.1.call-done) | copy-start | bytes 3932164
  217.7 7.0 %copy-start.14 = (f32[640,128]{1,0:T(8,128)S(1)}, f32[640,128]{1,0:T(8,128)}, u32[]{:S(2)}) copy-start(f32[640,128]{1,0:T(8,128)} %get-tuple-element.75) | copy-start | bytes 983044
  222.6 2.1 copy-start.20
  262.6 5.1 %copy-start.18 = (bf16[128,1024]{0,1:T(8,128)(2,1)S(1)}, bf16[128,1024]{0,1:T(8,128)(2,1)}, u32[]{:S(2)}) copy-start(bf16[128,1024]{0,1:T(8,128)(2,1)} %get-tuple-element.37) | copy-start | bytes 786436
  262.6 5.1 %copy-start.19 = (bf16[128,1024]{0,1:T(8,128)(2,1)S(1)}, bf16[128,1024]{0,1:T(8,128)(2,1)}, u32[]{:S(2)}) copy-start(bf16[128,1024]{0,1:T(8,128)(2,1)} %get-tuple-element.38) | copy-start | bytes 786436
  337.2 7.7 %copy-start.1 = (bf16[16,128,512]{2,1,0:T(8,128)(2,1)S(1)}, bf16[16,128,512]{2,1,0:T(8,128)(2,1)}, u32[]{:S(2)}) copy-start(bf16[16,128,512]{2,1,0:T(8,128)(2,1)} %param.12) | copy-start | bytes 6291460
Sparse Core Ops, SparseCore 0:
  12.5 37.6 reduce-scatter.3
  138.5 33.6 all-gather.2
  176.9 81.4 all-reduce.5
  260.2 61.4 all-gather.4

commit v2 on v1

--- a/solution.py
+++ b/solution.py
@@ -42,77 +42,77 @@
     return pl.ds(pl.multiple_of(index * width, width), width)
 
 
-def chan_gather_kernel(halo, x_ref, o_ref, send, recv, fsend, frecv, hsend, hrecv):
-    tm, chan, core, chips, partner, at = chan_place()
-    frames = lax.axis_size("tm")
-    rows, width = x_ref.shape
-    greeted = [partner] + [(tm, at(step)) for step in range(1, chips)]
-    after = ((tm + 1) % frames, chan)
-    before = ((tm + frames - 1) % frames, chan)
-    if halo:
-        greeted += [before, after]
-    greet(greeted)
-    spans = [pl.ds(halo, rows)]
-    sources = [x_ref]
-    mine = column(chan, width)
-    if halo:
-        spans += [pl.ds(0, halo), pl.ds(halo + rows, halo)]
-        sources += [o_ref.at[spans[1], mine], o_ref.at[spans[2], mine]]
-        edges = [
-            remote(x_ref.at[pl.ds(rows - halo, halo)], o_ref.at[spans[1], mine], hsend.at[0], hrecv.at[0], after),
-            remote(x_ref.at[pl.ds(0, halo)], o_ref.at[spans[2], mine], hsend.at[1], hrecv.at[1], before),
-        ]
-        for edge in edges:
-            edge.start()
-    started = []
-
-    def spread(part):
-        for step in range(1, chips):
-            copy = remote(
-                sources[part], o_ref.at[spans[part], mine], send.at[part, step], recv.at[part, step], (tm, at(step))
-            )
+def chan_gather_task(halo):
+    def body(x_ref, o_ref, send, recv, fsend, frecv, hsend, hrecv):
+        tm, chan, core, chips, partner, at = chan_place()
+        frames = lax.axis_size("tm")
+        rows, width = x_ref.shape
+        after = ((tm + 1) % frames, chan)
+        before = ((tm + frames - 1) % frames, chan)
+        spans = [pl.ds(halo, rows)]
+        sources = [x_ref]
+        mine = column(chan, width)
+        if halo:
+            spans += [pl.ds(0, halo), pl.ds(halo + rows, halo)]
+            sources += [o_ref.at[spans[1], mine], o_ref.at[spans[2], mine]]
+            edges = [
+                remote(x_ref.at[pl.ds(rows - halo, halo)], o_ref.at[spans[1], mine], hsend.at[0], hrecv.at[0], after),
+                remote(x_ref.at[pl.ds(0, halo)], o_ref.at[spans[2], mine], hsend.at[1], hrecv.at[1], before),
+            ]
+            for edge in edges:
+                edge.start()
+        started = []
+
+        def spread(part):
+            for step in range(1, chips):
+                copy = remote(
+                    sources[part], o_ref.at[spans[part], mine], send.at[part, step], recv.at[part, step], (tm, at(step))
+                )
+                copy.start()
+                started.append(copy)
+            copy = remote(sources[part], o_ref.at[spans[part], mine], send.at[part, 0], recv.at[part, 0], partner)
             copy.start()
             started.append(copy)
-        copy = remote(sources[part], o_ref.at[spans[part], mine], send.at[part, 0], recv.at[part, 0], partner)
-        copy.start()
-        started.append(copy)
-
-    spread(0)
-    if halo:
-        for edge in edges:
-            edge.wait_recv()
-        spread(1)
-        spread(2)
-    o_ref[spans[0], mine] = x_ref[...]
-
-    def arrival(part, index, sems, step):
-        slot = o_ref.at[spans[part], column(index, width)]
-        return remote(slot, slot, send.at[part, step], sems.at[part, step], partner)
-
-    for step in range(1, chips):
+
+        spread(0)
+        yield
+        if halo:
+            for edge in edges:
+                edge.wait_recv()
+            spread(1)
+            spread(2)
+        o_ref[spans[0], mine] = x_ref[...]
+
+        def arrival(part, index, sems, step):
+            slot = o_ref.at[spans[part], column(index, width)]
+            return remote(slot, slot, send.at[part, step], sems.at[part, step], partner)
+
+        for step in range(1, chips):
+            for part in range(len(spans)):
+                index = at(-step)
+                arrival(part, index, recv, step).wait_recv()
+                slot = o_ref.at[spans[part], column(index, width)]
+                copy = remote(slot, slot, fsend.at[part, step], frecv.at[part, step], partner)
+                copy.start()
+                started.append(copy)
+        yield
+        other = 1 - 2 * core
         for part in range(len(spans)):
-            index = at(-step)
-            arrival(part, index, recv, step).wait_recv()
-            slot = o_ref.at[spans[part], column(index, width)]
-            copy = remote(slot, slot, fsend.at[part, step], frecv.at[part, step], partner)
-            copy.start()
-            started.append(copy)
-    other = 1 - 2 * core
-    for part in range(len(spans)):
-        arrival(part, chan + other, recv, 0).wait_recv()
-        for step in range(1, chips):
-            arrival(part, at(-step) + other, frecv, step).wait_recv()
-    for copy in started:
-        copy.wait_send()
-    if halo:
-        for edge in edges:
-            edge.wait_send()
-
-
-def chan_scatter_kernel(x_ref, o_ref, pair, summed, landed, psend, precv, send, recv):
+            arrival(part, chan + other, recv, 0).wait_recv()
+            for step in range(1, chips):
+                arrival(part, at(-step) + other, frecv, step).wait_recv()
+        for copy in started:
+            copy.wait_send()
+        if halo:
+            for edge in edges:
+                edge.wait_send()
+
+    return body
+
+
+def chan_scatter_body(x_ref, o_ref, pair, summed, landed, psend, precv, send, recv):
     tm, chan, core, chips, partner, at = chan_place()
     width = o_ref.shape[1]
-    greet([partner] + [(tm, at(step)) for step in range(1, chips)])
     other = 1 - 2 * core
     order = list(range(1, chips)) + [0]
     started = []
@@ -123,6 +123,7 @@
         )
         copy.start()
         pairs[step] = copy
+    yield
     for step in range(1, chips):
         pairs[step].wait_recv()
         summed[step] = (
@@ -133,6 +134,7 @@
         started.append(copy)
     pairs[0].wait_recv()
     o_ref[...] = x_ref[:, column(chan, width)].astype(F32) + pair[0].astype(F32)
+    yield
     for copy, step in zip(started, range(1, chips)):
         copy.wait_recv()
         o_ref[...] += landed[step].astype(F32)
@@ -140,6 +142,213 @@
         copy.wait_send()
     for step in order:
         pairs[step].wait_send()
+
+
+def share_task(halo, base):
+    def body(x_ref, o_ref, send, recv, fsend, frecv):
+        tm, chan, core, chips, partner, at = chan_place()
+        count = lax.axis_size("tm")
+        rows, width = o_ref.shape[0] // count, o_ref.shape[1] // 2
+        own = pl.ds(halo, rows)
+
+        def slot(index, half):
+            return o_ref.at[pl.ds(pl.multiple_of(index * rows, rows), rows), column(half, width)]
+
+        started = []
+        source = x_ref.at[own, pl.ds(pl.multiple_of(base + core * width, width), width)]
+        for step in range(1, count):
+            copy = remote(source, slot(tm, core), send.at[step], recv.at[step], ((tm + step) % count, chan))
+            copy.start()
+            started.append(copy)
+        yield
+        o_ref[pl.ds(pl.multiple_of(tm * rows, rows), rows), :] = x_ref[own, pl.ds(base, 2 * width)]
+        for step in range(1, count):
+            landing = slot((tm + count - step) % count, core)
+            remote(landing, landing, send.at[step], recv.at[step], partner).wait_recv()
+            copy = remote(landing, landing, fsend.at[step], frecv.at[step], partner)
+            copy.start()
+            started.append(copy)
+        yield
+        for step in range(1, count):
+            landing = slot((tm + count - step) % count, 1 - core)
+            remote(landing, landing, send.at[step], frecv.at[step], partner).wait_recv()
+        for copy in started:
+            copy.wait_send()
+
+    return body
+
+
+def frames_gather_body(x_ref, o_ref, send, recv):
+    tm, chan = lax.axis_index("tm"), lax.axis_index("chan")
+    count = lax.axis_size("tm")
+    rows = x_ref.shape[0]
+
+    def slot(index):
+        return o_ref.at[pl.ds(pl.multiple_of(index * rows, rows), rows)]
+
+    started = []
+    for step in range(1, count):
+        copy = remote(x_ref, slot(tm), send.at[step], recv.at[step], ((tm + step) % count, chan))
+        copy.start()
+        started.append(copy)
+    yield
+    o_ref[pl.ds(pl.multiple_of(tm * rows, rows), rows)] = x_ref[...]
+    yield
+    for step in range(1, count):
+        landing = slot((tm + count - step) % count)
+        remote(landing, landing, send.at[step], recv.at[step], (tm, chan)).wait_recv()
+    for copy in started:
+        copy.wait_send()
+
+
+def reduce_body(x_ref, o_ref, landed, send, recv, gsend, grecv):
+    tm, chan = lax.axis_index("tm"), lax.axis_index("chan")
+    count = lax.axis_size("tm")
+    width = x_ref.shape[1] // count
+    started = []
+    for step in range(1, count):
+        to = (tm + step) % count
+        copy = remote(x_ref.at[:, column(to, width)], landed.at[step], send.at[step], recv.at[step], (to, chan))
+        copy.start()
+        started.append(copy)
+    yield
+    total = x_ref[:, column(tm, width)].astype(F32)
+    for step in range(1, count):
+        started[step - 1].wait_recv()
+        total += landed[step].astype(F32)
+    mine = o_ref.at[:, column(tm, width)]
+    o_ref[:, column(tm, width)] = total.astype(o_ref.dtype)
+    for step in range(1, count):
+        copy = remote(mine, mine, gsend.at[step], grecv.at[step], ((tm + step) % count, chan))
+        copy.start()
+        started.append(copy)
+    yield
+    for step in range(1, count):
+        landing = o_ref.at[:, column((tm + count - step) % count, width)]
+        remote(landing, landing, send.at[step], grecv.at[step], (tm, chan)).wait_recv()
+    for copy in started:
+        copy.wait_send()
+
+
+DMA = pltpu.SemaphoreType.DMA
+
+
+def chan_gather(value, halo):
+    rows, width = value.shape
+    chans = lax.axis_size("chan")
+    out = jax.ShapeDtypeStruct((rows + 2 * halo, width * chans), value.dtype)
+    return value, out, [DMA((3, chans // 2))] * 4 + [DMA((2,))] * 2, chan_gather_task(halo), False, halo > 0
+
+
+def chan_scatter(value):
+    rows, chans = value.shape[0], lax.axis_size("chan")
+    width, chips = value.shape[1] // chans, chans // 2
+    scratch = [pltpu.VMEM((chips, rows, width), value.dtype)] * 3 + [DMA((chips,))] * 4
+    return value, jax.ShapeDtypeStruct((rows, width), F32), scratch, chan_scatter_body, False, False
+
+
+def share(value, halo, part, parts):
+    count = lax.axis_size("tm")
+    rows, width = value.shape[0] - 2 * halo, value.shape[1] // parts
+    out = jax.ShapeDtypeStruct((rows * count, width), value.dtype)
+    return value, out, [DMA((count,))] * 4, share_task(halo, part * width), True, False
+
+
+def frames_gather(value):
+    count = lax.axis_size("tm")
+    out = jax.ShapeDtypeStruct((value.shape[0] * count, value.shape[1]), value.dtype)
+    return value, out, [DMA((count,))] * 2, frames_gather_body, True, False
+
+
+def frames_reduce(value):
+    count = lax.axis_size("tm")
+    landed = pltpu.VMEM((count, value.shape[0], value.shape[1] // count), value.dtype)
+    return value, jax.ShapeDtypeStruct(value.shape, value.dtype), [landed] + [DMA((count,))] * 4, reduce_body, True, False
+
+
+def together(number, *tasks):
+    along_chan = any(not task[4] for task in tasks) or any(len(task[2]) == 4 for task in tasks)
+    along_tm = any(task[4] for task in tasks)
+    edges = any(task[5] for task in tasks)
+
+    def kernel(*refs):
+        tm, chan, core, chips, partner, at = chan_place()
+        count = lax.axis_size("tm")
+        greeted = []
+        if along_chan:
+            greeted += [partner] + [(tm, at(step)) for step in range(1, chips)]
+        if along_tm:
+            greeted += [((tm + step) % count, chan) for step in range(1, count)]
+        elif edges:
+            greeted += [((tm + 1) % count, chan), ((tm + count - 1) % count, chan)]
+        greet(greeted)
+        size = len(tasks)
+        place = 2 * size
+        bodies = []
+        for index, task in enumerate(tasks):
+            scratch = refs[place : place + len(task[2])]
+            place += len(task[2])
+            bodies.append(task[3](refs[index], refs[size + index], *scratch))
+        for phase in range(3):
+            for body in bodies:
+                next(body, None)
+
+    whole = pl.BlockSpec(memory_space=pltpu.VMEM)
+    return pl.pallas_call(
+        kernel,
+        out_shape=[task[1] for task in tasks],
+        in_specs=[whole] * len(tasks),
+        out_specs=[whole] * len(tasks),
+        scratch_shapes=[item for task in tasks for item in task[2]],
+        compiler_params=pltpu.CompilerParams(
+            collective_id=number, has_side_effects=True, vmem_limit_bytes=VMEM_LIMIT
+        ),
+    )(*[task[0] for task in tasks])
+
+
+def saliency_kernel(spacings, pad, taps, ids_ref, eff_ref, *refs):
+    units = len(spacings)
+    grads, firsts = refs[:units], refs[units : 3 * units]
+    o_ref, turned = refs[3 * units], refs[3 * units + 1]
+    rows = turned.shape[1]
+    width = ids_ref.shape[1]
+    chunk = 512
+    for unit in range(units):
+        for tap in range(taps):
+            shift = (tap - taps // 2) * spacings[unit]
+
+            @pl.loop(0, rows // chunk)
+            def _(block):
+                start = pl.multiple_of(block * chunk, chunk)
+                window = grads[unit][pl.ds(start + pad - shift, chunk)]
+                same = ids_ref[pl.ds(start + pad - shift, chunk)] == ids_ref[pl.ds(start + pad, chunk)]
+                kept = jnp.where(same, window, 0.0)
+                turned[pl.ds(tap * width, width), pl.ds(start, chunk)] = kept.T.astype(turned.dtype)
+
+        for half in range(2):
+            source = firsts[2 * unit + half]
+            span = source.shape[1]
+            step = 256
+
+            @pl.loop(0, span // step)
+            def _(block):
+                inner = pl.ds(pl.multiple_of(block * step, step), step)
+                outer = pl.ds(pl.multiple_of(half * span + block * step, step), step)
+                grad = jnp.dot(turned[...], source[:, inner], preferred_element_type=F32)
+                o_ref[unit, :, outer] = eff_ref[unit, :, outer].astype(F32) * grad
+
+
+def saliency(spacings, pad, taps, ids, eff, grads, firsts):
+    whole = pl.BlockSpec(memory_space=pltpu.VMEM)
+    operands = [ids, eff] + grads + firsts
+    return pl.pallas_call(
+        functools.partial(saliency_kernel, spacings, pad, taps),
+        out_shape=jax.ShapeDtypeStruct(eff.shape, F32),
+        in_specs=[whole] * len(operands),
+        out_specs=whole,
+        scratch_shapes=[pltpu.VMEM((eff.shape[1], firsts[0].shape[0]), BF16)],
+        compiler_params=pltpu.CompilerParams(vmem_limit_bytes=VMEM_LIMIT),
+    )(*operands)
 
 
 def tm_scatter_kernel(x_ref, o_ref, landed, send, recv):
@@ -167,28 +376,6 @@
         copy.wait_send()
 
 
-def tm_gather_kernel(x_ref, o_ref, send, recv):
-    tm, chan = lax.axis_index("tm"), lax.axis_index("chan")
-    count = lax.axis_size("tm")
-    rows = x_ref.shape[0]
-    greet([((tm + step) % count, chan) for step in range(1, count)])
-
-    def slot(index):
-        return o_ref.at[pl.ds(pl.multiple_of(index * rows, rows), rows)]
-
-    started = []
-    for step in range(1, count):
-        copy = remote(x_ref, slot(tm), send.at[step], recv.at[step], ((tm + step) % count, chan))
-        copy.start()
-        started.append(copy)
-    o_ref[pl.ds(pl.multiple_of(tm * rows, rows), rows)] = x_ref[...]
-    for step in range(1, count):
-        landing = slot((tm + count - step) % count)
-        remote(landing, landing, send.at[step], recv.at[step], (tm, chan)).wait_recv()
-    for copy in started:
-        copy.wait_send()
-
-
 def turn_kernel(x_ref, o_ref, send, recv):
     tm, chan = lax.axis_index("tm"), lax.axis_index("chan")
     frames, chans = lax.axis_size("tm"), lax.axis_size("chan")
@@ -283,41 +470,6 @@
             lax.ppermute(head, "tm", [((i + 1) % count, i) for i in range(count)]),
         ],
         axis=0,
-    )
-
-
-def chan_gather(value, halo, number):
-    rows, width = value.shape
-    chans = lax.axis_size("chan")
-    if not plain_kernels(width):
-        return lax.all_gather(with_halo(value, halo) if halo else value, "chan", axis=1, tiled=True)
-    chips = chans // 2
-    dma = pltpu.SemaphoreType.DMA
-    return run(
-        functools.partial(chan_gather_kernel, halo),
-        (rows + 2 * halo, width * chans),
-        value.dtype,
-        [dma((3, chips))] * 4 + [dma((2,))] * 2,
-        number,
-        value,
-    )
-
-
-def chan_scatter(value, number):
-    rows, total = value.shape
-    chans = lax.axis_size("chan")
-    width = total // chans
-    if not plain_kernels(width):
-        return lax.psum_scatter(value, "chan", scatter_dimension=1, tiled=True).astype(F32)
-    chips = chans // 2
-    dma = pltpu.SemaphoreType.DMA
-    return run(
-        chan_scatter_kernel,
-        (rows, width),
-        F32,
-        [pltpu.VMEM((chips, rows, width), value.dtype)] * 3 + [dma((chips,))] * 4,
-        number,
-        value,
     )
 
 
@@ -334,16 +486,6 @@
         [pltpu.VMEM((count, rows, width), value.dtype)] + [dma((count,))] * 2,
         number,
         value,
-    )
-
-
-def tm_gather(value, number):
-    count = lax.axis_size("tm")
-    rows, width = value.shape
-    if not plain_kernels(width):
-        return lax.all_gather(value, "tm", axis=0, tiled=True)
-    return run(
-        tm_gather_kernel, (rows * count, width), value.dtype, [pltpu.SemaphoreType.DMA((count,))] * 2, number, value
     )
 
 
@@ -425,7 +567,6 @@
         return (own == other)[:, None]
 
     row_pos = tm_index * rows + jnp.arange(rows, dtype=jnp.int32)
-    all_pos = jnp.arange(rows * tm_count, dtype=jnp.int32)
     frame_pos = jnp.arange(total_frames, dtype=jnp.int32)
 
     dil_eff = expand(dilated_kernel, dilated_prune_mask)
@@ -454,79 +595,117 @@
     )
     hidden = tm_scatter(partial.astype(BF16).reshape(rows * tm_count, out_local), 1)
 
-    saved = []
-    number = 2
-    for unit in range(units):
-        spacing = 3 ** (unit + 1)
-        margin = (kernel_taps // 2) * spacing
-        halo = -(-margin // 16) * 16
-        first = snake_act(hidden, snake_freq_dilated[unit]).astype(BF16)
-        first_all = chan_gather(first, halo, number)
-        number += 1
-        spans = dot_last(first_all, dil_eff[unit].reshape(kernel_taps * out_local, channels))
+    spacings = [3 ** (unit + 1) for unit in range(units)]
+    reach = [(kernel_taps // 2) * spacing for spacing in spacings]
+    flat = dil_eff.reshape(units, kernel_taps * out_local, channels)
+    fast = units == 2 and plain_kernels(out_local, channels // 4, channels // tm_count) and frame_count % 16 == 0 and rows * tm_count % 512 == 0
+
+    def conv_of(first_all, unit, halo):
+        spans = dot_last(first_all, flat[unit])
         conv = jnp.zeros((rows, out_local), F32)
         for tap in range(kernel_taps):
-            shift = (tap - kernel_taps // 2) * spacing
+            shift = (tap - kernel_taps // 2) * spacings[unit]
             piece = spans[halo + shift : halo + shift + rows, tap * out_local : (tap + 1) * out_local]
             conv = conv + jnp.where(tap_mask(row_pos, shift), piece, 0.0)
-        second = snake_act(conv, snake_freq_pointwise[unit]).astype(BF16)
-        if unit < units - 1:
-            second_all = chan_gather(second, 0, number)
-            number += 1
-        else:
-            second_all = lax.all_gather(second, "chan", axis=1, tiled=True)
-        saved.append((hidden, first_all[halo : halo + rows], conv, second_all))
-        hidden = hidden + dot_last(second_all, point_eff[unit])
-    decoded = hidden.astype(BF16).T
-
-    first_frames = lax.all_gather(saved[0][1], "tm", axis=0, tiled=True)
-
-    def shifted_taps(grad_wide, pos, halo, spacing):
-        count = pos.shape[0]
+        return conv
+
+    def first_of(hidden, unit):
+        return snake_act(hidden, snake_freq_dilated[unit]).astype(BF16)
+
+    def second_of(conv, unit):
+        return snake_act(conv, snake_freq_pointwise[unit]).astype(BF16)
+
+    def grad_conv_of(grad_second, conv, unit):
+        return (grad_second * snake_slope(conv, snake_freq_pointwise[unit])).astype(BF16)
+
+    def spread_back(grad_b, unit):
+        return jnp.dot(grad_b, point_eff[unit], preferred_element_type=F32).astype(BF16)
+
+    def shifted_taps(grad_wide, unit, halo):
         pieces = []
         for tap in range(kernel_taps):
-            shift = (tap - kernel_taps // 2) * spacing
-            window = grad_wide[halo - shift : halo - shift + count]
-            pieces.append(jnp.where(tap_mask(pos, -shift), window, jnp.zeros((), BF16)))
+            shift = (tap - kernel_taps // 2) * spacings[unit]
+            window = grad_wide[halo - shift : halo - shift + rows]
+            pieces.append(jnp.where(tap_mask(row_pos, -shift), window, jnp.zeros((), BF16)))
         return jnp.concatenate(pieces, axis=1)
 
+    def outputs(decoded, dil, point_sums):
+        return (
+            decoded.astype(BF16).T,
+            dil.reshape(units, kernel_taps, out_local, channels),
+            point_eff.astype(F32) * point_sums.astype(F32),
+        )
+
+    if fast:
+        halos = [-(-margin // 16) * 16 for margin in reach]
+        (wide0,) = together(2, chan_gather(first_of(hidden, 0), halos[0]))
+        conv0 = conv_of(wide0, 0, halos[0])
+        second0, frames00 = together(3, chan_gather(second_of(conv0, 0), 0), share(wide0, halos[0], 0, 2))
+        hidden1 = hidden + dot_last(second0, point_eff[0])
+        wide1, frames01 = together(
+            4, chan_gather(first_of(hidden1, 1), halos[1]), share(wide0, halos[0], 1, 2)
+        )
+        conv1 = conv_of(wide1, 1, halos[1])
+        grad_conv1 = grad_conv_of(grad_second_last, conv1, 1)
+        grads1, second1 = together(5, frames_gather(grad_conv1), chan_gather(second_of(conv1, 1), 0))
+        decoded = hidden1 + dot_last(second1, point_eff[1])
+        pad = halos[1]
+        grads1 = jnp.pad(grads1, ((pad, pad), (0, 0)))
+        window = lax.dynamic_slice_in_dim(grads1, tm_index * rows, rows + 2 * pad, axis=0)
+        partial1 = jnp.dot(
+            shifted_taps(window, 1, pad), flat[1], preferred_element_type=F32
+        ).astype(BF16)
+        grad_first, frames10 = together(6, chan_scatter(partial1), share(wide1, halos[1], 0, 2))
+        grad_b0 = (cot.astype(F32) + grad_first * snake_slope(hidden1, snake_freq_dilated[1])).astype(BF16)
+        point_parts = jnp.concatenate([dot_first(grad_b0, second0), dot_first(cot, second1)]).astype(BF16)
+        grad_second0, frames11, point_sums = together(
+            7, chan_scatter(spread_back(grad_b0, 0)), share(wide1, halos[1], 1, 2), frames_reduce(point_parts)
+        )
+        (grads0,) = together(8, frames_gather(grad_conv_of(grad_second0, conv0, 0)))
+        grads0 = jnp.pad(grads0, ((pad, pad), (0, 0)))
+        wide_pos = jnp.arange(rows * tm_count + 2 * pad, dtype=jnp.int32) - pad
+        ids = track_ids(segment_lengths, jnp.floor_divide(wide_pos, stride), total_frames).astype(F32)
+        dil = saliency(
+            spacings,
+            pad,
+            kernel_taps,
+            jnp.broadcast_to(ids[:, None], (ids.shape[0], out_local)),
+            flat,
+            [grads0.astype(F32), grads1.astype(F32)],
+            [frames00, frames01, frames10, frames11],
+        )
+        return outputs(decoded, dil, point_sums.reshape(point_eff.shape))
+
+    saved = []
+    for unit in range(units):
+        first = first_of(hidden, unit)
+        wide = lax.all_gather(with_halo(first, reach[unit]), "chan", axis=1, tiled=True)
+        conv = conv_of(wide, unit, reach[unit])
+        second = lax.all_gather(second_of(conv, unit), "chan", axis=1, tiled=True)
+        saved.append((hidden, wide[reach[unit] : reach[unit] + rows], conv, second))
+        hidden = hidden + dot_last(second, point_eff[unit])
     grad_out = cot.astype(F32)
-    dil_out = [None] * units
-    point_out = [None] * units
+    parts = [None] * (2 * units)
     for unit in reversed(range(units)):
-        spacing = 3 ** (unit + 1)
-        margin = (kernel_taps // 2) * spacing
-        hidden_in, first_own, conv, second_all = saved[unit]
+        hidden_in, first_own, conv, second = saved[unit]
         grad_b = grad_out.astype(BF16)
-        point_grad = dot_first(grad_b, second_all)
         if unit == units - 1:
             grad_second = grad_second_last
         else:
-            grad_second = chan_scatter(
-                jnp.dot(grad_b, point_eff[unit], preferred_element_type=F32).astype(BF16), number
-            )
-            number += 1
-        grad_conv = (grad_second * snake_slope(conv, snake_freq_pointwise[unit])).astype(BF16)
-        weights = dil_eff[unit].reshape(kernel_taps * out_local, channels)
+            grad_second = lax.psum_scatter(
+                spread_back(grad_b, unit), "chan", scatter_dimension=1, tiled=True
+            ).astype(F32)
+        grad_conv = grad_conv_of(grad_second, conv, unit)
+        shifted = shifted_taps(with_halo(grad_conv, reach[unit]), unit, reach[unit])
+        parts[unit] = dot_first(shifted, first_own).astype(BF16)
+        parts[units + unit] = dot_first(grad_b, second).astype(BF16)
         if unit > 0:
-            shifted = shifted_taps(with_halo(grad_conv, margin), row_pos, margin, spacing)
-            grad_first = chan_scatter(
-                jnp.dot(shifted, weights, preferred_element_type=F32).astype(BF16), number
-            )
-            number += 1
-            dil_part, point_part = lax.psum(
-                (dot_first(shifted, first_own).astype(BF16), point_grad.astype(BF16)), "tm"
-            )
-            dil_grad = dil_part.astype(F32)
+            back = jnp.dot(shifted, flat[unit], preferred_element_type=F32).astype(BF16)
+            grad_first = lax.psum_scatter(back, "chan", scatter_dimension=1, tiled=True).astype(F32)
             grad_out = grad_out + grad_first * snake_slope(hidden_in, snake_freq_dilated[unit])
-        else:
-            grad_frames = jnp.pad(tm_gather(grad_conv, number), ((margin, margin), (0, 0)))
-            number += 1
-            dil_grad = dot_first(shifted_taps(grad_frames, all_pos, margin, spacing), first_frames)
-            point_part = lax.psum(point_grad.astype(BF16), "tm")
-        dil_out[unit] = (weights.astype(F32) * dil_grad).reshape(kernel_taps, out_local, channels)
-        point_out[unit] = point_eff[unit].astype(F32) * point_part.astype(F32)
-    return decoded, jnp.stack(dil_out), jnp.stack(point_out)
+    sums = lax.psum(parts, "tm")
+    dil = flat.astype(F32) * jnp.stack(sums[:units]).astype(F32)
+    return outputs(hidden, dil, jnp.stack(sums[units:]))
 
 
 def solution(mesh):

time: 352 us -> 275 us (0.78)
  waiting for transfers between devices: 88.3 us -> 0.04 us
  Pallas kernels: 144 us -> 201 us
  other arithmetic: 37.3 us -> 18 us
  matrix products: 34.3 us -> 21.2 us
  local copies, waits for them, and re-layouts: 31.1 us -> 19.4 us
    pallas_call x0 -> x8, Pallas kernels: none -> 176 us  [the longest x7 149 us: together(): pl.pallas_call(kernel, out_shape=[task[1] for task in tasks], in_specs=[w...]
    pallas_call x8 -> x2, Pallas kernels: 144 us -> 25.1 us  [run(): pl.pallas_call(kernel, out_shape=jax.ShapeDtypeStruct(out_shape, dtype),...]
    all_gather x2 -> x0, waiting for transfers between devices: 52.5 us -> none  [the longest x1 52.5 us: per_device(): first_frames = lax.all_gather(saved[0][1], 'tm', axis=0, tiled=True)]
    psum x1 -> x0, waiting for transfers between devices: 32.3 us -> none  [per_device(): lax.psum((dot_first(shifted, first_own).astype(BF16), point_grad.astype(B...]
    dot_general x4 -> x2, matrix products: 17.4 us -> 2.2 us  [dot_first(): lax.dot_general(left, right, (((0,), (0,)), ((), ())), preferred_element_...]
    unnamed x10 -> x5, other arithmetic: 8.91 us -> 0.92 us
    another operation x4 -> x1, other arithmetic: 8.08 us -> 0.18 us  [the longest x3 7.91 us: per_device(): return (decoded, jnp.stack(dil_out), jnp.stack(point_out))]
    unnamed x58 -> x52, local copies, waits for them, and re-layouts: 11.9 us -> 6.6 us
  transfers between devices with their start and end apart: 6 -> 1, of which waited for: 3 -> 0; matrix products, arithmetic and copies ran while one was open for 17% -> 13% of each run, Pallas kernels for 41% -> 33%
where the time goes in v2:
time: 275 us
  Pallas kernels  201 us (73%)
  matrix products  21.2 us (8%)
  local copies, waits for them, and re-layouts  19.4 us (7%)
  other arithmetic  18 us (7%)
  between operations  14.6 us (5%)
    pallas_call x7, Pallas kernels, together(): pl.pallas_call(kernel, out_shape=[task[1] for task in tasks], in_specs=[w...  149 us
    pallas_call x1, Pallas kernels, saliency(): pl.pallas_call(functools.partial(saliency_kernel, spacings, pad, taps), o...  26.8 us
    pallas_call x2, Pallas kernels, run(): pl.pallas_call(kernel, out_shape=jax.ShapeDtypeStruct(out_shape, dtype),...  25.1 us
    dot_general x5, matrix products, dot_last(): lax.dot_general(left, right, (((1,), (1,)), ((), ())), preferred_element_...  8.92 us
    unnamed x52, local copies, waits for them, and re-layouts  6.6 us
    dot_general x2, matrix products, expand(): jnp.dot(mask.reshape(-1, blocks).astype(BF16), spread, preferred_element_...  6.41 us
    mul x1, local copies, waits for them, and re-layouts, expand(): return (kernel.reshape(-1, width) * keep.astype(BF16)).reshape(kernel.shape)  5.94 us
    reshape x1, local copies, waits for them, and re-layouts, expand(): return (kernel.reshape(-1, width) * keep.astype(BF16)).reshape(kernel.shape)  5.94 us
  transfers between devices with their start and end apart: 1, of which 0 were waited for; matrix products, arithmetic and copies ran while one was open for 13% of the time, Pallas kernels for 33%

profile of v2, /device:TPU:0, one launch (start us, length us, event | category | flops | bytes accessed | tf_op | source)
XLA Modules:
  0.0 274.5 jit_solution(3753496661761735080)
XLA Ops:
  7.2 1.1 convert_element_type.204
  8.3 1.4 fusion.11
  9.7 0.8 copy-done.10
  10.5 1.6 convolution_convert_fusion.2
  12.5 0.3 fusion.53.x_ref
  12.8 13.0 %shard_map.130 = bf16[320,512]{1,0:T(8,128)(2,1)S(1)} custom-call(bf16[80,256]{1,0:T(8,128)(2,1)S(1)} %fusion.53.x_ref), custom_call_target="tpu_custom_call" | custom-call | tf_op jit(solution)/shard_map/pallas_call | solution.py:447
  25.8 1.3 convert_element_type.194
  27.1 0.9 fusion.27
  28.4 0.2 fusion.9
  28.6 0.4 copy.41
  29.0 12.1 %shard_map.131 = f32[640,128]{1,0:T(8,128)S(1)} custom-call(bf16[2560,128]{1,0:T(8,128)(2,1)S(1)} %bitcast.64), custom_call_target="tpu_custom_call" | custom-call | tf_op jit(solution)/shard_map/pallas_call | solution.py:447
  41.1 5.9 %copy.33 = bf16[1792,1024]{0,1:T(8,128)(2,1)} copy(bf16[1792,1024]{1,0:T(8,128)(2,1)} %bitcast.67) | data formatting | bytes 7340032 | tf_op jit(solution)/shard_map/reshape | solution.py:538
  47.0 1.1 add_convert_fusion.3.refs_0_
  48.1 5.1 %bitcast_multiply_fusion = bf16[1792,1024]{0,1:T(8,128)(2,1)} fusion(bf16[1792,1024]{0,1:T(8,128)(2,1)} %copy.33, bf16[1792,128]{1,0:T(8,128)(2,1)S(1)} %bitcast.68, s32[1024]{0:T(1024)S(1)} %add_select_fusion.10), kind=kOutput, calls=%fused_computation.1 | convolution fusion | flops 473694208 | bytes 7802880 | tf_op jit(solution)/shard_map/dot_general | solution.py:537
  53.2 0.8 copy.36
  54.0 23.1 %shard_map.132.refs_1_ = bf16[672,1024]{1,0:T(8,128)(2,1)S(1)} custom-call(bf16[640,128]{1,0:T(8,128)(2,1)S(1)} %add_convert_fusion.3.refs_0_), custom_call_target="tpu_custom_call" | custom-call | tf_op jit(solution)/shard_map/pallas_call | solution.py:297
  77.1 5.9 %copy.35 = bf16[1792,1024]{1,0:T(8,128)(2,1)} copy(bf16[1792,1024]{0,1:T(8,128)(2,1)} %bitcast_multiply_fusion) | data formatting | bytes 7340032 | tf_op jit(solution)/shard_map/mul | solution.py:538
  83.2 3.1 %fusion = f32[672,896]{1,0:T(8,128)S(1)} fusion(bf16[672,1024]{1,0:T(8,128)(2,1)S(1)} %shard_map.132.refs_1_, bf16[1792,1024]{0,1:T(8,128)(2,1)} %bitcast_multiply_fusion), kind=kOutput, calls=%fused_computation.2 | convolution fusion | flops 1233125376 | bytes 5619712 | tf_op jit(solution)/shard_map/dot_general | solution.py:524
  86.3 2.8 %add_convert_fusion.2 = (bf16[640,128]{1,0:T(8,128)(2,1)S(1)}, f32[640,128]{1,0:T(8,128)}) fusion(f32[128]{0:T(128)S(1)} %get-tuple-element.72, f32[672,896]{1,0:T(8,128)S(1)} %fusion, pred[640]{0:T(1024)(128)(4,1)S(1)} %get-tuple-element.60, pred[640]{0:T(1024)(128)(4,1)S(1)} %get-tuple-element.61, pred[640]{0:T(1024)(128)(4,1)S(1)} %get-tuple-element.62, ...), kind=kLoop, calls=%fused_computation.63 | loop fusion | flops 1392640 | bytes 2789632 | tf_op jit(solution)/shard_map/convert_element_type | solution.py:616
  89.1 20.8 %shard_map.133 = (bf16[640,1024]{1,0:T(8,128)(2,1)S(1)}, bf16[2560,512]{1,0:T(8,128)(2,1)S(1)}) custom-call(bf16[640,128]{1,0:T(8,128)(2,1)S(1)} %get-tuple-element.53.refs_0_, bf16[672,1024]{1,0:T(8,128)(2,1)S(1)} %shard_map.132.refs_1_), custom_call_target="tpu_custom_call" | custom-call | tf_op jit(solution)/shard_map/pallas_call | solution.py:297
  110.0 2.1 add_convert_fusion.1
  112.1 22.9 %shard_map.134 = (bf16[704,1024]{1,0:T(8,128)(2,1)S(1)}, bf16[2560,512]{1,0:T(8,128)(2,1)S(1)}) custom-call(bf16[640,128]{1,0:T(8,128)(2,1)S(1)} %get-tuple-element.76.refs_0_, bf16[672,1024]{1,0:T(8,128)(2,1)S(1)} %shard_map.132.refs_1_), custom_call_target="tpu_custom_call" | custom-call | tf_op jit(solution)/shard_map/pallas_call | solution.py:297
  135.2 1.7 fusion.4
  136.9 2.4 add_convert_fusion
  139.3 1.1 copy.39
  140.5 1.1 multiply_convert_fusion.1.refs_0_
  141.6 17.0 %shard_map.135 = (bf16[2560,128]{1,0:T(8,128)(2,1)S(1)}, bf16[640,1024]{1,0:T(8,128)(2,1)S(1)}) custom-call(bf16[640,128]{1,0:T(8,128)(2,1)S(1)} %multiply_convert_fusion.1.refs_0_, bf16[640,128]{1,0:T(8,128)(2,1)S(1)} %get-tuple-element.51.refs_1_), custom_call_target="tpu_custom_call" | custom-call | tf_op jit(solution)/shard_map/pallas_call | solution.py:297
  158.6 1.1 fusion.12
  159.7 1.2 fusion.14
  160.9 1.2 pad_convert_fusion.1.refs_1_
  162.7 0.2 fusion.46
  162.9 0.2 fusion.48
  163.1 0.2 fusion.37
  163.3 1.2 copy-done.9
  164.5 1.6 fusion.6.refs_0_
  166.0 23.2 %shard_map.136 = (f32[640,128]{1,0:T(8,128)S(1)}, bf16[2560,512]{1,0:T(8,128)(2,1)S(1)}) custom-call(bf16[640,1024]{1,0:T(8,128)(2,1)S(1)} %fusion.6.refs_0_, bf16[704,1024]{1,0:T(8,128)(2,1)S(1)} %get-tuple-element.15.refs_1_), custom_call_target="tpu_custom_call" | custom-call | tf_op jit(solution)/shard_map/pallas_call | solution.py:297
  189.3 1.1 fusion.26
  190.4 1.1 convolution_convert_fusion.5
  191.5 0.5 convolution_convert_fusion.1.refs_0_
  192.0 1.7 copy.37
  193.7 1.1 pad_maximum_fusion.refs_2_
  194.8 32.8 %shard_map.137 = (f32[640,128]{1,0:T(8,128)S(1)}, bf16[2560,512]{1,0:T(8,128)(2,1)}, bf16[256,1024]{1,0:T(8,128)(2,1)S(1)}) custom-call(bf16[640,1024]{1,0:T(8,128)(2,1)S(1)} %convolution_convert_fusion.1.refs_0_, bf16[704,1024]{1,0:T(8,128)(2,1)S(1)} %get-tuple-element.15.refs_1_, bf16[256,1024]{1,0:T(8,128)(2,1)S(1)} %pad_maximum_fusion.refs_2_), custom_call_target="tpu_custom_call" | custom-call | tf_op jit(solution)/shard_map/pallas_call | solution.py:297
  227.6 1.1 multiply_convert_fusion.refs_0_
  228.7 9.7 %shard_map.138 = bf16[2560,128]{1,0:T(8,128)(2,1)S(1)} custom-call(bf16[640,128]{1,0:T(8,128)(2,1)S(1)} %multiply_convert_fusion.refs_0_), custom_call_target="tpu_custom_call" | custom-call | tf_op jit(solution)/shard_map/pallas_call | solution.py:297
  238.4 1.2 convert_multiply_fusion
  239.7 0.4 broadcast_in_dim.381.ids_ref
  240.1 0.8 copy-done.2
  240.9 26.8 %shard_map.139 = f32[2,896,1024]{2,1,0:T(8,128)} custom-call(f32[2624,128]{1,0:T(8,128)S(1)} %broadcast_in_dim.381.ids_ref, bf16[2,896,1024]{2,1,0:T(8,128)(2,1)} %bitcast.65, f32[2624,128]{1,0:T(8,128)S(1)} %pad_convert_fusion.refs_0_, f32[2624,128]{1,0:T(8,128)S(1)} %copy-done.2, bf16[2560,512]{1,0:T(8,128)(2,1)} %copy-done.3, ...), custom_call_target="tpu_custom_call" | custom-call | tf_op jit(solution)/shard_map/pallas_call | solution.py:344
  (75 shorter events, 1.8 us)
Async XLA Ops:
  7.2 19.9 %copy-start = (bf16[16,128,512]{2,1,0:T(8,128)(2,1)S(1)}, bf16[16,128,512]{2,1,0:T(8,128)(2,1)}, u32[]{:S(2)}) copy-start(bf16[16,128,512]{2,1,0:T(8,128)(2,1)} %param.12) | copy-start | bytes 6291460
  7.2 3.3 %copy-start.14 = (bf16[128,640]{1,0:T(8,128)(2,1)S(1)}, bf16[128,640]{1,0:T(8,128)(2,1)}, u32[]{:S(2)}) copy-start(bf16[128,640]{1,0:T(8,128)(2,1)} %param.21) | copy-start | bytes 491524
  7.2 132.1 %reduce-scatter.4.cloned.1.call-start = ((), (), s32[]{:S(2)}) async-start(), calls=%async_computation.1 | async-start | bytes 1474560
  9.7 0.8 copy-start.10
  10.5 1.8 copy-start.23
  10.5 2.0 copy-start.21
  10.5 2.0 copy-start.19
  10.5 2.0 copy-start.22
  77.1 6.1 %copy-start.20 = (f32[2,128]{1,0:T(2,128)S(1)}, f32[2,128]{1,0:T(2,128)}, u32[]{:S(2)}) copy-start(f32[2,128]{1,0:T(2,128)} %param.19) | copy-start | bytes 3076
  89.1 20.8 %copy-start.11 = (bf16[256,1024]{1,0:T(8,128)(2,1)S(1)}, bf16[256,1024]{1,0:T(8,128)(2,1)}, u32[]{:S(2)}) copy-start(bf16[256,1024]{1,0:T(8,128)(2,1)} %copy-done.10) | copy-start | bytes 1572868
  109.9 2.2 copy-start.3
  109.9 2.2 copy-start.6
  110.0 25.2 %copy-start.8 = (bf16[1792,1024]{0,1:T(8,128)(2,1)S(1)}, bf16[1792,1024]{0,1:T(8,128)(2,1)}, u32[]{:S(2)}) copy-start(bf16[1792,1024]{0,1:T(8,128)(2,1)} %bitcast_multiply_fusion) | copy-start | bytes 11010052
  135.0 1.8 copy-start.4
  139.3 19.3 %copy-start.15 = (bf16[128,640]{1,0:T(8,128)(2,1)S(1)}, bf16[128,640]{1,0:T(8,128)(2,1)}, u32[]{:S(2)}) copy-start(bf16[128,640]{1,0:T(8,128)(2,1)} %param.21) | copy-start | bytes 491524
  140.4 19.3 %copy-start.12 = (bf16[256,1024]{1,0:T(8,128)(2,1)S(1)}, bf16[256,1024]{1,0:T(8,128)(2,1)}, u32[]{:S(2)}) copy-start(bf16[256,1024]{1,0:T(8,128)(2,1)} %copy-done.10) | copy-start | bytes 1572868
  140.5 19.2 %copy-start.16 = (f32[640,128]{1,0:T(8,128)S(1)}, f32[640,128]{1,0:T(8,128)}, u32[]{:S(2)}) copy-start(f32[640,128]{1,0:T(8,128)} %get-tuple-element.77) | copy-start | bytes 983044
  162.4 2.0 copy-start.9
  166.0 23.2 %copy-start.18 = (bf16[128,640]{0,1:T(8,128)(2,1)S(1)}, bf16[128,640]{0,1:T(8,128)(2,1)}, u32[]{:S(2)}) copy-start(bf16[128,640]{0,1:T(8,128)(2,1)} %copy.36) | copy-start | bytes 491524
  166.0 24.3 %copy-start.7 = (bf16[640,1024]{1,0:T(8,128)(2,1)S(1)}, bf16[640,1024]{1,0:T(8,128)(2,1)}, u32[]{:S(2)}) copy-start(bf16[640,1024]{1,0:T(8,128)(2,1)} %copy-done.6) | copy-start | bytes 3932164
  189.2 2.3 copy-start.5
  194.8 32.8 %copy-start.17 = (f32[640,128]{1,0:T(8,128)S(1)}, f32[640,128]{1,0:T(8,128)}, u32[]{:S(2)}) copy-start(f32[640,128]{1,0:T(8,128)} %get-tuple-element.54) | copy-start | bytes 983044
  227.6 10.8 %copy-start.13 = (bf16[256,1024]{1,0:T(8,128)(2,1)S(1)}, bf16[256,1024]{1,0:T(8,128)(2,1)}, u32[]{:S(2)}) copy-start(bf16[256,1024]{1,0:T(8,128)(2,1)} %copy-done.10) | copy-start | bytes 1572868
  239.6 1.3 copy-start.2
  240.9 26.8 %copy-start.1 = (bf16[16,128,512]{2,1,0:T(8,128)(2,1)S(1)}, bf16[16,128,512]{2,1,0:T(8,128)(2,1)}, u32[]{:S(2)}) copy-start(bf16[16,128,512]{2,1,0:T(8,128)(2,1)} %param.12) | copy-start | bytes 6291460
Sparse Core Ops, SparseCore 0:
  12.3 37.6 reduce-scatter.3

commit v3 on v2

--- a/solution.py
+++ b/solution.py
@@ -43,69 +43,43 @@
 
 
 def chan_gather_task(halo):
-    def body(x_ref, o_ref, send, recv, fsend, frecv, hsend, hrecv):
+    def body(x_ref, o_ref, send, recv, fsend, frecv):
         tm, chan, core, chips, partner, at = chan_place()
         frames = lax.axis_size("tm")
         rows, width = x_ref.shape
-        after = ((tm + 1) % frames, chan)
-        before = ((tm + frames - 1) % frames, chan)
-        spans = [pl.ds(halo, rows)]
-        sources = [x_ref]
         mine = column(chan, width)
+        other = 1 - 2 * core
+        parts = [(pl.ds(halo, rows), x_ref, tm, range(1, chips))]
         if halo:
-            spans += [pl.ds(0, halo), pl.ds(halo + rows, halo)]
-            sources += [o_ref.at[spans[1], mine], o_ref.at[spans[2], mine]]
-            edges = [
-                remote(x_ref.at[pl.ds(rows - halo, halo)], o_ref.at[spans[1], mine], hsend.at[0], hrecv.at[0], after),
-                remote(x_ref.at[pl.ds(0, halo)], o_ref.at[spans[2], mine], hsend.at[1], hrecv.at[1], before),
+            parts += [
+                (pl.ds(0, halo), x_ref.at[pl.ds(rows - halo, halo)], (tm + 1) % frames, range(chips)),
+                (pl.ds(halo + rows, halo), x_ref.at[pl.ds(0, halo)], (tm + frames - 1) % frames, range(chips)),
             ]
-            for edge in edges:
-                edge.start()
         started = []
 
-        def spread(part):
-            for step in range(1, chips):
-                copy = remote(
-                    sources[part], o_ref.at[spans[part], mine], send.at[part, step], recv.at[part, step], (tm, at(step))
-                )
-                copy.start()
-                started.append(copy)
-            copy = remote(sources[part], o_ref.at[spans[part], mine], send.at[part, 0], recv.at[part, 0], partner)
+        def begin(copy):
             copy.start()
             started.append(copy)
 
-        spread(0)
+        for part, (span, source, to, steps) in enumerate(parts):
+            for step in steps:
+                begin(remote(source, o_ref.at[span, mine], send.at[part, step], recv.at[part, step], (to, at(step))))
+        begin(remote(x_ref, o_ref.at[parts[0][0], mine], fsend.at[0, 0], frecv.at[0, 0], partner))
         yield
-        if halo:
-            for edge in edges:
-                edge.wait_recv()
-            spread(1)
-            spread(2)
-        o_ref[spans[0], mine] = x_ref[...]
-
-        def arrival(part, index, sems, step):
-            slot = o_ref.at[spans[part], column(index, width)]
-            return remote(slot, slot, send.at[part, step], sems.at[part, step], partner)
-
-        for step in range(1, chips):
-            for part in range(len(spans)):
-                index = at(-step)
-                arrival(part, index, recv, step).wait_recv()
-                slot = o_ref.at[spans[part], column(index, width)]
-                copy = remote(slot, slot, fsend.at[part, step], frecv.at[part, step], partner)
-                copy.start()
-                started.append(copy)
+        o_ref[parts[0][0], mine] = x_ref[...]
+        for step in range(chips):
+            for part, (span, source, to, steps) in enumerate(parts):
+                if step in steps:
+                    slot = o_ref.at[span, column(at(-step), width)]
+                    remote(slot, slot, send.at[part, step], recv.at[part, step], partner).wait_recv()
+                    begin(remote(slot, slot, fsend.at[part, step], frecv.at[part, step], partner))
         yield
-        other = 1 - 2 * core
-        for part in range(len(spans)):
-            arrival(part, chan + other, recv, 0).wait_recv()
-            for step in range(1, chips):
-                arrival(part, at(-step) + other, frecv, step).wait_recv()
+        for part, (span, source, to, steps) in enumerate(parts):
+            for step in range(chips):
+                slot = o_ref.at[span, column(at(-step) + other, width)]
+                remote(slot, slot, fsend.at[part, step], frecv.at[part, step], partner).wait_recv()
         for copy in started:
             copy.wait_send()
-        if halo:
-            for edge in edges:
-                edge.wait_send()
 
     return body
 
@@ -237,58 +211,90 @@
     rows, width = value.shape
     chans = lax.axis_size("chan")
     out = jax.ShapeDtypeStruct((rows + 2 * halo, width * chans), value.dtype)
-    return value, out, [DMA((3, chans // 2))] * 4 + [DMA((2,))] * 2, chan_gather_task(halo), False, halo > 0
+    return (value,), out, [DMA((3, chans // 2))] * 4, chan_gather_task(halo), ("chan", "edge") if halo else ("chan",)
 
 
 def chan_scatter(value):
     rows, chans = value.shape[0], lax.axis_size("chan")
     width, chips = value.shape[1] // chans, chans // 2
     scratch = [pltpu.VMEM((chips, rows, width), value.dtype)] * 3 + [DMA((chips,))] * 4
-    return value, jax.ShapeDtypeStruct((rows, width), F32), scratch, chan_scatter_body, False, False
+    return (value,), jax.ShapeDtypeStruct((rows, width), F32), scratch, chan_scatter_body, ("chan",)
 
 
 def share(value, halo, part, parts):
     count = lax.axis_size("tm")
     rows, width = value.shape[0] - 2 * halo, value.shape[1] // parts
     out = jax.ShapeDtypeStruct((rows * count, width), value.dtype)
-    return value, out, [DMA((count,))] * 4, share_task(halo, part * width), True, False
+    return (value,), out, [DMA((count,))] * 4, share_task(halo, part * width), ("chan", "tm")
 
 
 def frames_gather(value):
     count = lax.axis_size("tm")
     out = jax.ShapeDtypeStruct((value.shape[0] * count, value.shape[1]), value.dtype)
-    return value, out, [DMA((count,))] * 2, frames_gather_body, True, False
+    return (value,), out, [DMA((count,))] * 2, frames_gather_body, ("tm",)
 
 
 def frames_reduce(value):
     count = lax.axis_size("tm")
     landed = pltpu.VMEM((count, value.shape[0], value.shape[1] // count), value.dtype)
-    return value, jax.ShapeDtypeStruct(value.shape, value.dtype), [landed] + [DMA((count,))] * 4, reduce_body, True, False
+    scratch = [landed] + [DMA((count,))] * 4
+    return (value,), jax.ShapeDtypeStruct(value.shape, value.dtype), scratch, reduce_body, ("tm",)
+
+
+def frames_scatter(value):
+    count = lax.axis_size("tm")
+    rows, width = value.shape[0] // count, value.shape[1]
+    scratch = [pltpu.VMEM((count, rows, width), value.dtype)] + [DMA((count,))] * 2
+    return (value,), jax.ShapeDtypeStruct((rows, width), F32), scratch, frames_scatter_body, ("tm",)
+
+
+def expand_body(kernel_ref, mask_ref, o_ref):
+    yield
+    rows, width = kernel_ref.shape
+    blocks = mask_ref.shape[1]
+    spread = (
+        lax.broadcasted_iota(jnp.int32, (blocks, width), 1) // (width // blocks)
+        == lax.broadcasted_iota(jnp.int32, (blocks, width), 0)
+    ).astype(F32).astype(BF16)
+    step = 256
+
+    @pl.loop(0, rows // step)
+    def _(block):
+        span = pl.ds(pl.multiple_of(block * step, step), step)
+        keep = jnp.dot(mask_ref[span].astype(F32).astype(BF16), spread, preferred_element_type=F32)
+        o_ref[span] = (kernel_ref[span].astype(F32) * keep).astype(o_ref.dtype)
+
+    yield
+
+
+def expand_task(kernel, mask):
+    return (kernel, mask), jax.ShapeDtypeStruct(kernel.shape, kernel.dtype), [], expand_body, ()
 
 
 def together(number, *tasks):
-    along_chan = any(not task[4] for task in tasks) or any(len(task[2]) == 4 for task in tasks)
-    along_tm = any(task[4] for task in tasks)
-    edges = any(task[5] for task in tasks)
+    axes = set(axis for task in tasks for axis in task[4])
+    inputs = [item for task in tasks for item in task[0]]
 
     def kernel(*refs):
         tm, chan, core, chips, partner, at = chan_place()
         count = lax.axis_size("tm")
         greeted = []
-        if along_chan:
+        if "chan" in axes:
             greeted += [partner] + [(tm, at(step)) for step in range(1, chips)]
-        if along_tm:
+        if "tm" in axes:
             greeted += [((tm + step) % count, chan) for step in range(1, count)]
-        elif edges:
+        elif "edge" in axes:
             greeted += [((tm + 1) % count, chan), ((tm + count - 1) % count, chan)]
+        if "edge" in axes:
+            for step in range(1, chips):
+                greeted += [((tm + 1) % count, at(step)), ((tm + count - 1) % count, at(step))]
         greet(greeted)
-        size = len(tasks)
-        place = 2 * size
+        taken, out, place = 0, len(inputs), len(inputs) + len(tasks)
         bodies = []
-        for index, task in enumerate(tasks):
-            scratch = refs[place : place + len(task[2])]
-            place += len(task[2])
-            bodies.append(task[3](refs[index], refs[size + index], *scratch))
+        for task in tasks:
+            used = refs[taken : taken + len(task[0])] + (refs[out],) + refs[place : place + len(task[2])]
+            taken, out, place = taken + len(task[0]), out + 1, place + len(task[2])
+            bodies.append(task[3](*used))
         for phase in range(3):
             for body in bodies:
                 next(body, None)
@@ -297,65 +303,140 @@
     return pl.pallas_call(
         kernel,
         out_shape=[task[1] for task in tasks],
-        in_specs=[whole] * len(tasks),
+        in_specs=[whole] * len(inputs),
         out_specs=[whole] * len(tasks),
         scratch_shapes=[item for task in tasks for item in task[2]],
         compiler_params=pltpu.CompilerParams(
             collective_id=number, has_side_effects=True, vmem_limit_bytes=VMEM_LIMIT
         ),
-    )(*[task[0] for task in tasks])
-
-
-def saliency_kernel(spacings, pad, taps, ids_ref, eff_ref, *refs):
+    )(*inputs)
+
+
+def taps_kernel(halo, spacing, taps, x_ref, w_ref, ids_ref, alpha_ref, conv_ref, second_ref, spans):
+    rows, width = conv_ref.shape
+    step = 2 * width
+    total = taps * width
+    for base in range(0, total, step):
+        span = pl.ds(base, min(step, total - base))
+        spans[:, span] = lax.dot_general(
+            x_ref[...], w_ref[span], (((1,), (1,)), ((), ())), preferred_element_type=F32
+        )
+    alpha = alpha_ref[...]
+    chunk = 128 if rows % 128 == 0 else rows
+    for start in range(0, rows, chunk):
+        own = ids_ref[pl.ds(start + halo, chunk)]
+        conv = jnp.zeros((chunk, width), F32)
+        for tap in range(taps):
+            window = pl.ds(start + halo + (tap - taps // 2) * spacing, chunk)
+            conv = conv + jnp.where(ids_ref[window] == own, spans[window, pl.ds(tap * width, width)], 0.0)
+        conv_ref[pl.ds(start, chunk)] = conv
+        second_ref[pl.ds(start, chunk)] = snake_act(conv, alpha).astype(second_ref.dtype)
+
+
+def taps_call(wide, weights, ids, alpha, halo, spacing, taps):
+    rows, width = wide.shape[0] - 2 * halo, weights.shape[0] // taps
+    whole = pl.BlockSpec(memory_space=pltpu.VMEM)
+    return pl.pallas_call(
+        functools.partial(taps_kernel, halo, spacing, taps),
+        out_shape=[jax.ShapeDtypeStruct((rows, width), F32), jax.ShapeDtypeStruct((rows, width), BF16)],
+        in_specs=[whole] * 4,
+        out_specs=[whole] * 2,
+        scratch_shapes=[pltpu.VMEM((wide.shape[0], weights.shape[0]), F32)],
+        compiler_params=pltpu.CompilerParams(vmem_limit_bytes=VMEM_LIMIT),
+    )(wide, weights, ids, alpha)
+
+
+def saliency_kernel(spacings, taps, mask_ref, *refs):
     units = len(spacings)
-    grads, firsts = refs[:units], refs[units : 3 * units]
-    o_ref, turned = refs[3 * units], refs[3 * units + 1]
-    rows = turned.shape[1]
-    width = ids_ref.shape[1]
-    chunk = 512
-    for unit in range(units):
-        for tap in range(taps):
-            shift = (tap - taps // 2) * spacings[unit]
-
-            @pl.loop(0, rows // chunk)
-            def _(block):
-                start = pl.multiple_of(block * chunk, chunk)
-                window = grads[unit][pl.ds(start + pad - shift, chunk)]
-                same = ids_ref[pl.ds(start + pad - shift, chunk)] == ids_ref[pl.ds(start + pad, chunk)]
-                kept = jnp.where(same, window, 0.0)
-                turned[pl.ds(tap * width, width), pl.ds(start, chunk)] = kept.T.astype(turned.dtype)
-
-        for half in range(2):
-            source = firsts[2 * unit + half]
-            span = source.shape[1]
-            step = 256
-
-            @pl.loop(0, span // step)
-            def _(block):
-                inner = pl.ds(pl.multiple_of(block * step, step), step)
-                outer = pl.ds(pl.multiple_of(half * span + block * step, step), step)
-                grad = jnp.dot(turned[...], source[:, inner], preferred_element_type=F32)
-                o_ref[unit, :, outer] = eff_ref[unit, :, outer].astype(F32) * grad
-
-
-def saliency(spacings, pad, taps, ids, eff, grads, firsts):
-    whole = pl.BlockSpec(memory_space=pltpu.VMEM)
-    operands = [ids, eff] + grads + firsts
+    grads, eff_ref, firsts = refs[:units], refs[units], refs[units + 1 : 3 * units + 1]
+    o_ref, flipped, turned, eff, first, made, loads, stores = refs[3 * units + 1 :]
+    rows, width = grads[0].shape
+    order = list(reversed(range(units)))
+    span = firsts[0].shape[1]
+    copies = {}
+    for unit in order:
+        copies[unit] = [
+            pltpu.make_async_copy(
+                firsts[2 * unit + half], first.at[unit, :, pl.ds(half * span, span)], loads.at[unit, half]
+            )
+            for half in range(2)
+        ] + [pltpu.make_async_copy(eff_ref.at[unit], eff.at[unit], loads.at[unit, 2])]
+        for copy in copies[unit]:
+            copy.start()
+    chunk, lines, step = 512, 16, 256
+    blocks = 2 * span // step
+    for place, unit in enumerate(order):
+
+        @pl.loop(0, rows // chunk)
+        def _(block):
+            part = pl.ds(pl.multiple_of(block * chunk, chunk), chunk)
+            flipped[:, part] = grads[unit][part].astype(F32).T
+
+        @pl.loop(0, width // lines)
+        def _(block):
+            values = flipped[pl.ds(pl.multiple_of(block * lines, lines), lines)]
+            for tap in range(taps):
+                shift = ((tap - taps // 2) * spacings[unit]) % rows
+                moved = pltpu.roll(values, shift, 1) if shift else values
+                kept = moved * mask_ref[pl.ds(unit * taps + tap, 1)]
+                line = pl.multiple_of(tap * width + block * lines, lines)
+                turned[pl.ds(line, lines)] = kept.astype(turned.dtype)
+
+        for copy in copies[unit]:
+            copy.wait()
+
+        def store(slot, block):
+            outer = pl.ds(pl.multiple_of(block * step, step), step)
+            return pltpu.make_async_copy(made.at[slot], o_ref.at[unit, :, outer], stores.at[slot])
+
+        @pl.loop(0, blocks)
+        def _(block):
+            slot = block % 2
+            outer = pl.ds(pl.multiple_of(block * step, step), step)
+            grad = jnp.dot(turned[...], first[unit, :, outer], preferred_element_type=F32)
+            if place:
+                store(slot, block).wait()
+            else:
+
+                @pl.when(block >= 2)
+                def _():
+                    store(slot, block).wait()
+
+            made[slot] = eff[unit, :, outer].astype(F32) * grad
+            store(slot, block).start()
+
+        if place == units - 1:
+            for slot in range(2):
+                store(slot, slot).wait()
+
+
+def saliency(spacings, taps, masks, eff, grads, firsts):
+    whole, anywhere = pl.BlockSpec(memory_space=pltpu.VMEM), pl.BlockSpec(memory_space=pl.ANY)
+    units = len(spacings)
+    rows, width = grads[0].shape
+    operands = [masks] + grads + [eff] + firsts
     return pl.pallas_call(
-        functools.partial(saliency_kernel, spacings, pad, taps),
+        functools.partial(saliency_kernel, spacings, taps),
         out_shape=jax.ShapeDtypeStruct(eff.shape, F32),
-        in_specs=[whole] * len(operands),
-        out_specs=whole,
-        scratch_shapes=[pltpu.VMEM((eff.shape[1], firsts[0].shape[0]), BF16)],
+        in_specs=[whole] * (1 + units) + [anywhere] * (1 + 2 * units),
+        out_specs=anywhere,
+        scratch_shapes=[
+            pltpu.VMEM((width, rows), F32),
+            pltpu.VMEM((taps * width, rows), BF16),
+            pltpu.VMEM(eff.shape, BF16),
+            pltpu.VMEM((units, rows, eff.shape[2]), BF16),
+            pltpu.VMEM((2, eff.shape[1], 256), F32),
+            DMA((units, 3)),
+            DMA((2,)),
+        ],
         compiler_params=pltpu.CompilerParams(vmem_limit_bytes=VMEM_LIMIT),
     )(*operands)
 
 
-def tm_scatter_kernel(x_ref, o_ref, landed, send, recv):
+def frames_scatter_body(x_ref, o_ref, landed, send, recv):
     tm, chan = lax.axis_index("tm"), lax.axis_index("chan")
     count = lax.axis_size("tm")
     rows = o_ref.shape[0]
-    greet([((tm + step) % count, chan) for step in range(1, count)])
     started = []
     for step in range(1, count):
         to = (tm + step) % count
@@ -368,7 +449,9 @@
         )
         copy.start()
         started.append(copy)
+    yield
     o_ref[...] = x_ref[pl.ds(pl.multiple_of(tm * rows, rows), rows)].astype(F32)
+    yield
     for step in range(1, count):
         started[step - 1].wait_recv()
         o_ref[...] += landed[step].astype(F32)
@@ -470,22 +553,6 @@
             lax.ppermute(head, "tm", [((i + 1) % count, i) for i in range(count)]),
         ],
         axis=0,
-    )
-
-
-def tm_scatter(value, number):
-    count = lax.axis_size("tm")
-    rows, width = value.shape[0] // count, value.shape[1]
-    if not plain_kernels(width):
-        return lax.psum_scatter(value, "tm", scatter_dimension=0, tiled=True).astype(F32)
-    dma = pltpu.SemaphoreType.DMA
-    return run(
-        tm_scatter_kernel,
-        (rows, width),
-        F32,
-        [pltpu.VMEM((count, rows, width), value.dtype)] + [dma((count,))] * 2,
-        number,
-        value,
     )
 
 
@@ -569,7 +636,6 @@
     row_pos = tm_index * rows + jnp.arange(rows, dtype=jnp.int32)
     frame_pos = jnp.arange(total_frames, dtype=jnp.int32)
 
-    dil_eff = expand(dilated_kernel, dilated_prune_mask)
     point_eff = expand(pointwise_kernel, pointwise_prune_mask)
 
     act = snake_act(latent_input.astype(F32), snake_freq_upsample[:, None]).astype(BF16).T
@@ -593,12 +659,12 @@
     partial = product[:, half : half + stride] + jnp.concatenate(
         [jnp.where(prev_ok, low, 0.0), jnp.where(next_ok, high, 0.0)], axis=1
     )
-    hidden = tm_scatter(partial.astype(BF16).reshape(rows * tm_count, out_local), 1)
+    partial = partial.astype(BF16).reshape(rows * tm_count, out_local)
 
     spacings = [3 ** (unit + 1) for unit in range(units)]
     reach = [(kernel_taps // 2) * spacing for spacing in spacings]
-    flat = dil_eff.reshape(units, kernel_taps * out_local, channels)
-    fast = units == 2 and plain_kernels(out_local, channels // 4, channels // tm_count) and frame_count % 16 == 0 and rows * tm_count % 512 == 0
+    fast = units == 2 and plain_kernels(out_local, channels // 4, channels // tm_count)
+    fast = fast and frame_count % 16 == 0 and rows * tm_count % 512 == 0 and units * kernel_taps * out_local % 256 == 0
 
     def conv_of(first_all, unit, halo):
         spans = dot_last(first_all, flat[unit])
@@ -638,44 +704,68 @@
 
     if fast:
         halos = [-(-margin // 16) * 16 for margin in reach]
+        hidden, flat = together(
+            1,
+            frames_scatter(partial),
+            expand_task(
+                dilated_kernel.reshape(-1, channels),
+                dilated_prune_mask.reshape(-1, dilated_prune_mask.shape[-1]),
+            ),
+        )
+        flat = flat.reshape(units, kernel_taps * out_local, channels)
+
+        def taps_of(wide, unit):
+            pos = tm_index * rows - halos[unit] + jnp.arange(wide.shape[0], dtype=jnp.int32)
+            ids = track_ids(segment_lengths, jnp.floor_divide(pos, stride), total_frames).astype(F32)
+            ids = jnp.broadcast_to(ids[:, None], (wide.shape[0], out_local))
+            alpha = snake_freq_pointwise[unit][None]
+            return taps_call(wide, flat[unit], ids, alpha, halos[unit], spacings[unit], kernel_taps)
+
         (wide0,) = together(2, chan_gather(first_of(hidden, 0), halos[0]))
-        conv0 = conv_of(wide0, 0, halos[0])
-        second0, frames00 = together(3, chan_gather(second_of(conv0, 0), 0), share(wide0, halos[0], 0, 2))
+        conv0, mid0 = taps_of(wide0, 0)
+        second0, frames00 = together(3, chan_gather(mid0, 0), share(wide0, halos[0], 0, 2))
         hidden1 = hidden + dot_last(second0, point_eff[0])
         wide1, frames01 = together(
             4, chan_gather(first_of(hidden1, 1), halos[1]), share(wide0, halos[0], 1, 2)
         )
-        conv1 = conv_of(wide1, 1, halos[1])
+        conv1, mid1 = taps_of(wide1, 1)
         grad_conv1 = grad_conv_of(grad_second_last, conv1, 1)
-        grads1, second1 = together(5, frames_gather(grad_conv1), chan_gather(second_of(conv1, 1), 0))
+        grads1, second1 = together(5, frames_gather(grad_conv1), chan_gather(mid1, 0))
         decoded = hidden1 + dot_last(second1, point_eff[1])
         pad = halos[1]
-        grads1 = jnp.pad(grads1, ((pad, pad), (0, 0)))
-        window = lax.dynamic_slice_in_dim(grads1, tm_index * rows, rows + 2 * pad, axis=0)
+        window = lax.dynamic_slice_in_dim(jnp.pad(grads1, ((pad, pad), (0, 0))), tm_index * rows, rows + 2 * pad, axis=0)
         partial1 = jnp.dot(
             shifted_taps(window, 1, pad), flat[1], preferred_element_type=F32
         ).astype(BF16)
-        grad_first, frames10 = together(6, chan_scatter(partial1), share(wide1, halos[1], 0, 2))
+        grad_first, points1, frames10 = together(
+            6,
+            chan_scatter(partial1),
+            frames_reduce(dot_first(cot, second1).astype(BF16)),
+            share(wide1, halos[1], 0, 2),
+        )
         grad_b0 = (cot.astype(F32) + grad_first * snake_slope(hidden1, snake_freq_dilated[1])).astype(BF16)
-        point_parts = jnp.concatenate([dot_first(grad_b0, second0), dot_first(cot, second1)]).astype(BF16)
-        grad_second0, frames11, point_sums = together(
-            7, chan_scatter(spread_back(grad_b0, 0)), share(wide1, halos[1], 1, 2), frames_reduce(point_parts)
+        grad_second0, points0, frames11 = together(
+            7,
+            chan_scatter(spread_back(grad_b0, 0)),
+            frames_reduce(dot_first(grad_b0, second0).astype(BF16)),
+            share(wide1, halos[1], 1, 2),
         )
         (grads0,) = together(8, frames_gather(grad_conv_of(grad_second0, conv0, 0)))
-        grads0 = jnp.pad(grads0, ((pad, pad), (0, 0)))
-        wide_pos = jnp.arange(rows * tm_count + 2 * pad, dtype=jnp.int32) - pad
-        ids = track_ids(segment_lengths, jnp.floor_divide(wide_pos, stride), total_frames).astype(F32)
+        all_pos = jnp.arange(rows * tm_count, dtype=jnp.int32)
+        masks = jnp.stack(
+            [
+                tap_mask(all_pos, -(tap - kernel_taps // 2) * spacing)[:, 0].astype(F32)
+                for spacing in spacings
+                for tap in range(kernel_taps)
+            ]
+        )
         dil = saliency(
-            spacings,
-            pad,
-            kernel_taps,
-            jnp.broadcast_to(ids[:, None], (ids.shape[0], out_local)),
-            flat,
-            [grads0.astype(F32), grads1.astype(F32)],
-            [frames00, frames01, frames10, frames11],
-        )
-        return outputs(decoded, dil, point_sums.reshape(point_eff.shape))
-
+            spacings, kernel_taps, masks, flat, [grads0, grads1], [frames00, frames01, frames10, frames11]
+        )
+        return outputs(decoded, dil, jnp.stack([points0, points1]))
+
+    hidden = lax.psum_scatter(partial, "tm", scatter_dimension=0, tiled=True).astype(F32)
+    flat = expand(dilated_kernel, dilated_prune_mask).reshape(units, kernel_taps * out_local, channels)
     saved = []
     for unit in range(units):
         first = first_of(hidden, unit)

time: 275 us -> 261 us (0.949)
  matrix products: 21.2 us -> 11.1 us
  other arithmetic: 18 us -> 13.9 us
    pallas_call x7 -> x8, Pallas kernels: 149 us -> 164 us  [together(): pl.pallas_call(kernel, out_shape=[task[1] for task in tasks], in_specs=[w...]
    pallas_call x2 -> x1, Pallas kernels: 25.1 us -> 12.8 us  [run(): pl.pallas_call(kernel, out_shape=jax.ShapeDtypeStruct(out_shape, dtype),...]
    unnamed x52 -> x88, local copies, waits for them, and re-layouts: 6.6 us -> 16 us
    convert_element_type x6 -> x4, other arithmetic: 6.7 us -> 0.28 us  [the longest x1 0.13 us: per_device(): partial = partial.astype(BF16).reshape(rows * tm_count, out_local)]
    mul x1 -> x0, local copies, waits for them, and re-layouts: 5.94 us -> none  [expand(): return (kernel.reshape(-1, width) * keep.astype(BF16)).reshape(kernel.shape)]
    reshape x1 -> x0, local copies, waits for them, and re-layouts: 5.94 us -> none  [expand(): return (kernel.reshape(-1, width) * keep.astype(BF16)).reshape(kernel.shape)]
    dot_general x2 -> x1, matrix products: 6.41 us -> 1.36 us  [expand(): jnp.dot(mask.reshape(-1, blocks).astype(BF16), spread, preferred_element_...]
    dot_general x5 -> x3, matrix products: 8.92 us -> 4.26 us  [dot_last(): lax.dot_general(left, right, (((1,), (1,)), ((), ())), preferred_element_...]
  transfers between devices with their start and end apart: 1 -> 1, of which waited for: 0 -> 0; matrix products, arithmetic and copies ran while one was open for 13% -> 6% of each run, Pallas kernels for 33% -> 40%
where the time goes in v3:
time: 261 us; the launch traced here: 260 us
  Pallas kernels  202 us (77%)
  local copies, waits for them, and re-layouts  18.7 us (7%)
  between operations  14.9 us (6%)
  other arithmetic  13.9 us (5%)
  matrix products  11.1 us (4%)
    pallas_call x8, Pallas kernels, together(): pl.pallas_call(kernel, out_shape=[task[1] for task in tasks], in_specs=[w...  164 us
    pallas_call x1, Pallas kernels, saliency(): pl.pallas_call(functools.partial(saliency_kernel, spacings, taps), out_sh...  19.4 us
    unnamed x88, local copies, waits for them, and re-layouts  16 us
    pallas_call x1, Pallas kernels, run(): pl.pallas_call(kernel, out_shape=jax.ShapeDtypeStruct(out_shape, dtype),...  12.8 us
    pallas_call x2, Pallas kernels, taps_call(): pl.pallas_call(functools.partial(taps_kernel, halo, spacing, taps), out_s...  5.61 us
  transfers between devices with their start and end apart: 1, of which 0 were waited for; matrix products, arithmetic and copies ran while one was open for 6% of the time, Pallas kernels for 40%

profile of v3, /device:TPU:0, one launch (start us, length us, event | category | flops | bytes accessed | tf_op | source)
XLA Modules:
  0.0 260.2 jit_solution(4660910567392785828)
XLA Ops:
  7.2 1.1 convert_element_type.306
  8.3 1.4 fusion.2
  9.7 0.8 copy-done.19
  10.5 1.6 convolution_convert_fusion.2
  12.2 0.6 add_select_fusion.4
  12.8 0.6 add_select_fusion.3
  13.5 0.6 add_select_fusion.2
  14.1 0.6 add_select_fusion.1
  14.8 0.5 multiply_bitcast_fusion.1
  15.3 0.5 multiply_bitcast_fusion
  16.4 12.8 %shard_map.130 = bf16[320,512]{1,0:T(8,128)(2,1)S(1)} custom-call(bf16[80,256]{1,0:T(8,128)(2,1)S(1)} %fusion.31.x_ref), custom_call_target="tpu_custom_call" | custom-call | tf_op jit(solution)/shard_map/pallas_call | solution.py:530
  29.3 0.9 fusion.7
  30.7 0.4 copy.33
  31.2 0.7 copy-done.15
  31.9 14.5 %shard_map.131 = (f32[640,128]{1,0:T(8,128)S(1)}, bf16[1792,1024]{1,0:T(8,128)(2,1)S(1)}) custom-call(bf16[2560,128]{1,0:T(8,128)(2,1)S(1)} %bitcast.59, bf16[1792,1024]{1,0:T(8,128)(2,1)} %bitcast.65, s32[1792,128]{1,0:T(8,128)S(1)} %bitcast.60), custom_call_target="tpu_custom_call" | custom-call | tf_op jit(solution)/shard_map/pallas_call | solution.py:303
  46.5 1.1 add_convert_fusion.1.refs_0_
  47.6 25.2 %shard_map.132.x_ref.refs_1_ = bf16[672,1024]{1,0:T(8,128)(2,1)S(1)} custom-call(bf16[640,128]{1,0:T(8,128)(2,1)S(1)} %add_convert_fusion.1.refs_0_), custom_call_target="tpu_custom_call" | custom-call | tf_op jit(solution)/shard_map/pallas_call | solution.py:303
  72.8 1.6 fusion.102
  74.6 2.8 %shard_map.133 = (f32[640,128]{1,0:T(8,128)S(1)}, bf16[640,128]{1,0:T(8,128)(2,1)S(1)}) custom-call(bf16[672,1024]{1,0:T(8,128)(2,1)S(1)} %shard_map.132.x_ref.refs_1_, bf16[896,1024]{1,0:T(8,128)(2,1)S(1)} %get-tuple-element.70.w_ref, f32[672,128]{1,0:T(8,128)S(1)} %broadcast_in_dim.299.ids_ref, f32[1,128]{1,0:T(1,128)S(1)} %get-tuple-element.94.alpha_ref), custom_call_target="tpu_custom_call" | custom-call | tf_op jit(solution)/shard_map/pallas_call | solution.py:339
  77.4 0.7 copy-done.16
  78.1 20.6 %shard_map.134 = (bf16[640,1024]{1,0:T(8,128)(2,1)S(1)}, bf16[2560,512]{1,0:T(8,128)(2,1)S(1)}) custom-call(bf16[640,128]{1,0:T(8,128)(2,1)S(1)} %get-tuple-element.23.refs_0_, bf16[672,1024]{1,0:T(8,128)(2,1)S(1)} %shard_map.132.x_ref.refs_1_), custom_call_target="tpu_custom_call" | custom-call | tf_op jit(solution)/shard_map/pallas_call | solution.py:303
  98.7 1.1 copy-done.13
  99.8 2.2 add_convert_fusion
  102.0 0.6 add_select_fusion
  102.6 1.7 copy.26
  104.3 1.0 copy-done.18
  105.4 24.7 %shard_map.135 = (bf16[704,1024]{1,0:T(8,128)(2,1)S(1)}, bf16[2560,512]{1,0:T(8,128)(2,1)S(1)}) custom-call(bf16[640,128]{1,0:T(8,128)(2,1)S(1)} %copy-done.18, bf16[672,1024]{1,0:T(8,128)(2,1)S(1)} %shard_map.132.x_ref.refs_1_), custom_call_target="tpu_custom_call" | custom-call | tf_op jit(solution)/shard_map/pallas_call | solution.py:303
  130.1 1.5 copy-done.10
  131.8 2.8 %shard_map.136 = (f32[640,128]{1,0:T(8,128)S(1)}, bf16[640,128]{1,0:T(8,128)(2,1)S(1)}) custom-call(bf16[704,1024]{1,0:T(8,128)(2,1)S(1)} %get-tuple-element.25.x_ref.refs_2_, bf16[896,1024]{1,0:T(8,128)(2,1)S(1)} %copy-done.6, f32[704,128]{1,0:T(8,128)S(1)} %broadcast_in_dim.301.ids_ref, f32[1,128]{1,0:T(1,128)S(1)} %get-tuple-element.93.alpha_ref), custom_call_target="tpu_custom_call" | custom-call | tf_op jit(solution)/shard_map/pallas_call | solution.py:339
  135.8 1.1 copy.31
  136.9 1.3 multiply_convert_fusion.1.refs_0_
  138.2 17.0 %shard_map.137 = (bf16[2560,128]{1,0:T(8,128)(2,1)S(1)}, bf16[640,1024]{1,0:T(8,128)(2,1)S(1)}) custom-call(bf16[640,128]{1,0:T(8,128)(2,1)S(1)} %multiply_convert_fusion.1.refs_0_, bf16[640,128]{1,0:T(8,128)(2,1)S(1)} %get-tuple-element.27.refs_1_), custom_call_target="tpu_custom_call" | custom-call | tf_op jit(solution)/shard_map/pallas_call | solution.py:303
  155.6 1.2 fusion.5
  158.1 1.2 copy-done.2
  159.2 1.5 convolution_convert_fusion.1.refs_0_
  160.8 27.7 %shard_map.138 = (f32[640,128]{1,0:T(8,128)S(1)}, bf16[128,1024]{1,0:T(8,128)(2,1)S(1)}, bf16[2560,512]{1,0:T(8,128)(2,1)S(1)}) custom-call(bf16[640,1024]{1,0:T(8,128)(2,1)S(1)} %convolution_convert_fusion.1.refs_0_, bf16[128,1024]{1,0:T(8,128)(2,1)S(1)} %fusion.3.refs_1_, bf16[704,1024]{1,0:T(8,128)(2,1)S(1)} %copy-done.4), custom_call_target="tpu_custom_call" | custom-call | tf_op jit(solution)/shard_map/pallas_call | solution.py:303
  188.5 1.1 fusion.6
  189.6 0.4 convolution_convert_fusion.5.refs_1_
  190.0 1.6 convolution_convert_fusion.refs_0_
  191.6 1.7 copy.28
  193.3 1.4 copy-done.5
  194.7 1.3 copy-done.7
  196.0 23.3 %shard_map.139 = (f32[640,128]{1,0:T(8,128)S(1)}, bf16[128,1024]{1,0:T(8,128)(2,1)S(1)}, bf16[2560,512]{1,0:T(8,128)(2,1)S(1)}) custom-call(bf16[640,1024]{1,0:T(8,128)(2,1)S(1)} %copy-done.7, bf16[128,1024]{1,0:T(8,128)(2,1)S(1)} %convolution_convert_fusion.5.refs_1_, bf16[704,1024]{1,0:T(8,128)(2,1)S(1)} %copy-done.5), custom_call_target="tpu_custom_call" | custom-call | tf_op jit(solution)/shard_map/pallas_call | solution.py:303
  219.3 1.5 copy-done.12
  220.9 1.1 multiply_convert_fusion.refs_0_
  222.0 10.7 %shard_map.140.refs_0_ = bf16[2560,128]{1,0:T(8,128)(2,1)S(1)} custom-call(bf16[640,128]{1,0:T(8,128)(2,1)S(1)} %multiply_convert_fusion.refs_0_), custom_call_target="tpu_custom_call" | custom-call | tf_op jit(solution)/shard_map/pallas_call | solution.py:303
  232.7 1.1 convert_multiply_fusion
  233.9 19.4 %shard_map.141 = f32[2,896,1024]{2,1,0:T(8,128)} custom-call(f32[14,2560]{1,0:T(8,128)S(1)} %stack.8.mask_ref, bf16[2560,128]{1,0:T(8,128)(2,1)S(1)} %shard_map.140.refs_0_, bf16[2560,128]{1,0:T(8,128)(2,1)S(1)} %get-tuple-element.29.refs_1_, bf16[2,896,1024]{2,1,0:T(8,128)(2,1)} %bitcast.58, bf16[2560,512]{1,0:T(8,128)(2,1)S(1)} %copy-done.9, ...), custom_call_target="tpu_custom_call" | custom-call | tf_op jit(solution)/shard_map/pallas_call | solution.py:418
  (126 shorter events, 4.3 us)
Async XLA Ops:
  7.2 22.1 %copy-start = (bf16[16,128,512]{2,1,0:T(8,128)(2,1)S(1)}, bf16[16,128,512]{2,1,0:T(8,128)(2,1)}, u32[]{:S(2)}) copy-start(bf16[16,128,512]{2,1,0:T(8,128)(2,1)} %param.12) | copy-start | bytes 6291460
  7.2 3.3 %copy-start.23 = (bf16[128,640]{1,0:T(8,128)(2,1)S(1)}, bf16[128,640]{1,0:T(8,128)(2,1)}, u32[]{:S(2)}) copy-start(bf16[128,640]{1,0:T(8,128)(2,1)} %param.21) | copy-start | bytes 491524
  7.2 128.6 %reduce-scatter.4.cloned.1.call-start = ((), (), s32[]{:S(2)}) async-start(), calls=%async_computation.1 | async-start | bytes 1474560
  9.7 0.8 copy-start.19
  10.5 4.2 %copy-start.41 = (s32[3]{0:T(128)S(1)}, s32[3]{0:T(128)}, u32[]{:S(2)}) copy-start(s32[3]{0:T(128)} %param.20) | copy-start | bytes 40
  10.5 4.4 %copy-start.39 = (f32[2,128]{1,0:T(2,128)S(1)}, f32[2,128]{1,0:T(2,128)}, u32[]{:S(2)}) copy-start(f32[2,128]{1,0:T(2,128)} %param.18) | copy-start | bytes 3076
  10.5 4.8 %copy-start.38 = (f32[2,128]{1,0:T(2,128)S(1)}, f32[2,128]{1,0:T(2,128)}, u32[]{:S(2)}) copy-start(f32[2,128]{1,0:T(2,128)} %param.19) | copy-start | bytes 3076
  10.5 5.6 %copy-start.32 = (bf16[256,80]{0,1:T(8,128)(2,1)S(1)}, bf16[256,80]{0,1:T(8,128)(2,1)}, u32[]{:S(2)}) copy-start(bf16[256,80]{0,1:T(8,128)(2,1)} %param.11) | copy-start | bytes 122884
  10.5 5.6 %copy-start.40 = (f32[256]{0:T(256)S(1)}, f32[256]{0:T(256)}, u32[]{:S(2)}) copy-start(f32[256]{0:T(256)} %param.17) | copy-start | bytes 3076
  14.8 15.4 %copy-start.33 = (s32[3]{0:T(128)}, s32[3]{0:T(128)S(1)}, u32[]{:S(2)}) copy-start(s32[3]{0:T(128)S(1)} %bitcast_subtract_fusion) | copy-start | bytes 40
  30.7 1.2 copy-start.15
  46.5 28.0 %copy-start.1 = (bf16[1792,1024]{1,0:T(8,128)(2,1)}, bf16[1792,1024]{1,0:T(8,128)(2,1)S(1)}, u32[]{:S(2)}) copy-start(bf16[1792,1024]{1,0:T(8,128)(2,1)S(1)} %get-tuple-element.22) | copy-start | bytes 11010052
  77.3 0.7 copy-start.16
  78.1 21.7 %copy-start.20 = (bf16[256,1024]{1,0:T(8,128)(2,1)S(1)}, bf16[256,1024]{1,0:T(8,128)(2,1)}, u32[]{:S(2)}) copy-start(bf16[256,1024]{1,0:T(8,128)(2,1)} %copy-done.19) | copy-start | bytes 1572868
  98.7 1.1 copy-start.13
  98.7 3.3 %copy-start.8 = (bf16[2560,512]{1,0:T(8,128)(2,1)}, bf16[2560,512]{1,0:T(8,128)(2,1)S(1)}, u32[]{:S(2)}) copy-start(bf16[2560,512]{1,0:T(8,128)(2,1)S(1)} %get-tuple-element.33.refs_3_) | copy-start | bytes 7864324
  104.3 27.4 %copy-start.6 = (bf16[896,1024]{1,0:T(8,128)(2,1)S(1)}, bf16[896,1024]{1,0:T(8,128)(2,1)}, u32[]{:S(2)}) copy-start(bf16[896,1024]{1,0:T(8,128)(2,1)} %get-tuple-element.69.w_ref) | copy-start | bytes 5505028
  104.3 1.1 copy-start.18
  130.0 1.5 copy-start.10
  131.5 3.1 %copy-start.3 = (bf16[704,1024]{1,0:T(8,128)(2,1)}, bf16[704,1024]{1,0:T(8,128)(2,1)S(1)}, u32[]{:S(2)}) copy-start(bf16[704,1024]{1,0:T(8,128)(2,1)S(1)} %get-tuple-element.25.x_ref.refs_2_) | copy-start | bytes 4325380
  131.7 2.9 %copy-start.27 = (s32[2560]{0:T(1024)S(1)}, s32[2560]{0:T(1024)}, u32[]{:S(2)}) copy-start(s32[2560]{0:T(1024)} %add_select_fusion.4) | copy-start | bytes 30724
  131.7 2.9 %copy-start.28 = (s32[2560]{0:T(1024)S(1)}, s32[2560]{0:T(1024)}, u32[]{:S(2)}) copy-start(s32[2560]{0:T(1024)} %add_select_fusion.3) | copy-start | bytes 30724
  131.7 2.9 %copy-start.29 = (s32[2560]{0:T(1024)S(1)}, s32[2560]{0:T(1024)}, u32[]{:S(2)}) copy-start(s32[2560]{0:T(1024)} %add_select_fusion.2) | copy-start | bytes 30724
  131.7 2.9 %copy-start.30 = (s32[2560]{0:T(1024)S(1)}, s32[2560]{0:T(1024)}, u32[]{:S(2)}) copy-start(s32[2560]{0:T(1024)} %add_select_fusion.1) | copy-start | bytes 30724
  131.7 2.9 %copy-start.31 = (s32[2560]{0:T(1024)S(1)}, s32[2560]{0:T(1024)}, u32[]{:S(2)}) copy-start(s32[2560]{0:T(1024)} %add_select_fusion) | copy-start | bytes 30724
  131.8 2.9 %copy-start.34 = (s32[3]{0:T(128)S(1)}, s32[3]{0:T(128)}, u32[]{:S(2)}) copy-start(s32[3]{0:T(128)} %copy-done.33) | copy-start | bytes 40
  134.7 2.2 copy-start.37
  134.7 20.6 %copy-start.24 = (bf16[128,640]{1,0:T(8,128)(2,1)S(1)}, bf16[128,640]{1,0:T(8,128)(2,1)}, u32[]{:S(2)}) copy-start(bf16[128,640]{1,0:T(8,128)(2,1)} %param.21) | copy-start | bytes 491524
  136.9 18.8 %copy-start.21 = (bf16[256,1024]{1,0:T(8,128)(2,1)S(1)}, bf16[256,1024]{1,0:T(8,128)(2,1)}, u32[]{:S(2)}) copy-start(bf16[256,1024]{1,0:T(8,128)(2,1)} %copy-done.19) | copy-start | bytes 1572868
  136.9 18.7 %copy-start.25 = (f32[640,128]{1,0:T(8,128)S(1)}, f32[640,128]{1,0:T(8,128)}, u32[]{:S(2)}) copy-start(f32[640,128]{1,0:T(8,128)} %get-tuple-element.99) | copy-start | bytes 983044
  157.2 2.0 copy-start.2
  159.2 1.5 copy-start.4
  160.8 27.7 %copy-start.26 = (bf16[128,640]{0,1:T(8,128)(2,1)S(1)}, bf16[128,640]{0,1:T(8,128)(2,1)}, u32[]{:S(2)}) copy-start(bf16[128,640]{0,1:T(8,128)(2,1)} %copy.26) | copy-start | bytes 491524
  160.8 27.7 %copy-start.35 = (f32[128]{0:T(128)S(1)}, f32[128]{0:T(128)}, u32[]{:S(2)}) copy-start(f32[128]{0:T(128)} %get-tuple-element.95) | copy-start | bytes 1540
  160.8 28.8 %copy-start.14 = (bf16[640,1024]{1,0:T(8,128)(2,1)S(1)}, bf16[640,1024]{1,0:T(8,128)(2,1)}, u32[]{:S(2)}) copy-start(bf16[640,1024]{1,0:T(8,128)(2,1)} %copy-done.13) | copy-start | bytes 3932164
  188.5 1.6 copy-start.11
  193.3 1.4 copy-start.5
  194.7 1.3 copy-start.7
  196.0 24.9 %copy-start.17 = (f32[640,128]{1,0:T(8,128)S(1)}, f32[640,128]{1,0:T(8,128)}, u32[]{:S(2)}) copy-start(f32[640,128]{1,0:T(8,128)} %copy-done.16) | copy-start | bytes 983044
  196.0 24.9 %copy-start.36 = (f32[128]{0:T(128)S(1)}, f32[128]{0:T(128)}, u32[]{:S(2)}) copy-start(f32[128]{0:T(128)} %get-tuple-element.91) | copy-start | bytes 1540
  219.3 1.6 copy-start.12
  220.9 11.8 %copy-start.22 = (bf16[256,1024]{1,0:T(8,128)(2,1)S(1)}, bf16[256,1024]{1,0:T(8,128)(2,1)}, u32[]{:S(2)}) copy-start(bf16[256,1024]{1,0:T(8,128)(2,1)} %copy-done.19) | copy-start | bytes 1572868
  222.0 11.9 %copy-start.9 = (bf16[2560,512]{1,0:T(8,128)(2,1)S(1)}, bf16[2560,512]{1,0:T(8,128)(2,1)}, u32[]{:S(2)}) copy-start(bf16[2560,512]{1,0:T(8,128)(2,1)} %copy-done.8) | copy-start | bytes 7864324
Sparse Core Ops, SparseCore 0:
  12.3 37.8 reduce-scatter.3

commit v4 on v3

--- a/solution.py
+++ b/solution.py
@@ -61,19 +61,20 @@
             copy.start()
             started.append(copy)
 
-        for part, (span, source, to, steps) in enumerate(parts):
+        for part, (span, source, to, steps) in reversed(list(enumerate(parts))):
             for step in steps:
                 begin(remote(source, o_ref.at[span, mine], send.at[part, step], recv.at[part, step], (to, at(step))))
         begin(remote(x_ref, o_ref.at[parts[0][0], mine], fsend.at[0, 0], frecv.at[0, 0], partner))
         yield
         o_ref[parts[0][0], mine] = x_ref[...]
-        for step in range(chips):
-            for part, (span, source, to, steps) in enumerate(parts):
-                if step in steps:
-                    slot = o_ref.at[span, column(at(-step), width)]
-                    remote(slot, slot, send.at[part, step], recv.at[part, step], partner).wait_recv()
-                    begin(remote(slot, slot, fsend.at[part, step], frecv.at[part, step], partner))
         yield
+        for part, (span, source, to, steps) in enumerate(parts):
+            for step in steps:
+                slot = o_ref.at[span, column(at(-step), width)]
+                remote(slot, slot, send.at[part, step], recv.at[part, step], partner).wait_recv()
+                begin(remote(slot, slot, fsend.at[part, step], frecv.at[part, step], partner))
+                if part == 0:
+                    yield
         for part, (span, source, to, steps) in enumerate(parts):
             for step in range(chips):
                 slot = o_ref.at[span, column(at(-step) + other, width)]
@@ -106,6 +107,7 @@
         copy = remote(summed.at[step], landed.at[step], send.at[step], recv.at[step], (tm, at(step)))
         copy.start()
         started.append(copy)
+        yield
     pairs[0].wait_recv()
     o_ref[...] = x_ref[:, column(chan, width)].astype(F32) + pair[0].astype(F32)
     yield
@@ -136,13 +138,14 @@
             started.append(copy)
         yield
         o_ref[pl.ds(pl.multiple_of(tm * rows, rows), rows), :] = x_ref[own, pl.ds(base, 2 * width)]
+        yield
         for step in range(1, count):
             landing = slot((tm + count - step) % count, core)
             remote(landing, landing, send.at[step], recv.at[step], partner).wait_recv()
             copy = remote(landing, landing, fsend.at[step], frecv.at[step], partner)
             copy.start()
             started.append(copy)
-        yield
+            yield
         for step in range(1, count):
             landing = slot((tm + count - step) % count, 1 - core)
             remote(landing, landing, send.at[step], frecv.at[step], partner).wait_recv()
@@ -167,7 +170,8 @@
         started.append(copy)
     yield
     o_ref[pl.ds(pl.multiple_of(tm * rows, rows), rows)] = x_ref[...]
-    yield
+    for turns in range(4):
+        yield
     for step in range(1, count):
         landing = slot((tm + count - step) % count)
         remote(landing, landing, send.at[step], recv.at[step], (tm, chan)).wait_recv()
@@ -197,6 +201,8 @@
         copy.start()
         started.append(copy)
     yield
+    yield
+    yield
     for step in range(1, count):
         landing = o_ref.at[:, column((tm + count - step) % count, width)]
         remote(landing, landing, send.at[step], grecv.at[step], (tm, chan)).wait_recv()
@@ -249,7 +255,8 @@
 
 
 def expand_body(kernel_ref, mask_ref, o_ref):
-    yield
+    for turns in range(5):
+        yield
     rows, width = kernel_ref.shape
     blocks = mask_ref.shape[1]
     spread = (
@@ -295,9 +302,8 @@
             used = refs[taken : taken + len(task[0])] + (refs[out],) + refs[place : place + len(task[2])]
             taken, out, place = taken + len(task[0]), out + 1, place + len(task[2])
             bodies.append(task[3](*used))
-        for phase in range(3):
-            for body in bodies:
-                next(body, None)
+        while bodies:
+            bodies = [body for body in bodies if next(body, body) is not body]
 
     whole = pl.BlockSpec(memory_space=pltpu.VMEM)
     return pl.pallas_call(
@@ -346,91 +352,106 @@
     )(wide, weights, ids, alpha)
 
 
-def saliency_kernel(spacings, taps, mask_ref, *refs):
-    units = len(spacings)
-    grads, eff_ref, firsts = refs[:units], refs[units], refs[units + 1 : 3 * units + 1]
-    o_ref, flipped, turned, eff, first, made, loads, stores = refs[3 * units + 1 :]
-    rows, width = grads[0].shape
-    order = list(reversed(range(units)))
-    span = firsts[0].shape[1]
-    copies = {}
-    for unit in order:
-        copies[unit] = [
-            pltpu.make_async_copy(
-                firsts[2 * unit + half], first.at[unit, :, pl.ds(half * span, span)], loads.at[unit, half]
-            )
-            for half in range(2)
-        ] + [pltpu.make_async_copy(eff_ref.at[unit], eff.at[unit], loads.at[unit, 2])]
-        for copy in copies[unit]:
-            copy.start()
-    chunk, lines, step = 512, 16, 256
+def tap_windows(spacing, taps, grad_ref, mask_ref, flipped, turned):
+    rows, width = grad_ref.shape
+    chunk, lines = 512, 16
+
+    @pl.loop(0, rows // chunk)
+    def _(block):
+        part = pl.ds(pl.multiple_of(block * chunk, chunk), chunk)
+        flipped[:, part] = grad_ref[part].astype(F32).T
+
+    @pl.loop(0, width // lines)
+    def _(block):
+        values = flipped[pl.ds(pl.multiple_of(block * lines, lines), lines)]
+        for tap in range(taps):
+            shift = ((tap - taps // 2) * spacing) % rows
+            moved = pltpu.roll(values, shift, 1) if shift else values
+            line = pl.multiple_of(tap * width + block * lines, lines)
+            turned[pl.ds(line, lines)] = (moved * mask_ref[pl.ds(tap, 1)]).astype(turned.dtype)
+
+
+def saliency_task(spacing, taps, masks, grads, eff, firsts):
+    rows, width = grads.shape
+
+    def body(grad_ref, mask_ref, eff_ref, left_ref, right_ref, o_ref, flipped, turned):
+        yield
+        tap_windows(spacing, taps, grad_ref, mask_ref, flipped, turned)
+        span, step = left_ref.shape[1], 256
+        for half, source in enumerate((left_ref, right_ref)):
+
+            @pl.loop(0, span // step)
+            def _(block):
+                inner = pl.ds(pl.multiple_of(block * step, step), step)
+                outer = pl.ds(pl.multiple_of(half * span + block * step, step), step)
+                grad = jnp.dot(turned[...], source[:, inner], preferred_element_type=F32)
+                o_ref[:, outer] = eff_ref[:, outer].astype(F32) * grad
+
+    scratch = [pltpu.VMEM((width, rows), F32), pltpu.VMEM((taps * width, rows), BF16)]
+    return (grads, masks, eff, *firsts), jax.ShapeDtypeStruct(eff.shape, F32), scratch, body, ()
+
+
+def saliency_kernel(
+    spacing, taps, mask_ref, grad_ref, eff_ref, left_ref, right_ref, last_ref, o_ref,
+    flipped, turned, eff, first, made, loads, stores, whole_store,
+):
+    span, step = left_ref.shape[1], 256
     blocks = 2 * span // step
-    for place, unit in enumerate(order):
-
-        @pl.loop(0, rows // chunk)
-        def _(block):
-            part = pl.ds(pl.multiple_of(block * chunk, chunk), chunk)
-            flipped[:, part] = grads[unit][part].astype(F32).T
-
-        @pl.loop(0, width // lines)
-        def _(block):
-            values = flipped[pl.ds(pl.multiple_of(block * lines, lines), lines)]
-            for tap in range(taps):
-                shift = ((tap - taps // 2) * spacings[unit]) % rows
-                moved = pltpu.roll(values, shift, 1) if shift else values
-                kept = moved * mask_ref[pl.ds(unit * taps + tap, 1)]
-                line = pl.multiple_of(tap * width + block * lines, lines)
-                turned[pl.ds(line, lines)] = kept.astype(turned.dtype)
-
-        for copy in copies[unit]:
-            copy.wait()
-
-        def store(slot, block):
-            outer = pl.ds(pl.multiple_of(block * step, step), step)
-            return pltpu.make_async_copy(made.at[slot], o_ref.at[unit, :, outer], stores.at[slot])
-
-        @pl.loop(0, blocks)
-        def _(block):
-            slot = block % 2
-            outer = pl.ds(pl.multiple_of(block * step, step), step)
-            grad = jnp.dot(turned[...], first[unit, :, outer], preferred_element_type=F32)
-            if place:
-                store(slot, block).wait()
-            else:
-
-                @pl.when(block >= 2)
-                def _():
-                    store(slot, block).wait()
-
-            made[slot] = eff[unit, :, outer].astype(F32) * grad
-            store(slot, block).start()
-
-        if place == units - 1:
-            for slot in range(2):
-                store(slot, slot).wait()
-
-
-def saliency(spacings, taps, masks, eff, grads, firsts):
+    copies = [
+        pltpu.make_async_copy(left_ref, first.at[:, pl.ds(0, span)], loads.at[0]),
+        pltpu.make_async_copy(right_ref, first.at[:, pl.ds(span, span)], loads.at[1]),
+        pltpu.make_async_copy(eff_ref, eff, loads.at[2]),
+    ]
+    last = pltpu.make_async_copy(last_ref, o_ref.at[1], whole_store.at[0])
+    for copy in copies:
+        copy.start()
+    last.start()
+    tap_windows(spacing, taps, grad_ref, mask_ref, flipped, turned)
+    for copy in copies:
+        copy.wait()
+
+    def store(slot, block):
+        outer = pl.ds(pl.multiple_of(block * step, step), step)
+        return pltpu.make_async_copy(made.at[slot], o_ref.at[0, :, outer], stores.at[slot])
+
+    @pl.loop(0, blocks)
+    def _(block):
+        slot = block % 2
+        outer = pl.ds(pl.multiple_of(block * step, step), step)
+        grad = jnp.dot(turned[...], first[:, outer], preferred_element_type=F32)
+
+        @pl.when(block >= 2)
+        def _():
+            store(slot, block).wait()
+
+        made[slot] = eff[:, outer].astype(F32) * grad
+        store(slot, block).start()
+
+    for slot in range(2):
+        store(slot, slot).wait()
+    last.wait()
+
+
+def saliency(spacing, taps, masks, eff, grads, firsts, last):
     whole, anywhere = pl.BlockSpec(memory_space=pltpu.VMEM), pl.BlockSpec(memory_space=pl.ANY)
-    units = len(spacings)
-    rows, width = grads[0].shape
-    operands = [masks] + grads + [eff] + firsts
+    rows, width = grads.shape
     return pl.pallas_call(
-        functools.partial(saliency_kernel, spacings, taps),
-        out_shape=jax.ShapeDtypeStruct(eff.shape, F32),
-        in_specs=[whole] * (1 + units) + [anywhere] * (1 + 2 * units),
+        functools.partial(saliency_kernel, spacing, taps),
+        out_shape=jax.ShapeDtypeStruct((2,) + eff.shape, F32),
+        in_specs=[whole] * 2 + [anywhere] * 4,
         out_specs=anywhere,
         scratch_shapes=[
             pltpu.VMEM((width, rows), F32),
             pltpu.VMEM((taps * width, rows), BF16),
             pltpu.VMEM(eff.shape, BF16),
-            pltpu.VMEM((units, rows, eff.shape[2]), BF16),
-            pltpu.VMEM((2, eff.shape[1], 256), F32),
-            DMA((units, 3)),
+            pltpu.VMEM((rows, eff.shape[1]), BF16),
+            pltpu.VMEM((2, eff.shape[0], 256), F32),
+            DMA((3,)),
             DMA((2,)),
+            DMA((1,)),
         ],
         compiler_params=pltpu.CompilerParams(vmem_limit_bytes=VMEM_LIMIT),
-    )(*operands)
+    )(masks, grads, eff, *firsts, last)
 
 
 def frames_scatter_body(x_ref, o_ref, landed, send, recv):
@@ -451,7 +472,8 @@
         started.append(copy)
     yield
     o_ref[...] = x_ref[pl.ds(pl.multiple_of(tm * rows, rows), rows)].astype(F32)
-    yield
+    for turns in range(4):
+        yield
     for step in range(1, count):
         started[step - 1].wait_recv()
         o_ref[...] += landed[step].astype(F32)
@@ -640,12 +662,7 @@
 
     act = snake_act(latent_input.astype(F32), snake_freq_upsample[:, None]).astype(BF16).T
     cot = cotangent.T
-    grad_second_last = lax.psum_scatter(
-        jnp.dot(cot, point_eff[units - 1], preferred_element_type=F32).astype(BF16),
-        "chan",
-        scatter_dimension=1,
-        tiled=True,
-    ).astype(F32)
+    last_parts = jnp.dot(cot, point_eff[units - 1], preferred_element_type=F32).astype(BF16)
 
     act_all = turn(act, 0)
     product = dot_last(act_all, upsample_kernel.reshape(taps * out_local, in_local)).reshape(
@@ -704,13 +721,14 @@
 
     if fast:
         halos = [-(-margin // 16) * 16 for margin in reach]
-        hidden, flat = together(
+        flat, grad_second_last, hidden = together(
             1,
-            frames_scatter(partial),
             expand_task(
                 dilated_kernel.reshape(-1, channels),
                 dilated_prune_mask.reshape(-1, dilated_prune_mask.shape[-1]),
             ),
+            chan_scatter(last_parts),
+            frames_scatter(partial),
         )
         flat = flat.reshape(units, kernel_taps * out_local, channels)
 
@@ -750,18 +768,22 @@
             frames_reduce(dot_first(grad_b0, second0).astype(BF16)),
             share(wide1, halos[1], 1, 2),
         )
-        (grads0,) = together(8, frames_gather(grad_conv_of(grad_second0, conv0, 0)))
         all_pos = jnp.arange(rows * tm_count, dtype=jnp.int32)
-        masks = jnp.stack(
-            [
-                tap_mask(all_pos, -(tap - kernel_taps // 2) * spacing)[:, 0].astype(F32)
-                for spacing in spacings
-                for tap in range(kernel_taps)
-            ]
-        )
-        dil = saliency(
-            spacings, kernel_taps, masks, flat, [grads0, grads1], [frames00, frames01, frames10, frames11]
-        )
+        masks = [
+            jnp.stack(
+                [
+                    tap_mask(all_pos, -(tap - kernel_taps // 2) * spacing)[:, 0].astype(F32)
+                    for tap in range(kernel_taps)
+                ]
+            )
+            for spacing in spacings
+        ]
+        grads0, last = together(
+            8,
+            frames_gather(grad_conv_of(grad_second0, conv0, 0)),
+            saliency_task(spacings[1], kernel_taps, masks[1], grads1, flat[1], [frames10, frames11]),
+        )
+        dil = saliency(spacings[0], kernel_taps, masks[0], flat[0], grads0, [frames00, frames01], last)
         return outputs(decoded, dil, jnp.stack([points0, points1]))
 
     hidden = lax.psum_scatter(partial, "tm", scatter_dimension=0, tiled=True).astype(F32)
@@ -780,7 +802,7 @@
         hidden_in, first_own, conv, second = saved[unit]
         grad_b = grad_out.astype(BF16)
         if unit == units - 1:
-            grad_second = grad_second_last
+            grad_second = lax.psum_scatter(last_parts, "chan", scatter_dimension=1, tiled=True).astype(F32)
         else:
             grad_second = lax.psum_scatter(
                 spread_back(grad_b, unit), "chan", scatter_dimension=1, tiled=True

time: 261 us -> 341 us (1.31)
  Pallas kernels: 202 us -> 308 us
  between operations: 14.9 us -> 1.46 us
  local copies, waits for them, and re-layouts: 18.7 us -> 13 us
  matrix products: 11.1 us -> 7.16 us
    pallas_call x1, Pallas kernels: 19.4 us -> 113 us  [saliency(): pl.pallas_call(functools.partial(saliency_kernel, spacing, taps), out_sha...]
    pallas_call x8, Pallas kernels: 164 us -> 178 us  [together(): pl.pallas_call(kernel, out_shape=[task[1] for task in tasks], in_specs=[w...]
    unnamed x88 -> x57, local copies, waits for them, and re-layouts: 16 us -> 9.51 us
  transfers between devices with their start and end apart: 1 -> 0, of which waited for: 0 -> 0; matrix products, arithmetic and copies ran while one was open for 6% -> 0% of each run, Pallas kernels for 40% -> 0%
where the time goes in v4:
time: 341 us
  Pallas kernels  308 us (90%)
  local copies, waits for them, and re-layouts  13 us (4%)
  other arithmetic  11.6 us (3%)
  matrix products  7.16 us (2%)
    pallas_call x8, Pallas kernels, together(): pl.pallas_call(kernel, out_shape=[task[1] for task in tasks], in_specs=[w...  178 us
    pallas_call x1, Pallas kernels, saliency(): pl.pallas_call(functools.partial(saliency_kernel, spacing, taps), out_sha...  113 us
    pallas_call x1, Pallas kernels, run(): pl.pallas_call(kernel, out_shape=jax.ShapeDtypeStruct(out_shape, dtype),...  11.2 us
    unnamed x57, local copies, waits for them, and re-layouts  9.51 us

profile of v4, /device:TPU:0, one launch (start us, length us, event | category | flops | bytes accessed | tf_op | source)
XLA Modules:
  0.0 340.9 jit_solution(10669627888394635989)
XLA Ops:
  0.7 1.0 reduce-window.9
  1.7 0.7 bitcast_subtract_fusion
  2.3 0.8 multiply_bitcast_fusion.1
  3.1 0.8 multiply_bitcast_fusion
  4.6 0.4 convert_reduce_fusion
  5.5 0.3 fusion.32.x_ref
  5.8 0.8 copy.21
  6.6 11.2 %shard_map.130 = bf16[320,512]{1,0:T(8,128)(2,1)S(1)} custom-call(bf16[80,256]{1,0:T(8,128)(2,1)S(1)} %fusion.32.x_ref), custom_call_target="tpu_custom_call" | custom-call | tf_op jit(solution)/shard_map/pallas_call | solution.py:552
  18.1 0.3 fusion.3
  18.5 0.5 fusion.refs_2_
  19.0 0.9 fusion.8
  20.0 0.2 pad_select_fusion
  20.3 0.4 copy.27
  20.8 0.7 copy-done.13
  21.5 24.4 %shard_map.131 = (bf16[1792,1024]{1,0:T(8,128)(2,1)}, f32[640,128]{1,0:T(8,128)S(1)}, f32[640,128]{1,0:T(8,128)S(1)}) custom-call(bf16[1792,1024]{1,0:T(8,128)(2,1)} %bitcast.61, s32[1792,128]{1,0:T(8,128)S(1)} %bitcast.56, bf16[640,1024]{1,0:T(8,128)(2,1)S(1)} %fusion.refs_2_, bf16[2560,128]{1,0:T(8,128)(2,1)S(1)} %bitcast.55), custom_call_target="tpu_custom_call" | custom-call | tf_op jit(solution)/shard_map/pallas_call | solution.py:309
  46.0 1.1 add_convert_fusion.1.refs_0_
  47.1 21.1 %shard_map.132.x_ref.refs_1_ = bf16[672,1024]{1,0:T(8,128)(2,1)S(1)} custom-call(bf16[640,128]{1,0:T(8,128)(2,1)S(1)} %add_convert_fusion.1.refs_0_), custom_call_target="tpu_custom_call" | custom-call | tf_op jit(solution)/shard_map/pallas_call | solution.py:309
  68.2 2.4 fusion.103
  70.6 2.8 shard_map.133
  73.4 1.3 copy-done.3
  74.7 24.3 %shard_map.134 = (bf16[640,1024]{1,0:T(8,128)(2,1)S(1)}, bf16[2560,512]{1,0:T(8,128)(2,1)S(1)}) custom-call(bf16[640,128]{1,0:T(8,128)(2,1)S(1)} %get-tuple-element.26.refs_0_, bf16[672,1024]{1,0:T(8,128)(2,1)S(1)} %shard_map.132.x_ref.refs_1_), custom_call_target="tpu_custom_call" | custom-call | tf_op jit(solution)/shard_map/pallas_call | solution.py:309
  99.0 1.5 add_convert_fusion
  100.5 0.4 copy-done.11
  101.0 22.9 %shard_map.135 = (bf16[704,1024]{1,0:T(8,128)(2,1)S(1)}, bf16[2560,512]{1,0:T(8,128)(2,1)S(1)}) custom-call(bf16[640,128]{1,0:T(8,128)(2,1)S(1)} %get-tuple-element.101.refs_0_, bf16[672,1024]{1,0:T(8,128)(2,1)S(1)} %shard_map.132.x_ref.refs_1_), custom_call_target="tpu_custom_call" | custom-call | tf_op jit(solution)/shard_map/pallas_call | solution.py:309
  123.9 1.5 copy-done.10
  125.4 2.8 shard_map.136
  128.3 1.1 multiply_convert_fusion.1.refs_0_
  129.4 16.8 %shard_map.137 = (bf16[2560,128]{1,0:T(8,128)(2,1)S(1)}, bf16[640,1024]{1,0:T(8,128)(2,1)S(1)}) custom-call(bf16[640,128]{1,0:T(8,128)(2,1)S(1)} %multiply_convert_fusion.1.refs_0_, bf16[640,128]{1,0:T(8,128)(2,1)S(1)} %get-tuple-element.31.refs_1_), custom_call_target="tpu_custom_call" | custom-call | tf_op jit(solution)/shard_map/pallas_call | solution.py:309
  146.2 1.2 fusion.6
  147.4 0.4 fusion.4.refs_1_
  147.8 1.9 copy.23
  149.8 0.2 fusion.20
  150.0 0.2 fusion.22
  150.3 0.2 fusion.25
  150.5 0.2 fusion.27
  150.7 0.2 fusion.16
  150.9 1.2 copy-done.17
  152.1 1.5 convolution_convert_fusion.1.refs_0_
  153.6 29.2 %shard_map.138 = (f32[640,128]{1,0:T(8,128)S(1)}, bf16[128,1024]{1,0:T(8,128)(2,1)S(1)}, bf16[2560,512]{1,0:T(8,128)(2,1)S(1)}) custom-call(bf16[640,1024]{1,0:T(8,128)(2,1)S(1)} %convolution_convert_fusion.1.refs_0_, bf16[128,1024]{1,0:T(8,128)(2,1)S(1)} %fusion.4.refs_1_, bf16[704,1024]{1,0:T(8,128)(2,1)S(1)} %copy-done.6), custom_call_target="tpu_custom_call" | custom-call | tf_op jit(solution)/shard_map/pallas_call | solution.py:309
  182.9 1.1 fusion.7
  184.0 0.4 convolution_convert_fusion.5.refs_1_
  184.5 0.5 convolution_convert_fusion.refs_0_
  185.0 25.4 %shard_map.139 = (f32[640,128]{1,0:T(8,128)S(1)}, bf16[128,1024]{1,0:T(8,128)(2,1)S(1)}, bf16[2560,512]{1,0:T(8,128)(2,1)S(1)}) custom-call(bf16[640,1024]{1,0:T(8,128)(2,1)S(1)} %convolution_convert_fusion.refs_0_, bf16[128,1024]{1,0:T(8,128)(2,1)S(1)} %convolution_convert_fusion.5.refs_1_, bf16[704,1024]{1,0:T(8,128)(2,1)S(1)} %copy-done.6), custom_call_target="tpu_custom_call" | custom-call | tf_op jit(solution)/shard_map/pallas_call | solution.py:309
  210.4 1.5 copy-done.7
  211.8 1.1 multiply_convert_fusion.refs_0_
  213.0 13.9 %shard_map.140 = (bf16[2560,128]{1,0:T(8,128)(2,1)S(1)}, f32[896,1024]{1,0:T(8,128)}) custom-call(bf16[640,128]{1,0:T(8,128)(2,1)S(1)} %multiply_convert_fusion.refs_0_, bf16[2560,128]{1,0:T(8,128)(2,1)S(1)} %get-tuple-element.33.refs_1_, f32[7,2560]{1,0:T(8,128)S(1)} %stack.11.refs_2_, bf16[896,1024]{1,0:T(8,128)(2,1)S(1)} %copy-done.2, ...), custom_call_target="tpu_custom_call" | custom-call | tf_op jit(solution)/shard_map/pallas_call | solution.py:309
  226.9 112.9 %shard_map.141 = f32[2,896,1024]{2,1,0:T(8,128)} custom-call(f32[7,2560]{1,0:T(8,128)S(1)} %stack.10.mask_ref, bf16[2560,128]{1,0:T(8,128)(2,1)S(1)} %get-tuple-element.39.grad_ref, bf16[896,1024]{1,0:T(8,128)(2,1)S(1)} %copy-done.4, bf16[2560,512]{1,0:T(8,128)(2,1)S(1)} %copy-done.9, bf16[2560,512]{1,0:T(8,128)(2,1)} %copy-done.10, ...), custom_call_target="tpu_custom_call" | custom-call | tf_op jit(solution)/shard_map/pallas_call | solution.py:438
  339.8 1.1 convert_multiply_fusion
  (93 shorter events, 1.9 us)
Async XLA Ops:
  0.6 18.4 %copy-start = (bf16[16,128,512]{2,1,0:T(8,128)(2,1)S(1)}, bf16[16,128,512]{2,1,0:T(8,128)(2,1)}, u32[]{:S(2)}) copy-start(bf16[16,128,512]{2,1,0:T(8,128)(2,1)} %param.12) | copy-start | bytes 6291460
  0.6 5.2 %copy-start.18 = (bf16[128,640]{1,0:T(8,128)(2,1)S(1)}, bf16[128,640]{1,0:T(8,128)(2,1)}, u32[]{:S(2)}) copy-start(bf16[128,640]{1,0:T(8,128)(2,1)} %param.21) | copy-start | bytes 491524
  0.7 4.8 %copy-start.26 = (f32[256]{0:T(256)S(1)}, f32[256]{0:T(256)}, u32[]{:S(2)}) copy-start(f32[256]{0:T(256)} %param.17) | copy-start | bytes 3076
  0.7 5.1 %copy-start.24 = (s32[2,128,128]{2,1,0:T(8,128)S(1)}, s32[2,128,128]{2,1,0:T(8,128)}, u32[]{:S(2)}) copy-start(s32[2,128,128]{2,1,0:T(8,128)} %param.16) | copy-start | bytes 393220
  0.7 4.8 %copy-start.25 = (bf16[256,80]{0,1:T(8,128)(2,1)S(1)}, bf16[256,80]{0,1:T(8,128)(2,1)}, u32[]{:S(2)}) copy-start(bf16[256,80]{0,1:T(8,128)(2,1)} %param.11) | copy-start | bytes 122884
  5.0 13.1 %copy-start.23 = (bf16[2,128,1024]{2,1,0:T(8,128)(2,1)S(1)}, bf16[2,128,1024]{2,1,0:T(8,128)(2,1)}, u32[]{:S(2)}) copy-start(bf16[2,128,1024]{2,1,0:T(8,128)(2,1)} %param.14) | copy-start | bytes 1572868
  18.5 127.7 %copy-start.14 = (bf16[256,1024]{1,0:T(8,128)(2,1)}, bf16[256,1024]{1,0:T(8,128)(2,1)S(1)}, u32[]{:S(2)}) copy-start(bf16[256,1024]{1,0:T(8,128)(2,1)S(1)} %fusion.3) | copy-start | bytes 1572868
  20.3 1.2 copy-start.13
  70.6 54.8 %copy-start.1 = (bf16[896,1024]{1,0:T(8,128)(2,1)}, bf16[896,1024]{1,0:T(8,128)(2,1)S(1)}, u32[]{:S(2)}) copy-start(bf16[896,1024]{1,0:T(8,128)(2,1)S(1)} %get-tuple-element.72.w_ref.refs_3_) | copy-start | bytes 5505028
  73.4 1.3 copy-start.3
  99.0 1.5 copy-start.8
  99.0 1.9 copy-start.11
  100.5 45.7 %copy-start.20 = (f32[640,128]{1,0:T(8,128)}, f32[640,128]{1,0:T(8,128)S(1)}, u32[]{:S(2)}) copy-start(f32[640,128]{1,0:T(8,128)S(1)} %get-tuple-element.102) | copy-start | bytes 983044
  123.9 1.5 copy-start.10
  125.4 2.8 copy-start.5
  129.4 18.0 %copy-start.19 = (bf16[128,640]{1,0:T(8,128)(2,1)S(1)}, bf16[128,640]{1,0:T(8,128)(2,1)}, u32[]{:S(2)}) copy-start(bf16[128,640]{1,0:T(8,128)(2,1)} %param.21) | copy-start | bytes 491524
  150.0 2.0 copy-start.17
  152.1 1.5 copy-start.6
  153.6 29.3 %copy-start.21 = (f32[640,128]{1,0:T(8,128)S(1)}, f32[640,128]{1,0:T(8,128)}, u32[]{:S(2)}) copy-start(f32[640,128]{1,0:T(8,128)} %copy-done.20) | copy-start | bytes 983044
  153.6 29.3 %copy-start.22 = (bf16[128,640]{0,1:T(8,128)(2,1)S(1)}, bf16[128,640]{0,1:T(8,128)(2,1)}, u32[]{:S(2)}) copy-start(bf16[128,640]{0,1:T(8,128)(2,1)} %copy.21) | copy-start | bytes 491524
  153.6 30.4 %copy-start.12 = (bf16[640,1024]{1,0:T(8,128)(2,1)S(1)}, bf16[640,1024]{1,0:T(8,128)(2,1)}, u32[]{:S(2)}) copy-start(bf16[640,1024]{1,0:T(8,128)(2,1)} %copy-done.11) | copy-start | bytes 3932164
  182.9 1.6 copy-start.15
  185.0 28.0 %copy-start.2 = (bf16[896,1024]{1,0:T(8,128)(2,1)S(1)}, bf16[896,1024]{1,0:T(8,128)(2,1)}, u32[]{:S(2)}) copy-start(bf16[896,1024]{1,0:T(8,128)(2,1)} %copy-done.1) | copy-start | bytes 5505028
  210.4 1.5 copy-start.7
  213.0 13.9 %copy-start.4 = (bf16[896,1024]{1,0:T(8,128)(2,1)S(1)}, bf16[896,1024]{1,0:T(8,128)(2,1)}, u32[]{:S(2)}) copy-start(bf16[896,1024]{1,0:T(8,128)(2,1)} %copy-done.3) | copy-start | bytes 5505028
  213.0 13.9 %copy-start.9 = (bf16[2560,512]{1,0:T(8,128)(2,1)S(1)}, bf16[2560,512]{1,0:T(8,128)(2,1)}, u32[]{:S(2)}) copy-start(bf16[2560,512]{1,0:T(8,128)(2,1)} %copy-done.8) | copy-start | bytes 7864324
  226.9 112.9 %copy-start.16 = (bf16[256,1024]{1,0:T(8,128)(2,1)S(1)}, bf16[256,1024]{1,0:T(8,128)(2,1)}, u32[]{:S(2)}) copy-start(bf16[256,1024]{1,0:T(8,128)(2,1)} %copy-done.14) | copy-start | bytes 1572868

commit v5 on v4

--- a/solution.py
+++ b/solution.py
@@ -107,10 +107,10 @@
         copy = remote(summed.at[step], landed.at[step], send.at[step], recv.at[step], (tm, at(step)))
         copy.start()
         started.append(copy)
-        yield
     pairs[0].wait_recv()
     o_ref[...] = x_ref[:, column(chan, width)].astype(F32) + pair[0].astype(F32)
-    yield
+    for turns in range(4):
+        yield
     for copy, step in zip(started, range(1, chips)):
         copy.wait_recv()
         o_ref[...] += landed[step].astype(F32)
@@ -438,7 +438,7 @@
     return pl.pallas_call(
         functools.partial(saliency_kernel, spacing, taps),
         out_shape=jax.ShapeDtypeStruct((2,) + eff.shape, F32),
-        in_specs=[whole] * 2 + [anywhere] * 4,
+        in_specs=[whole] * 2 + [anywhere] * 3 + [whole],
         out_specs=anywhere,
         scratch_shapes=[
             pltpu.VMEM((width, rows), F32),

time: 341 us -> 241 us (0.71)
  Pallas kernels: 308 us -> 207 us
    pallas_call x1, Pallas kernels: 113 us -> 12.6 us  [saliency(): pl.pallas_call(functools.partial(saliency_kernel, spacing, taps), out_sha...]
where the time goes in v5:
time: 241 us
  Pallas kernels  207 us (86%)
  local copies, waits for them, and re-layouts  13 us (5%)
  other arithmetic  11.6 us (5%)
  matrix products  7.16 us (3%)
    pallas_call x8, Pallas kernels, together(): pl.pallas_call(kernel, out_shape=[task[1] for task in tasks], in_specs=[w...  178 us
    pallas_call x1, Pallas kernels, saliency(): pl.pallas_call(functools.partial(saliency_kernel, spacing, taps), out_sha...  12.6 us
    pallas_call x1, Pallas kernels, run(): pl.pallas_call(kernel, out_shape=jax.ShapeDtypeStruct(out_shape, dtype),...  11.2 us
    unnamed x57, local copies, waits for them, and re-layouts  9.51 us
    pallas_call x2, Pallas kernels, taps_call(): pl.pallas_call(functools.partial(taps_kernel, halo, spacing, taps), out_s...  5.61 us

profile of v5, /device:TPU:0, one launch (start us, length us, event | category | flops | bytes accessed | tf_op | source)
XLA Modules:
  0.0 240.7 jit_solution(5092947758324982837)
XLA Ops:
  0.7 1.0 reduce-window.9
  1.7 0.7 bitcast_subtract_fusion
  2.3 0.8 multiply_bitcast_fusion.1
  3.1 0.8 multiply_bitcast_fusion
  4.6 0.4 convert_reduce_fusion
  5.5 0.3 fusion.32.x_ref
  5.8 0.8 copy.21
  6.6 11.2 %shard_map.130 = bf16[320,512]{1,0:T(8,128)(2,1)S(1)} custom-call(bf16[80,256]{1,0:T(8,128)(2,1)S(1)} %fusion.32.x_ref), custom_call_target="tpu_custom_call" | custom-call | tf_op jit(solution)/shard_map/pallas_call | solution.py:552
  18.1 0.3 fusion.3
  18.5 0.5 fusion.refs_2_
  19.0 0.9 fusion.8
  20.0 0.2 pad_select_fusion
  20.3 0.4 copy.27
  20.8 0.7 copy-done.13
  21.5 24.4 %shard_map.131 = (bf16[1792,1024]{1,0:T(8,128)(2,1)}, f32[640,128]{1,0:T(8,128)S(1)}, f32[640,128]{1,0:T(8,128)S(1)}) custom-call(bf16[1792,1024]{1,0:T(8,128)(2,1)} %bitcast.61, s32[1792,128]{1,0:T(8,128)S(1)} %bitcast.56, bf16[640,1024]{1,0:T(8,128)(2,1)S(1)} %fusion.refs_2_, bf16[2560,128]{1,0:T(8,128)(2,1)S(1)} %bitcast.55), custom_call_target="tpu_custom_call" | custom-call | tf_op jit(solution)/shard_map/pallas_call | solution.py:309
  46.0 1.1 add_convert_fusion.1.refs_0_
  47.1 21.1 %shard_map.132.x_ref.refs_1_ = bf16[672,1024]{1,0:T(8,128)(2,1)S(1)} custom-call(bf16[640,128]{1,0:T(8,128)(2,1)S(1)} %add_convert_fusion.1.refs_0_), custom_call_target="tpu_custom_call" | custom-call | tf_op jit(solution)/shard_map/pallas_call | solution.py:309
  68.2 2.4 %fusion.103 = (bf16[896,1024]{1,0:T(8,128)(2,1)S(1)}, bf16[896,1024]{1,0:T(8,128)(2,1)S(1)}) fusion(bf16[1792,1024]{1,0:T(8,128)(2,1)} %get-tuple-element.25), kind=kLoop, calls=%fused_computation.379 | loop fusion | bytes 7340032 | tf_op jit(solution)/shard_map/slice | solution.py:740
  70.6 2.8 %shard_map.133 = (f32[640,128]{1,0:T(8,128)S(1)}, bf16[640,128]{1,0:T(8,128)(2,1)S(1)}) custom-call(bf16[672,1024]{1,0:T(8,128)(2,1)S(1)} %shard_map.132.x_ref.refs_1_, bf16[896,1024]{1,0:T(8,128)(2,1)S(1)} %get-tuple-element.73.w_ref.eff_ref, f32[672,128]{1,0:T(8,128)S(1)} %broadcast_in_dim.299.ids_ref, f32[1,128]{1,0:T(1,128)S(1)} %get-tuple-element.97.alpha_ref), custom_call_target="tpu_custom_call" | custom-call | tf_op jit(solution)/shard_map/pallas_call | solution.py:345
  73.4 1.3 copy-done.3
  74.7 24.3 %shard_map.134 = (bf16[640,1024]{1,0:T(8,128)(2,1)S(1)}, bf16[2560,512]{1,0:T(8,128)(2,1)S(1)}) custom-call(bf16[640,128]{1,0:T(8,128)(2,1)S(1)} %get-tuple-element.26.refs_0_, bf16[672,1024]{1,0:T(8,128)(2,1)S(1)} %shard_map.132.x_ref.refs_1_), custom_call_target="tpu_custom_call" | custom-call | tf_op jit(solution)/shard_map/pallas_call | solution.py:309
  99.0 1.5 add_convert_fusion
  100.5 0.4 copy-done.11
  101.0 22.9 %shard_map.135 = (bf16[704,1024]{1,0:T(8,128)(2,1)S(1)}, bf16[2560,512]{1,0:T(8,128)(2,1)S(1)}) custom-call(bf16[640,128]{1,0:T(8,128)(2,1)S(1)} %get-tuple-element.101.refs_0_, bf16[672,1024]{1,0:T(8,128)(2,1)S(1)} %shard_map.132.x_ref.refs_1_), custom_call_target="tpu_custom_call" | custom-call | tf_op jit(solution)/shard_map/pallas_call | solution.py:309
  123.9 1.5 copy-done.10
  125.4 2.8 %shard_map.136 = (f32[640,128]{1,0:T(8,128)S(1)}, bf16[640,128]{1,0:T(8,128)(2,1)S(1)}) custom-call(bf16[704,1024]{1,0:T(8,128)(2,1)S(1)} %get-tuple-element.29.x_ref.refs_2_, bf16[896,1024]{1,0:T(8,128)(2,1)S(1)} %get-tuple-element.72.w_ref.refs_3_, f32[704,128]{1,0:T(8,128)S(1)} %broadcast_in_dim.301.ids_ref, f32[1,128]{1,0:T(1,128)S(1)} %get-tuple-element.96.alpha_ref), custom_call_target="tpu_custom_call" | custom-call | tf_op jit(solution)/shard_map/pallas_call | solution.py:345
  128.3 1.1 multiply_convert_fusion.1.refs_0_
  129.4 16.8 %shard_map.137 = (bf16[2560,128]{1,0:T(8,128)(2,1)S(1)}, bf16[640,1024]{1,0:T(8,128)(2,1)S(1)}) custom-call(bf16[640,128]{1,0:T(8,128)(2,1)S(1)} %multiply_convert_fusion.1.refs_0_, bf16[640,128]{1,0:T(8,128)(2,1)S(1)} %get-tuple-element.31.refs_1_), custom_call_target="tpu_custom_call" | custom-call | tf_op jit(solution)/shard_map/pallas_call | solution.py:309
  146.2 1.2 fusion.6
  147.4 0.4 fusion.4.refs_1_
  147.8 1.9 copy.23
  149.8 0.2 fusion.20
  150.0 0.2 fusion.22
  150.3 0.2 fusion.25
  150.5 0.2 fusion.27
  150.7 0.2 fusion.16
  150.9 1.2 copy-done.17
  152.1 1.5 convolution_convert_fusion.1.refs_0_
  153.6 29.2 %shard_map.138 = (f32[640,128]{1,0:T(8,128)S(1)}, bf16[128,1024]{1,0:T(8,128)(2,1)S(1)}, bf16[2560,512]{1,0:T(8,128)(2,1)S(1)}) custom-call(bf16[640,1024]{1,0:T(8,128)(2,1)S(1)} %convolution_convert_fusion.1.refs_0_, bf16[128,1024]{1,0:T(8,128)(2,1)S(1)} %fusion.4.refs_1_, bf16[704,1024]{1,0:T(8,128)(2,1)S(1)} %copy-done.6), custom_call_target="tpu_custom_call" | custom-call | tf_op jit(solution)/shard_map/pallas_call | solution.py:309
  182.9 1.1 fusion.7
  184.0 0.4 convolution_convert_fusion.5.refs_1_
  184.5 0.5 convolution_convert_fusion.refs_0_
  185.0 25.4 %shard_map.139 = (f32[640,128]{1,0:T(8,128)S(1)}, bf16[128,1024]{1,0:T(8,128)(2,1)S(1)}, bf16[2560,512]{1,0:T(8,128)(2,1)S(1)}) custom-call(bf16[640,1024]{1,0:T(8,128)(2,1)S(1)} %convolution_convert_fusion.refs_0_, bf16[128,1024]{1,0:T(8,128)(2,1)S(1)} %convolution_convert_fusion.5.refs_1_, bf16[704,1024]{1,0:T(8,128)(2,1)S(1)} %copy-done.6), custom_call_target="tpu_custom_call" | custom-call | tf_op jit(solution)/shard_map/pallas_call | solution.py:309
  210.4 1.5 copy-done.7
  211.8 1.1 multiply_convert_fusion.refs_0_
  213.0 13.9 %shard_map.140 = (bf16[2560,128]{1,0:T(8,128)(2,1)S(1)}, f32[896,1024]{1,0:T(8,128)}) custom-call(bf16[640,128]{1,0:T(8,128)(2,1)S(1)} %multiply_convert_fusion.refs_0_, bf16[2560,128]{1,0:T(8,128)(2,1)S(1)} %get-tuple-element.33.refs_1_, f32[7,2560]{1,0:T(8,128)S(1)} %stack.11.refs_2_, bf16[896,1024]{1,0:T(8,128)(2,1)S(1)} %copy-done.2, ...), custom_call_target="tpu_custom_call" | custom-call | tf_op jit(solution)/shard_map/pallas_call | solution.py:309
  226.9 12.6 %shard_map.141 = f32[2,896,1024]{2,1,0:T(8,128)} custom-call(f32[7,2560]{1,0:T(8,128)S(1)} %stack.10.mask_ref, bf16[2560,128]{1,0:T(8,128)(2,1)S(1)} %get-tuple-element.39.grad_ref, bf16[896,1024]{1,0:T(8,128)(2,1)S(1)} %copy-done.4, bf16[2560,512]{1,0:T(8,128)(2,1)S(1)} %copy-done.9, bf16[2560,512]{1,0:T(8,128)(2,1)} %copy-done.10, ...), custom_call_target="tpu_custom_call" | custom-call | tf_op jit(solution)/shard_map/pallas_call | solution.py:438
  239.5 1.1 convert_multiply_fusion
  (93 shorter events, 1.9 us)
Async XLA Ops:
  0.6 18.4 %copy-start = (bf16[16,128,512]{2,1,0:T(8,128)(2,1)S(1)}, bf16[16,128,512]{2,1,0:T(8,128)(2,1)}, u32[]{:S(2)}) copy-start(bf16[16,128,512]{2,1,0:T(8,128)(2,1)} %param.12) | copy-start | bytes 6291460
  0.6 5.2 %copy-start.18 = (bf16[128,640]{1,0:T(8,128)(2,1)S(1)}, bf16[128,640]{1,0:T(8,128)(2,1)}, u32[]{:S(2)}) copy-start(bf16[128,640]{1,0:T(8,128)(2,1)} %param.21) | copy-start | bytes 491524
  0.7 4.8 %copy-start.26 = (f32[256]{0:T(256)S(1)}, f32[256]{0:T(256)}, u32[]{:S(2)}) copy-start(f32[256]{0:T(256)} %param.17) | copy-start | bytes 3076
  0.7 5.1 %copy-start.24 = (s32[2,128,128]{2,1,0:T(8,128)S(1)}, s32[2,128,128]{2,1,0:T(8,128)}, u32[]{:S(2)}) copy-start(s32[2,128,128]{2,1,0:T(8,128)} %param.16) | copy-start | bytes 393220
  0.7 4.8 %copy-start.25 = (bf16[256,80]{0,1:T(8,128)(2,1)S(1)}, bf16[256,80]{0,1:T(8,128)(2,1)}, u32[]{:S(2)}) copy-start(bf16[256,80]{0,1:T(8,128)(2,1)} %param.11) | copy-start | bytes 122884
  5.0 13.1 %copy-start.23 = (bf16[2,128,1024]{2,1,0:T(8,128)(2,1)S(1)}, bf16[2,128,1024]{2,1,0:T(8,128)(2,1)}, u32[]{:S(2)}) copy-start(bf16[2,128,1024]{2,1,0:T(8,128)(2,1)} %param.14) | copy-start | bytes 1572868
  18.5 127.7 %copy-start.14 = (bf16[256,1024]{1,0:T(8,128)(2,1)}, bf16[256,1024]{1,0:T(8,128)(2,1)S(1)}, u32[]{:S(2)}) copy-start(bf16[256,1024]{1,0:T(8,128)(2,1)S(1)} %fusion.3) | copy-start | bytes 1572868
  20.3 1.2 copy-start.13
  70.6 54.8 %copy-start.1 = (bf16[896,1024]{1,0:T(8,128)(2,1)}, bf16[896,1024]{1,0:T(8,128)(2,1)S(1)}, u32[]{:S(2)}) copy-start(bf16[896,1024]{1,0:T(8,128)(2,1)S(1)} %get-tuple-element.72.w_ref.refs_3_) | copy-start | bytes 5505028
  73.4 1.3 copy-start.3
  99.0 1.5 copy-start.8
  99.0 1.9 copy-start.11
  100.5 45.7 %copy-start.20 = (f32[640,128]{1,0:T(8,128)}, f32[640,128]{1,0:T(8,128)S(1)}, u32[]{:S(2)}) copy-start(f32[640,128]{1,0:T(8,128)S(1)} %get-tuple-element.102) | copy-start | bytes 983044
  123.9 1.5 copy-start.10
  125.4 2.8 %copy-start.5 = (bf16[704,1024]{1,0:T(8,128)(2,1)}, bf16[704,1024]{1,0:T(8,128)(2,1)S(1)}, u32[]{:S(2)}) copy-start(bf16[704,1024]{1,0:T(8,128)(2,1)S(1)} %get-tuple-element.29.x_ref.refs_2_) | copy-start | bytes 4325380
  129.4 18.0 %copy-start.19 = (bf16[128,640]{1,0:T(8,128)(2,1)S(1)}, bf16[128,640]{1,0:T(8,128)(2,1)}, u32[]{:S(2)}) copy-start(bf16[128,640]{1,0:T(8,128)(2,1)} %param.21) | copy-start | bytes 491524
  150.0 2.0 copy-start.17
  152.1 1.5 copy-start.6
  153.6 29.3 %copy-start.21 = (f32[640,128]{1,0:T(8,128)S(1)}, f32[640,128]{1,0:T(8,128)}, u32[]{:S(2)}) copy-start(f32[640,128]{1,0:T(8,128)} %copy-done.20) | copy-start | bytes 983044
  153.6 29.3 %copy-start.22 = (bf16[128,640]{0,1:T(8,128)(2,1)S(1)}, bf16[128,640]{0,1:T(8,128)(2,1)}, u32[]{:S(2)}) copy-start(bf16[128,640]{0,1:T(8,128)(2,1)} %copy.21) | copy-start | bytes 491524
  153.6 30.4 %copy-start.12 = (bf16[640,1024]{1,0:T(8,128)(2,1)S(1)}, bf16[640,1024]{1,0:T(8,128)(2,1)}, u32[]{:S(2)}) copy-start(bf16[640,1024]{1,0:T(8,128)(2,1)} %copy-done.11) | copy-start | bytes 3932164
  182.9 1.6 copy-start.15
  185.0 28.0 %copy-start.2 = (bf16[896,1024]{1,0:T(8,128)(2,1)S(1)}, bf16[896,1024]{1,0:T(8,128)(2,1)}, u32[]{:S(2)}) copy-start(bf16[896,1024]{1,0:T(8,128)(2,1)} %copy-done.1) | copy-start | bytes 5505028
  210.4 1.5 copy-start.7
  213.0 13.9 %copy-start.4 = (bf16[896,1024]{1,0:T(8,128)(2,1)S(1)}, bf16[896,1024]{1,0:T(8,128)(2,1)}, u32[]{:S(2)}) copy-start(bf16[896,1024]{1,0:T(8,128)(2,1)} %copy-done.3) | copy-start | bytes 5505028
  213.0 13.9 %copy-start.9 = (bf16[2560,512]{1,0:T(8,128)(2,1)S(1)}, bf16[2560,512]{1,0:T(8,128)(2,1)}, u32[]{:S(2)}) copy-start(bf16[2560,512]{1,0:T(8,128)(2,1)} %copy-done.8) | copy-start | bytes 7864324
  226.9 12.6 %copy-start.16 = (bf16[256,1024]{1,0:T(8,128)(2,1)S(1)}, bf16[256,1024]{1,0:T(8,128)(2,1)}, u32[]{:S(2)}) copy-start(bf16[256,1024]{1,0:T(8,128)(2,1)} %copy-done.14) | copy-start | bytes 1572868
